TPU v7x, 32 devices: a whole 2x2x4 slice. The times are simulated.
32 devices in a mesh: dp: 4 (over z), space: 8 (over y, x, core).
Axes of the slice: x: 2, y: 2, z: 4, core: 2. Of those that a mesh axis runs over, the one named last changes fastest.
Arguments:
- features: bfloat16 [4, 96, 16, 56, 448], P('dp', None, None, 'space'), may hold values from -6 to 6
- conv_weight: bfloat16 [3, 3, 3, 3, 96], replicated, may hold values from -0.125 to 0.125
- out_grad: bfloat16 [4, 16, 128, 384], P('dp', 'space'), may hold values from -6 to 6
- pos_embed: bfloat16 [128, 384], replicated, may hold values from -3 to 3
- patch_weight: bfloat16 [588, 384], replicated, may hold values from -0.25 to 0.25
- norm1: float32 [384], replicated, may hold values from 0.1 to 1.9
- qkv_weight: bfloat16 [384, 1152], replicated, may hold values from -0.3125 to 0.3125
- proj_weight: bfloat16 [384, 384], replicated, may hold values from -0.3125 to 0.3125
- norm2: float32 [384], replicated, may hold values from 0.1 to 1.9
- fc1_weight: bfloat16 [384, 1536], replicated, may hold values from -0.3125 to 0.3125
- fc2_weight: bfloat16 [1536, 384], replicated, may hold values from -0.15625 to 0.15625
Outputs:
- block_out: bfloat16 [4, 16, 128, 384], P('dp', 'space')
- feature_grad: bfloat16 [4, 96, 16, 56, 448], P('dp', None, None, 'space')
- conv_grad: float32 [3, 3, 3, 3, 96], replicated
- qkv_grad: float32 [384, 1152], P('space')
- proj_grad: float32 [384, 384], P('space')
- fc1_grad: float32 [384, 1536], P('space')
- fc2_grad: float32 [1536, 384], P('space')
All inputs are finite; a program needn't handle non-finite values.
Results may differ from a plain program's by a relative error of at most 0.025.
Values may be sent and summed in bfloat16 or wider, within the bound.
No kernel may reach another device: no remote copies, remote signals or barrier semaphores. Data moves between devices by JAX's collectives and lax.ppermute only.
A program may use at most 192 MiB of HBM per device.

v0:
```python
import functools
import math

import jax
import jax.numpy as jnp
from jax import lax
from jax.experimental import pallas as pl
from jax.experimental.pallas import tpu as pltpu
from jax.sharding import PartitionSpec as P

HEADS = 6
PATCH = 14
COLOURS = 3
TAPS = 3
F32 = jnp.float32
BF16 = jnp.bfloat16
MIB = 1 << 20


def dot(a, b):
    return jnp.dot(a, b, preferred_element_type=F32)


def dot_nt(a, b):
    return lax.dot_general(a, b, (((1,), (1,)), ((), ())), preferred_element_type=F32)


def dot_tn(a, b):
    return lax.dot_general(a, b, (((0,), (0,)), ((), ())), preferred_element_type=F32)


def split(index, size):
    if size & (size - 1) == 0:
        shift = size.bit_length() - 1
        return index >> shift, index & (size - 1)
    high = jnp.floor((index.astype(F32) + 0.5) * (1.0 / size)).astype(jnp.int32)
    return high, index - high * size


def rows_of(count):
    return lax.broadcasted_iota(jnp.int32, (count, 1), 0)


def cols_of(count):
    return lax.broadcasted_iota(jnp.int32, (1, count), 1)


def match(left, right):
    return jnp.where(left == right, 1.0, 0.0).astype(BF16)


def round_up(value, unit):
    return -(-value // unit) * unit


class Sizes:
    def __init__(self, features, space):
        self.space = space
        self.channels, self.frames, self.rows, self.cols = features.shape[1:]
        self.per_dev = self.frames // space
        self.ext = self.rows + 2
        self.height = self.rows * space
        self.patch_rows = self.height // PATCH
        self.patch_cols = self.cols // PATCH
        self.tokens = self.patch_rows * self.patch_cols
        self.block = round_up(self.ext * COLOURS * self.per_dev, 16)
        self.q_used = COLOURS * PATCH
        self.q_pad = round_up(self.q_used, 64)
        self.plane = COLOURS * self.frames
        self.group = TAPS * self.plane
        self.window = TAPS * self.group
        self.depth = self.channels * self.frames


def wire_keys(sizes, index):
    peer, rest = split(index, sizes.block)
    plane, frame = split(rest, sizes.per_dev)
    ext, colour = split(plane, COLOURS)
    key = (frame * COLOURS + colour) * 4096 + peer * sizes.rows + ext
    return jnp.where(plane < sizes.ext * COLOURS, key, -2)


def patch_keys(sizes, index):
    lead, q = split(index, sizes.q_pad)
    frame, patch_row = split(lead, sizes.patch_rows)
    colour, row = split(q, PATCH)
    key = (frame * COLOURS + colour) * 4096 + patch_row * PATCH + row + 1
    return jnp.where(q < sizes.q_used, key, -1)


def tile_keys(sizes, index):
    return index


def tile_wire_keys(sizes, index):
    peer, rest = split(index, sizes.block)
    plane, frame = split(rest, sizes.per_dev)
    key = plane * sizes.frames + peer * sizes.per_dev + frame
    return jnp.where(plane < sizes.ext * COLOURS, key, -2)


def flipped(tap):
    row, _ = split(tap, TAPS * COLOURS)
    return tap + (TAPS - 1 - 2 * row) * (TAPS * COLOURS)


def column_order(sizes):
    inner, patch = split(rows_of(sizes.cols), sizes.patch_cols)
    return match(patch * PATCH + inner, cols_of(sizes.cols))


def conv_forward_kernel(sizes, weight_ref, x_ref, out_ref, band_ref, acc_ref, plane_ref):
    step = pl.program_id(0)
    taps = TAPS * TAPS * COLOURS

    @pl.when(step == 0)
    def _():
        tap, frame_out = split(rows_of(sizes.window), sizes.frames)
        channel, frame_in = split(cols_of(sizes.depth), sizes.frames)
        spread = match(rows_of(sizes.channels), channel)
        pick = match(flipped(tap), cols_of(taps))
        lag = frame_in - frame_out + 2
        total = None
        for a in range(TAPS):
            weight = weight_ref[a * taps : (a + 1) * taps, :]
            wide = dot(dot(pick, weight).astype(BF16), spread)
            wide = jnp.where(lag == a, wide, 0.0)
            total = wide if total is None else total + wide
        band_ref[...] = total.astype(BF16)

    x = x_ref[...].reshape(sizes.depth, sizes.cols)
    product = dot(band_ref[...], x)
    base = pl.multiple_of(step * sizes.group, 16)
    keep = sizes.window - sizes.group

    @pl.when(step == 0)
    def _():
        acc_ref[pl.ds(0, sizes.window), :] = product

    @pl.when(step > 0)
    def _():
        acc_ref[pl.ds(base, keep), :] += product[:keep]
        acc_ref[pl.ds(pl.multiple_of(base + keep, 16), sizes.group), :] = product[keep:]

    @pl.when(step == sizes.rows - 1)
    def _():
        zero = jnp.zeros((sizes.plane, 1), F32)
        for ext in range(sizes.ext):
            at = ext * sizes.group
            first = acc_ref[at : at + sizes.plane, :]
            second = acc_ref[at + sizes.plane : at + 2 * sizes.plane, :]
            third = acc_ref[at + 2 * sizes.plane : at + 3 * sizes.plane, :]
            first = jnp.concatenate([zero, first[:, : sizes.cols - 1]], axis=1)
            third = jnp.concatenate([third[:, 1:], zero], axis=1)
            plane_ref[ext * sizes.plane : (ext + 1) * sizes.plane, :] = (
                first + second + third
            ).astype(BF16)
        wire = tile_wire_keys(sizes, rows_of(sizes.space * sizes.block))
        order = match(wire, cols_of(sizes.ext * sizes.plane))
        moved = dot(order, plane_ref[...]).astype(BF16)
        out_ref[...] = moved.reshape(sizes.space, sizes.block, sizes.cols)


def conv_forward(sizes, weight, x):
    return pl.pallas_call(
        functools.partial(conv_forward_kernel, sizes),
        grid=(sizes.rows,),
        in_specs=[
            pl.BlockSpec(weight.shape, lambda h: (0, 0)),
            pl.BlockSpec((sizes.channels, 1, sizes.frames, sizes.cols), lambda h: (0, h, 0, 0)),
        ],
        out_specs=pl.BlockSpec((sizes.space, sizes.block, sizes.cols), lambda h: (0, 0, 0)),
        out_shape=jax.ShapeDtypeStruct((sizes.space, sizes.block, sizes.cols), BF16),
        scratch_shapes=[
            pltpu.VMEM((sizes.window, sizes.depth), BF16),
            pltpu.VMEM((sizes.ext * sizes.group, sizes.cols), F32),
            pltpu.VMEM((sizes.ext * sizes.plane, sizes.cols), BF16),
        ],
        compiler_params=pltpu.CompilerParams(vmem_limit_bytes=48 * MIB),
        cost_estimate=pl.CostEstimate(
            flops=2 * sizes.rows * sizes.window * sizes.depth * sizes.cols,
            bytes_accessed=2 * x.size,
            transcendentals=0,
        ),
        name="conv_forward",
    )(weight, x)


def prepare_kernel(sizes, weight_ref, patch_ref, patch_out_ref, band_ref):
    taps = TAPS * TAPS * COLOURS
    inner, q = split(rows_of(PATCH * sizes.q_pad), sizes.q_pad)
    source = jnp.where(q < sizes.q_used, q * PATCH + inner, -1)
    patch_out_ref[...] = dot(match(source, cols_of(patch_ref.shape[0])), patch_ref[...]).astype(BF16)

    tap, frame_in = split(cols_of(sizes.window), sizes.frames)
    pick = match(rows_of(taps), flipped(tap))
    chunk = sizes.depth // 4
    for part in range(4):
        channel, frame_out = split(rows_of(chunk) + part * chunk, sizes.frames)
        spread = match(channel, cols_of(sizes.channels))
        lag = frame_out - frame_in + 2
        total = None
        for a in range(TAPS):
            weight = weight_ref[a * taps : (a + 1) * taps, :]
            wide = dot(spread, dot_tn(weight, pick).astype(BF16))
            wide = jnp.where(lag == a, wide, 0.0)
            total = wide if total is None else total + wide
        band_ref[part * chunk : (part + 1) * chunk, :] = total.astype(BF16)


def prepare(sizes, weight, patch_weight):
    width = patch_weight.shape[1]
    return pl.pallas_call(
        functools.partial(prepare_kernel, sizes),
        out_shape=(
            jax.ShapeDtypeStruct((PATCH * sizes.q_pad, width), BF16),
            jax.ShapeDtypeStruct((sizes.depth, sizes.window), BF16),
        ),
        compiler_params=pltpu.CompilerParams(vmem_limit_bytes=48 * MIB),
        cost_estimate=pl.CostEstimate(
            flops=4 * 10**9, bytes_accessed=4 * MIB, transcendentals=0
        ),
        name="prepare",
    )(weight, patch_weight)


def normalise(values):
    average = jnp.mean(values, axis=-1, keepdims=True)
    centered = values - average
    variance = jnp.mean(centered * centered, axis=-1, keepdims=True)
    scale = lax.rsqrt(variance + 1e-06)
    return centered * scale, scale


def normalise_back(grad, unit, scale):
    mean_grad = jnp.mean(grad, axis=-1, keepdims=True)
    mean_both = jnp.mean(grad * unit, axis=-1, keepdims=True)
    return scale * (grad - mean_grad - unit * mean_both)


def block_kernel(
    sizes,
    me_ref,
    wire_ref,
    cotangent_ref,
    pos_ref,
    patch_ref,
    norm1_ref,
    qkv_ref,
    proj_ref,
    norm2_ref,
    fc1_ref,
    fc2_ref,
    out_ref,
    wire_out_ref,
    grads_ref,
    pixels_ref,
    patches_ref,
    column_ref,
    packed_ref,
    probs_ref,
    attended_ref,
    grad_packed_ref,
    qkv_grad_ref,
    proj_grad_ref,
    fc1_grad_ref,
    fc2_grad_ref,
):
    tokens, width = pos_ref.shape
    frames = sizes.per_dev
    count = frames * tokens
    hidden_width = fc1_ref.shape[1]
    head = width // HEADS
    wire_rows = sizes.space * sizes.block
    leads = frames * sizes.patch_rows
    q_pad = sizes.q_pad
    pc = sizes.patch_cols

    order = match(patch_keys(sizes, rows_of(leads * q_pad)), wire_keys(sizes, cols_of(wire_rows)))
    pixels_ref[...] = dot(order, wire_ref[...].reshape(wire_rows, sizes.cols)).astype(BF16)
    columns = column_order(sizes)
    column_ref[...] = columns
    for lead in range(leads):
        turned = dot_nt(columns, pixels_ref[lead * q_pad : (lead + 1) * q_pad, :])
        for inner in range(PATCH):
            patches_ref[lead * pc : (lead + 1) * pc, inner * q_pad : (inner + 1) * q_pad] = turned[
                inner * pc : (inner + 1) * pc, :
            ].astype(BF16)

    pos = pos_ref[...].astype(F32)
    embedded = dot(patches_ref[...], patch_ref[...])
    embedded = embedded + (pos if frames == 1 else jnp.concatenate([pos] * frames, axis=0))
    gain1 = norm1_ref[...]
    gain2 = norm2_ref[...]
    unit1, scale1 = normalise(embedded)
    normed = (unit1 * gain1).astype(BF16)
    packed_ref[...] = dot(normed, qkv_ref[...]).astype(BF16)

    lanes = min(128, width)
    per_group = lanes // head
    lane_head, _ = split(cols_of(lanes), head)
    inv = 1.0 / float(head) ** 0.5
    for frame in range(frames):
        at = slice(frame * tokens, (frame + 1) * tokens)
        for group in range(width // lanes):
            cut = slice(group * lanes, (group + 1) * lanes)
            queries = packed_ref[at, cut]
            keys_in = packed_ref[at, width + group * lanes : width + (group + 1) * lanes]
            values_in = packed_ref[at, 2 * width + group * lanes : 2 * width + (group + 1) * lanes]
            joined = None
            for sub in range(per_group):
                mine = lane_head == sub
                masked = queries * jnp.where(mine, 1.0, 0.0).astype(BF16)
                scores = dot_nt(masked, keys_in) * inv
                scores = jnp.exp(scores - jnp.max(scores, axis=-1, keepdims=True))
                probs = scores / jnp.sum(scores, axis=-1, keepdims=True)
                probs_ref[(frame * HEADS) + group * per_group + sub] = probs
                value = dot(probs.astype(BF16), values_in)
                joined = value if joined is None else jnp.where(mine, value, joined)
            attended_ref[at, cut] = joined.astype(BF16)

    residual = embedded + dot(attended_ref[...], proj_ref[...])
    unit2, scale2 = normalise(residual)
    normed2 = (unit2 * gain2).astype(BF16)
    cotangent = cotangent_ref[...].reshape(count, width)

    chunk = width
    result = residual
    grad_normed2 = None
    for part in range(hidden_width // chunk):
        cut = slice(part * chunk, (part + 1) * chunk)
        before = dot(normed2, fc1_ref[:, cut])
        cdf = 0.5 + 0.5 * lax.erf(before * math.sqrt(0.5))
        hidden = (before * cdf).astype(BF16)
        result = result + dot(hidden, fc2_ref[cut, :])
        slope = cdf + before * (jnp.exp(-0.5 * before * before) * (1.0 / math.sqrt(2.0 * math.pi)))
        grad_hidden = dot_nt(cotangent, fc2_ref[cut, :]).astype(BF16)
        grad_before = (grad_hidden.astype(F32) * slope).astype(BF16)
        fc2_grad_ref[cut, :] = dot_tn(hidden, cotangent)
        fc1_grad_ref[:, cut] = dot_tn(normed2, grad_before)
        piece = dot_nt(grad_before, fc1_ref[:, cut])
        grad_normed2 = piece if grad_normed2 is None else grad_normed2 + piece
    out_ref[...] = result.astype(BF16).reshape(frames, tokens, width)

    grad_normed2 = grad_normed2.astype(BF16).astype(F32) * gain2
    grad_residual = cotangent.astype(F32) + normalise_back(grad_normed2, unit2, scale2)
    grad_residual_b = grad_residual.astype(BF16)
    proj_grad_ref[...] = dot_tn(attended_ref[...], grad_residual_b)
    attended_ref[...] = dot_nt(grad_residual_b, proj_ref[...]).astype(BF16)

    for frame in range(frames):
        at = slice(frame * tokens, (frame + 1) * tokens)
        for group in range(width // lanes):
            cut = slice(group * lanes, (group + 1) * lanes)
            cut_k = slice(width + group * lanes, width + (group + 1) * lanes)
            cut_v = slice(2 * width + group * lanes, 2 * width + (group + 1) * lanes)
            queries = packed_ref[at, cut]
            keys_in = packed_ref[at, cut_k]
            values_in = packed_ref[at, cut_v]
            grad_att = attended_ref[at, cut]
            grad_q = grad_k = grad_v = None
            for sub in range(per_group):
                mine = lane_head == sub
                mask = jnp.where(mine, 1.0, 0.0).astype(BF16)
                masked_q = queries * mask
                masked_g = grad_att * mask
                probs = probs_ref[(frame * HEADS) + group * per_group + sub]
                probs_b = probs.astype(BF16)
                grad_probs = dot_nt(masked_g, values_in).astype(BF16).astype(F32)
                inner = jnp.sum(grad_probs * probs, axis=-1, keepdims=True)
                grad_scores = (probs * (grad_probs - inner) * inv).astype(BF16)
                one_q = dot(grad_scores, keys_in)
                one_k = dot_tn(grad_scores, masked_q)
                one_v = dot_tn(probs_b, masked_g)
                grad_q = one_q if grad_q is None else jnp.where(mine, one_q, grad_q)
                grad_k = one_k if grad_k is None else grad_k + one_k
                grad_v = one_v if grad_v is None else grad_v + one_v
            grad_packed_ref[at, cut] = grad_q.astype(BF16)
            grad_packed_ref[at, cut_k] = grad_k.astype(BF16)
            grad_packed_ref[at, cut_v] = grad_v.astype(BF16)

    grad_packed = grad_packed_ref[...]
    grad_normed = dot_nt(grad_packed, qkv_ref[...]).astype(BF16).astype(F32) * gain1
    grad_embedded = (grad_residual + normalise_back(grad_normed, unit1, scale1)).astype(BF16)
    patches_ref[...] = dot_nt(grad_embedded, patch_ref[...]).astype(BF16)
    columns = column_ref[...]
    for lead in range(leads):
        turned = jnp.concatenate(
            [
                patches_ref[lead * pc : (lead + 1) * pc, inner * q_pad : (inner + 1) * q_pad]
                for inner in range(PATCH)
            ],
            axis=0,
        )
        pixels_ref[lead * q_pad : (lead + 1) * q_pad, :] = dot_tn(turned, columns).astype(BF16)
    order = match(wire_keys(sizes, rows_of(wire_rows)), patch_keys(sizes, cols_of(leads * q_pad)))
    moved = dot(order, pixels_ref[...]).astype(BF16)
    wire_out_ref[...] = moved.reshape(sizes.space, sizes.block, sizes.cols)

    qkv_grad_ref[...] = dot_tn(normed, grad_packed)
    me = me_ref[0]
    share = width // sizes.space
    for peer in range(sizes.space):
        at = slice(peer * share, (peer + 1) * share)
        pieces = [fc1_grad_ref[at, c * width : (c + 1) * width] for c in range(hidden_width // width)]
        wide = hidden_width // sizes.space
        pieces.append(fc2_grad_ref[peer * wide : (peer + 1) * wide, :])
        pieces += [qkv_grad_ref[at, c * width : (c + 1) * width] for c in range(3)]
        pieces.append(proj_grad_ref[at, :])
        grads_ref[me ^ peer] = jnp.concatenate(pieces, axis=0).astype(BF16)


def transformer(sizes, me, wire, cotangent, params):
    pos, patch, norm1, qkv, proj, norm2, fc1, fc2 = params
    tokens, width = pos.shape
    hidden_width = fc1.shape[1]
    count = sizes.per_dev * tokens
    share_rows = (qkv.size + proj.size + fc1.size + fc2.size) // (width * sizes.space)
    vmem = pl.BlockSpec(memory_space=pltpu.VMEM)
    return pl.pallas_call(
        functools.partial(block_kernel, sizes),
        in_specs=[pl.BlockSpec(memory_space=pltpu.SMEM)] + [vmem] * 10,
        out_specs=(vmem, vmem, vmem),
        out_shape=(
            jax.ShapeDtypeStruct(cotangent.shape, BF16),
            jax.ShapeDtypeStruct(wire.shape, BF16),
            jax.ShapeDtypeStruct((sizes.space, share_rows, width), BF16),
        ),
        scratch_shapes=[
            pltpu.VMEM((sizes.per_dev * sizes.patch_rows * sizes.q_pad, sizes.cols), BF16),
            pltpu.VMEM((count, PATCH * sizes.q_pad), BF16),
            pltpu.VMEM((sizes.cols, sizes.cols), BF16),
            pltpu.VMEM((count, 3 * width), BF16),
            pltpu.VMEM((sizes.per_dev * HEADS, tokens, tokens), F32),
            pltpu.VMEM((count, width), BF16),
            pltpu.VMEM((count, 3 * width), BF16),
            pltpu.VMEM(qkv.shape, F32),
            pltpu.VMEM(proj.shape, F32),
            pltpu.VMEM(fc1.shape, F32),
            pltpu.VMEM(fc2.shape, F32),
        ],
        compiler_params=pltpu.CompilerParams(vmem_limit_bytes=48 * MIB),
        cost_estimate=pl.CostEstimate(
            flops=6 * count * (patch.size + qkv.size + proj.size + fc1.size + fc2.size),
            bytes_accessed=16 * MIB,
            transcendentals=2 * count * hidden_width,
        ),
        name="transformer",
    )(me, wire, cotangent, pos, patch, norm1[None], qkv, proj, norm2[None], fc1, fc2)


def conv_weight_kernel(sizes, wire_ref, x_ref, out_ref, taps_ref, cross_ref, diag_ref):
    step = pl.program_id(0)
    wire_rows = sizes.space * sizes.block
    taps = TAPS * TAPS * COLOURS

    @pl.when(step == 0)
    def _():
        order = match(rows_of(sizes.ext * sizes.plane), tile_wire_keys(sizes, cols_of(wire_rows)))
        tile = dot(order, wire_ref[...].reshape(wire_rows, sizes.cols)).astype(BF16)
        for tap in range(TAPS):
            if tap == 1:
                moved = tile
            else:
                shift = match(rows_of(sizes.cols), cols_of(sizes.cols) + (1 - tap))
                moved = dot(tile, shift).astype(BF16)
            for ext in range(sizes.ext):
                at = ext * sizes.group + tap * sizes.plane
                taps_ref[at : at + sizes.plane, :] = moved[
                    ext * sizes.plane : (ext + 1) * sizes.plane
                ]

    x = x_ref[...].reshape(sizes.depth, sizes.cols)
    window = taps_ref[pl.ds(pl.multiple_of(step * sizes.group, 16), sizes.window), :]
    product = dot_nt(window, x)

    @pl.when(step == 0)
    def _():
        cross_ref[...] = product

    @pl.when(step > 0)
    def _():
        cross_ref[...] += product

    @pl.when(step == sizes.rows - 1)
    def _():
        diag_ref[...] = jnp.zeros(diag_ref.shape, F32)
        channel, frame_in = split(cols_of(sizes.depth), sizes.frames)
        lag = frame_in - rows_of(sizes.frames) + 2
        for tap in range(taps):
            cross = cross_ref[tap * sizes.frames : (tap + 1) * sizes.frames, :]
            row, rest = divmod(tap, TAPS * COLOURS)
            real = (TAPS - 1 - row) * TAPS * COLOURS + rest
            for a in range(TAPS):
                at = a * taps + real
                diag_ref[at : at + 1, :] = jnp.sum(
                    jnp.where(lag == a, cross, 0.0), axis=0, keepdims=True
                )
        spread = match(rows_of(out_ref.shape[1]), channel)
        left = diag_ref[...]
        total = jnp.zeros(out_ref.shape, F32)
        for _ in range(3):
            part = left.astype(BF16)
            left = left - part.astype(F32)
            total = total + dot_nt(part, spread)
        out_ref[...] = total


def conv_weight_grad(sizes, wire, x):
    taps = TAPS * TAPS * TAPS * COLOURS
    taps_pad = round_up(taps, 16)
    lanes = round_up(sizes.channels, 128)
    return pl.pallas_call(
        functools.partial(conv_weight_kernel, sizes),
        grid=(sizes.rows,),
        in_specs=[
            pl.BlockSpec(wire.shape, lambda h: (0, 0, 0)),
            pl.BlockSpec((sizes.channels, 1, sizes.frames, sizes.cols), lambda h: (0, h, 0, 0)),
        ],
        out_specs=(
            pl.BlockSpec((taps_pad, lanes), lambda h: (0, 0)),
            pl.BlockSpec((sizes.ext * sizes.group, sizes.cols), lambda h: (0, 0)),
        ),
        out_shape=(
            jax.ShapeDtypeStruct((taps_pad, lanes), F32),
            jax.ShapeDtypeStruct((sizes.ext * sizes.group, sizes.cols), BF16),
        ),
        scratch_shapes=[
            pltpu.VMEM((sizes.window, sizes.depth), F32),
            pltpu.VMEM((taps_pad, sizes.depth), F32),
        ],
        compiler_params=pltpu.CompilerParams(vmem_limit_bytes=48 * MIB),
        cost_estimate=pl.CostEstimate(
            flops=2 * sizes.rows * sizes.window * sizes.depth * sizes.cols,
            bytes_accessed=2 * x.size,
            transcendentals=0,
        ),
        name="conv_weight_grad",
    )(wire, x)


def feature_kernel(sizes, band_ref, taps_ref, out_ref):
    step = pl.program_id(0)
    window = taps_ref[pl.ds(pl.multiple_of(step * sizes.group, 16), sizes.window), :]
    out_ref[...] = dot(band_ref[...], window).astype(BF16).reshape(out_ref.shape)


def feature_gradient(sizes, band, taps):
    shape = (sizes.channels, sizes.rows, sizes.frames, sizes.cols)
    return pl.pallas_call(
        functools.partial(feature_kernel, sizes),
        grid=(sizes.rows,),
        in_specs=[
            pl.BlockSpec(band.shape, lambda h: (0, 0)),
            pl.BlockSpec(taps.shape, lambda h: (0, 0)),
        ],
        out_specs=pl.BlockSpec((shape[0], 1, shape[2], shape[3]), lambda h: (0, h, 0, 0)),
        out_shape=jax.ShapeDtypeStruct(shape, BF16),
        compiler_params=pltpu.CompilerParams(vmem_limit_bytes=48 * MIB),
        cost_estimate=pl.CostEstimate(
            flops=2 * sizes.rows * sizes.window * sizes.depth * sizes.cols,
            bytes_accessed=2 * math.prod(shape),
            transcendentals=0,
        ),
        name="feature_grad",
    )(band, taps)


def swap(values, axis, bit):
    return lax.ppermute(values, axis, [(i, i ^ (1 << bit)) for i in range(lax.axis_size(axis))])


def add(left, right):
    return (left.astype(F32) + right.astype(F32)).astype(BF16)


def reduce_blocks(blocks, bits):
    size = len(bits)
    blocks = blocks.reshape((2,) * size + blocks.shape[1:])
    while bits:
        bit, bits = bits[0], bits[1:]
        dim = blocks.ndim - 3 - sorted((bit,) + bits).index(bit)
        keep = lax.index_in_dim(blocks, 0, dim, keepdims=False)
        send = lax.index_in_dim(blocks, 1, dim, keepdims=False)
        blocks = add(keep, swap(send, "space", bit))
    return blocks


def sum_over_dp(values):
    index = lax.axis_index("dp")
    stages = (lax.axis_size("dp") - 1).bit_length()
    for bit in range(stages):
        mine = (index >> bit) & 1
        half = values.shape[0] // 2
        low, high = values[:half], values[half:]
        keep = jnp.where(mine == 0, low, high)
        send = jnp.where(mine == 0, high, low)
        values = add(keep, swap(send, "dp", bit))
    for bit in reversed(range(stages)):
        mine = (index >> bit) & 1
        other = swap(values, "dp", bit)
        values = jnp.where(
            mine == 0,
            jnp.concatenate([values, other], axis=0),
            jnp.concatenate([other, values], axis=0),
        )
    return values


def shards(
    features,
    conv_weight,
    out_grad,
    pos_embed,
    patch_weight,
    norm1,
    qkv_weight,
    proj_weight,
    norm2,
    fc1_weight,
    fc2_weight,
):
    space = lax.axis_size("space")
    sizes = Sizes(features, space)
    width = pos_embed.shape[1]
    hidden_width = fc1_weight.shape[1]
    me = lax.axis_index("space").astype(jnp.int32).reshape(1)
    x = features[0].transpose(0, 2, 1, 3)
    taps = conv_weight.reshape(-1, sizes.channels)

    wire = conv_forward(sizes, taps, x)
    wire = lax.all_to_all(wire, "space", split_axis=0, concat_axis=0, tiled=True)
    patch, band = prepare(sizes, taps, patch_weight)
    params = (pos_embed, patch, norm1, qkv_weight, proj_weight, norm2, fc1_weight, fc2_weight)
    block_out, wire_grad, grads = transformer(sizes, me, wire, out_grad[0], params)

    wire_grad = lax.all_to_all(wire_grad, "space", split_axis=0, concat_axis=0, tiled=True)
    conv_part, tap_rows = conv_weight_grad(sizes, wire_grad, x)
    feature_grad = feature_gradient(sizes, band, tap_rows)

    bits = tuple(range((space - 1).bit_length()))
    rows = grads.shape[1]
    half = rows // 2
    first = reduce_blocks(grads[:, :half], bits)
    second = reduce_blocks(grads[:, half:], bits[:1] + bits[2:] + bits[1:2])
    total = sum_over_dp(jnp.concatenate([first, second], axis=0)).astype(F32)

    share = width // space
    wide = hidden_width // space
    parts = hidden_width // width
    at = 0
    fc1_grad = jnp.concatenate([total[i * share : (i + 1) * share] for i in range(parts)], axis=1)
    at = parts * share
    fc2_grad = total[at : at + wide]
    at += wide
    qkv_grad = jnp.concatenate(
        [total[at + i * share : at + (i + 1) * share] for i in range(3)], axis=1
    )
    proj_grad = total[at + 3 * share :]

    conv_all = lax.all_to_all(
        jnp.broadcast_to(conv_part.astype(BF16)[None], (space,) + conv_part.shape),
        "space",
        split_axis=0,
        concat_axis=0,
        tiled=True,
    )
    conv_total = jnp.sum(conv_all.astype(F32), axis=0)
    for bit in range((lax.axis_size("dp") - 1).bit_length()):
        conv_total = conv_total + swap(conv_total, "dp", bit)
    conv_total = conv_total[: taps.shape[0], : sizes.channels].reshape(conv_weight.shape)

    return (
        block_out[None],
        feature_grad.transpose(0, 2, 1, 3)[None],
        conv_total,
        qkv_grad,
        proj_grad,
        fc1_grad,
        fc2_grad,
    )


def solution(mesh):
    placed = (
        P("dp", None, None, "space", None),
        P(),
        P("dp", "space", None, None),
        P(),
        P(),
        P(),
        P(),
        P(),
        P(),
        P(),
        P(),
    )
    return jax.shard_map(
        shards,
        mesh=mesh,
        in_specs=placed,
        out_specs=(
            P("dp", "space", None, None),
            P("dp", None, None, "space", None),
            P(),
            P("space", None),
            P("space", None),
            P("space", None),
            P("space", None),
        ),
        check_vma=False,
    )
```

profile of v0, /device:TPU:0, one launch (start us, length us, event | category | flops | bytes accessed | tf_op | source)
XLA Modules:
  0.0 135.8 jit_solution(3052866307004946980)
XLA Ops:
  0.6 0.8 reshape.43.weight_ref
  1.4 0.0 copy-start.16
  1.4 0.0 copy-start.3
  1.4 13.0 %conv_forward.1 = bf16[8,64,448]{2,1,0:T(8,128)(2,1)} custom-call(bf16[81,96]{1,0:T(8,128)(2,1)S(1)} %reshape.43.weight_ref, bf16[96,7,16,448]{3,2,1,0:T(8,128)(2,1)} %bitcast.71), custom_call_target="tpu_custom_call" | custom-call | flops 4161798144 | bytes 9633792 | tf_op jit(solution)/shard_map/conv_forward/pallas_call | solution.py:165
  14.4 5.2 %all-to-all-start = ((bf16[8,64,448]{2,1,0:T(8,128)(2,1)}), bf16[8,64,448]{2,1,0:T(8,128)(2,1)S(1)}, u32[]{:S(2)}, u32[]{:S(2)}) async-start(bf16[8,64,448]{2,1,0:T(8,128)(2,1)} %conv_forward.1), calls=%async_computation | async-start | bytes 1048576 | tf_op jit(solution)/shard_map/all_to_all | solution.py:632
  19.7 0.0 copy-start
  19.7 3.9 %prepare.1 = (bf16[896,384]{1,0:T(8,128)(2,1)S(1)}, bf16[1536,432]{1,0:T(8,128)(2,1)S(1)}) custom-call(bf16[81,96]{1,0:T(8,128)(2,1)S(1)} %reshape.43.weight_ref, bf16[588,384]{1,0:T(8,128)(2,1)S(1)} %copy-done.3), custom_call_target="tpu_custom_call" | custom-call | flops 4000000000 | bytes 4194304 | tf_op jit(solution)/shard_map/prepare/pallas_call | solution.py:213
  23.6 1.2 copy-done.7
  24.8 0.8 copy-done.9
  25.6 3.7 %all-to-all-done.wire_ref = bf16[8,64,448]{2,1,0:T(8,128)(2,1)S(1)} async-done(((bf16[8,64,448]{2,1,0:T(8,128)(2,1)}), bf16[8,64,448]{2,1,0:T(8,128)(2,1)S(1)}, u32[]{:S(2)}, u32[]{:S(2)}) %all-to-all-start) | async-done | bytes 458784 | tf_op jit(solution)/shard_map/all_to_all | solution.py:632
  29.4 0.0 copy-start.2
  29.4 1.2 copy-done.2
  30.5 1.0 copy-done.4
  31.5 0.9 copy-done.5
  32.4 1.1 copy-done.10
  33.5 18.5 %transformer.1 = (bf16[2,128,384]{2,1,0:T(8,128)(2,1)}, bf16[8,64,448]{2,1,0:T(8,128)(2,1)}, bf16[8,576,384]{2,1,0:T(8,128)(2,1)}) custom-call(s32[1]{0:T(128)} %bitcast.me_ref, bf16[8,64,448]{2,1,0:T(8,128)(2,1)S(1)} %all-to-all-done.wire_ref, bf16[2,128,384]{2,1,0:T(8,128)(2,1)S(1)} %bitcast.66, bf16[128,384]{1,0:T(8,128)(2,1)S(1)} %copy-done.6, ...), custom_call_target="tpu_custom_call" | custom-call | flops 3246391296 | bytes 16777216 | tf_op jit(solution)/shard_map/transformer/pallas_call | solution.py:420
  52.1 2.4 %fusion.7 = (bf16[8,288,384]{2,1,0:T(8,128)(2,1)S(1)}, bf16[8,288,384]{2,1,0:T(8,128)(2,1)S(1)}) fusion(bf16[8,576,384]{2,1,0:T(8,128)(2,1)} %get-tuple-element.20), kind=kLoop, calls=%fused_computation.35 | loop fusion | bytes 7077888 | tf_op jit(solution)/shard_map/slice | solution.py:645
  54.4 0.1 slice_bitcast_fusion
  54.5 0.1 collective-permute-start.5
  54.6 0.2 fusion.8
  54.8 0.1 copy.34
  54.9 0.6 collective-permute-start.2
  55.5 1.6 %collective-permute-done.5 = bf16[2,2,288,384]{3,2,1,0:T(8,128)(2,1)S(1)} collective-permute-done((bf16[2,2,288,384]{3,2,1,0:T(8,128)(2,1)S(1)}, bf16[2,2,288,384]{3,2,1,0:T(8,128)(2,1)S(1)}, u32[]{:S(2)}, u32[]{:S(2)}) %collective-permute-start.5) | collective-permute-done | bytes 884768 | tf_op jit(solution)/shard_map/ppermute | solution.py:570
  57.0 0.2 fusion
  57.3 0.6 collective-permute-start.6
  57.9 0.3 collective-permute-done.2
  58.3 0.2 fusion.1
  58.6 0.6 collective-permute-start.3
  59.2 10.4 %collective-permute-done.6 = bf16[2,288,384]{2,1,0:T(8,128)(2,1)S(1)} collective-permute-done((bf16[2,288,384]{2,1,0:T(8,128)(2,1)S(1)}, bf16[2,288,384]{2,1,0:T(8,128)(2,1)S(1)}, u32[]{:S(2)}, u32[]{:S(2)}) %collective-permute-start.6) | collective-permute-done | bytes 442400 | tf_op jit(solution)/shard_map/ppermute | solution.py:570
  69.6 0.1 fusion.2
  69.8 0.6 collective-permute-start.7
  70.4 0.5 collective-permute-done.3
  70.9 0.1 fusion.3
  71.0 0.0 copy-start.11
  71.0 0.9 collective-permute-start.4
  71.9 3.5 %all-to-all-start.1 = ((bf16[8,64,448]{2,1,0:T(8,128)(2,1)}), bf16[8,64,448]{2,1,0:T(8,128)(2,1)S(1)}, u32[]{:S(2)}, u32[]{:S(2)}) async-start(bf16[8,64,448]{2,1,0:T(8,128)(2,1)} %get-tuple-element.17), calls=%async_computation.1 | async-start | bytes 1048576 | tf_op jit(solution)/shard_map/all_to_all | solution.py:637
  75.5 1.0 collective-permute-done.7
  76.5 1.3 collective-permute-done.4
  77.7 0.8 broadcast_select_fusion
  78.5 1.6 %collective-permute-start.8 = (bf16[288,384]{1,0:T(8,128)(2,1)}, bf16[288,384]{1,0:T(8,128)(2,1)}, u32[]{:S(2)}, u32[]{:S(2)}) collective-permute-start(bf16[288,384]{1,0:T(8,128)(2,1)} %broadcast_select_fusion), channel_id=1, source_target_pairs={{0,8},{8,0},{16,24},{24,16},{1,9},{9,1},{17,25},{25,17},{2,10},{10... | collective-permute-start | bytes 663560 | tf_op jit(solution)/shard_map/ppermute | solution.py:570
  80.1 5.0 %all-to-all-done.1.wire_ref = bf16[8,64,448]{2,1,0:T(8,128)(2,1)S(1)} async-done(((bf16[8,64,448]{2,1,0:T(8,128)(2,1)}), bf16[8,64,448]{2,1,0:T(8,128)(2,1)S(1)}, u32[]{:S(2)}, u32[]{:S(2)}) %all-to-all-start.1) | async-done | bytes 458784 | tf_op jit(solution)/shard_map/all_to_all | solution.py:637
  85.1 13.0 %conv_weight_grad.1 = (f32[96,128]{1,0:T(8,128)S(1)}, bf16[1296,448]{1,0:T(8,128)(2,1)S(1)}) custom-call(bf16[8,64,448]{2,1,0:T(8,128)(2,1)S(1)} %all-to-all-done.1.wire_ref, bf16[96,7,16,448]{3,2,1,0:T(8,128)(2,1)} %bitcast.72), custom_call_target="tpu_custom_call" | custom-call | flops 4161798144 | bytes 9633792 | tf_op jit(solution)/shard_map/conv_weight_grad/pallas_call | solution.py:513
  98.2 0.7 broadcast_in_dim.22
  98.9 3.4 %all-to-all-start.2 = ((bf16[8,96,128]{2,1,0:T(8,128)(2,1)}), bf16[8,96,128]{2,1,0:T(8,128)(2,1)S(1)}, u32[]{:S(2)}, u32[]{:S(2)}) async-start(bf16[8,96,128]{2,1,0:T(8,128)(2,1)} %broadcast_in_dim.22), calls=%async_computation.2 | async-start | bytes 393216 | tf_op jit(solution)/shard_map/all_to_all | solution.py:661
  102.3 1.4 %add_convert_fusion = bf16[288,384]{1,0:T(8,128)(2,1)S(1)} fusion(bf16[288,384]{1,0:T(8,128)(2,1)} %collective-permute-done.8, pred[]{:T(512)S(6)} %eq.4, bf16[288,384]{1,0:T(8,128)(2,1)} %copy-done.14, bf16[2,288,384]{2,1,0:T(8,128)(2,1)} %copy-done.11, bf16[288,384]{1,0:T(8,128)(2,1)} %copy-done.13, bf16[2,288,384]{2,1,0:T(8,128)(2,1)S(1)} %fusion.2), kind=kLoop, calls=%fused_computation.22 | loop fusion | flops 1437696 | bytes 1327105 | tf_op jit(solution)/shard_map/convert_element_type | solution.py:574
  103.7 0.7 copy-done.12
  104.4 2.7 %collective-permute-start.9 = (bf16[144,384]{1,0:T(8,128)(2,1)S(1)}, bf16[144,384]{1,0:T(8,128)(2,1)S(1)}, u32[]{:S(2)}, u32[]{:S(2)}) collective-permute-start(bf16[144,384]{1,0:T(8,128)(2,1)S(1)} %broadcast_select_fusion.1), channel_id=1, source_target_pairs={{0,16},{8,24},{16,0},{24,8},{1,17},{9,25},{17,1},{25,9},{2,18},{10... | collective-permute-start | bytes 331784 | tf_op jit(solution)/shard_map/ppermute | solution.py:570
  107.1 1.4 all-to-all-done.2
  108.5 1.6 %collective-permute-start = (f32[96,128]{1,0:T(8,128)S(1)}, f32[96,128]{1,0:T(8,128)S(1)}, u32[]{:S(2)}, u32[]{:S(2)}) collective-permute-start(f32[96,128]{1,0:T(8,128)S(1)} %convert_reduce_fusion), channel_id=1, source_target_pairs={{0,8},{8,0},{16,24},{24,16},{1,9},{9,1},{17,25},{25,17},{2,10},{10... | collective-permute-start | bytes 147464 | tf_op jit(solution)/shard_map/ppermute | solution.py:570
  110.1 3.1 %collective-permute-done.9 = bf16[144,384]{1,0:T(8,128)(2,1)S(1)} collective-permute-done((bf16[144,384]{1,0:T(8,128)(2,1)S(1)}, bf16[144,384]{1,0:T(8,128)(2,1)S(1)}, u32[]{:S(2)}, u32[]{:S(2)}) %collective-permute-start.9) | collective-permute-done | bytes 110624 | tf_op jit(solution)/shard_map/ppermute | solution.py:570
  113.2 1.0 add_convert_fusion.1
  114.2 0.4 collective-permute-start.10
  114.6 8.5 %feature_grad.1 = bf16[96,7,16,448]{3,2,1,0:T(8,128)(2,1)} custom-call(bf16[1536,432]{1,0:T(8,128)(2,1)S(1)} %copy-done.8, bf16[1296,448]{1,0:T(8,128)(2,1)S(1)} %get-tuple-element.18.taps_ref), custom_call_target="tpu_custom_call" | custom-call | flops 4161798144 | bytes 9633792 | tf_op jit(solution)/shard_map/feature_grad/pallas_call | solution.py:550
  123.1 2.7 %collective-permute-start.1 = (f32[96,128]{1,0:T(8,128)S(1)}, f32[96,128]{1,0:T(8,128)S(1)}, u32[]{:S(2)}, u32[]{:S(2)}) collective-permute-start(f32[96,128]{1,0:T(8,128)S(1)} %add.30), channel_id=1, source_target_pairs={{0,16},{8,24},{16,0},{24,8},{1,17},{9,25},{17,1},{25,9},{2,18},{10... | collective-permute-start | bytes 147464 | tf_op jit(solution)/shard_map/ppermute | solution.py:570
  125.7 0.1 maximum_select_fusion.1
  125.8 1.2 collective-permute-start.11
  127.0 1.1 collective-permute-done.1
  128.2 0.6 reshape.44
  128.8 4.0 %collective-permute-done.11 = bf16[288,384]{1,0:T(8,128)(2,1)S(1)} collective-permute-done((bf16[288,384]{1,0:T(8,128)(2,1)S(1)}, bf16[288,384]{1,0:T(8,128)(2,1)S(1)}, u32[]{:S(2)}, u32[]{:S(2)}) %collective-permute-start.11) | collective-permute-done | bytes 221216 | tf_op jit(solution)/shard_map/ppermute | solution.py:570
  132.8 0.1 fusion.4
  132.9 0.7 slice.128
  133.7 0.7 fusion.9
  134.3 0.7 pad_maximum_fusion.1
  135.0 0.7 pad_maximum_fusion
  (36 shorter events, 0.3 us)
Async XLA Ops:
  1.4 18.2 %copy-start.15 = (f32[384]{0:T(512)S(1)}, f32[384]{0:T(512)}, u32[]{:S(2)}) copy-start(f32[384]{0:T(512)} %param.16) | copy-start | bytes 4612
  1.4 18.2 %copy-start.16 = (f32[384]{0:T(512)S(1)}, f32[384]{0:T(512)}, u32[]{:S(2)}) copy-start(f32[384]{0:T(512)} %param.19) | copy-start | bytes 4612
  1.4 18.2 %copy-start.3 = (bf16[588,384]{1,0:T(8,128)(2,1)S(1)}, bf16[588,384]{1,0:T(8,128)(2,1)}, u32[]{:S(2)}) copy-start(bf16[588,384]{1,0:T(8,128)(2,1)} %patch_ref.1) | copy-start | bytes 1354756
  14.4 14.9 %all-to-all-start = ((bf16[8,64,448]{2,1,0:T(8,128)(2,1)}), bf16[8,64,448]{2,1,0:T(8,128)(2,1)S(1)}, u32[]{:S(2)}, u32[]{:S(2)}) async-start(bf16[8,64,448]{2,1,0:T(8,128)(2,1)} %conv_forward.1), calls=%async_computation | async-start | bytes 1048576 | tf_op jit(solution)/shard_map/all_to_all | solution.py:632
  19.7 9.7 %copy-start = (bf16[384,1536]{1,0:T(8,128)(2,1)S(1)}, bf16[384,1536]{1,0:T(8,128)(2,1)}, u32[]{:S(2)}) copy-start(bf16[384,1536]{1,0:T(8,128)(2,1)} %fc1_ref.1) | copy-start | bytes 3538948
  19.7 9.7 %copy-start.1 = (bf16[1536,384]{1,0:T(8,128)(2,1)S(1)}, bf16[1536,384]{1,0:T(8,128)(2,1)}, u32[]{:S(2)}) copy-start(bf16[1536,384]{1,0:T(8,128)(2,1)} %fc2_ref.1) | copy-start | bytes 3538948
  19.7 9.7 %copy-start.6 = (bf16[128,384]{1,0:T(8,128)(2,1)S(1)}, bf16[128,384]{1,0:T(8,128)(2,1)}, u32[]{:S(2)}) copy-start(bf16[128,384]{1,0:T(8,128)(2,1)} %pos_ref.1) | copy-start | bytes 294916
  23.6 1.2 copy-start.7
  24.8 0.8 copy-start.9
  29.4 1.2 copy-start.2
  30.5 1.0 copy-start.4
  31.5 0.9 copy-start.5
  32.4 1.1 copy-start.10
  54.5 2.5 %collective-permute-start.5 = (bf16[2,2,288,384]{3,2,1,0:T(8,128)(2,1)S(1)}, bf16[2,2,288,384]{3,2,1,0:T(8,128)(2,1)S(1)}, u32[]{:S(2)}, u32[]{:S(2)}) collective-permute-start(bf16[2,2,288,384]{3,2,1,0:T(8,128)(2,1)S(1)} %slice_bitcast_fusion), channel_id=1, source_target_pairs={{0,1},{1,0},{2,3},{3,2},{4,5},{5,4},{6,7},{7,6},{8,9},{9,8},{10,11... | collective-permute-start | bytes 2654216 | tf_op jit(solution)/shard_map/ppermute | solution.py:570
  54.9 3.4 %collective-permute-start.2 = (bf16[2,2,288,384]{3,2,0,1:T(8,128)(2,1)S(1)}, bf16[2,2,288,384]{3,2,0,1:T(8,128)(2,1)S(1)}, u32[]{:S(2)}, u32[]{:S(2)}) collective-permute-start(bf16[2,2,288,384]{3,2,0,1:T(8,128)(2,1)S(1)} %bitcast.70), channel_id=1, source_target_pairs={{0,1},{1,0},{2,3},{3,2},{4,5},{5,4},{6,7},{7,6},{8,9},{9,8},{10,11... | collective-permute-start | bytes 2654216 | tf_op jit(solution)/shard_map/ppermute | solution.py:570
  57.3 12.3 %collective-permute-start.6 = (bf16[2,288,384]{2,1,0:T(8,128)(2,1)S(1)}, bf16[2,288,384]{2,1,0:T(8,128)(2,1)S(1)}, u32[]{:S(2)}, u32[]{:S(2)}) collective-permute-start(bf16[2,288,384]{2,1,0:T(8,128)(2,1)S(1)} %slice_bitcast_fusion.2), channel_id=1, source_target_pairs={{0,4},{1,5},{2,6},{3,7},{4,0},{5,1},{6,2},{7,3},{8,12},{9,13},{10,... | collective-permute-start | bytes 1327112 | tf_op jit(solution)/shard_map/ppermute | solution.py:570
  58.6 12.3 %collective-permute-start.3 = (bf16[2,288,384]{2,1,0:T(8,128)(2,1)S(1)}, bf16[2,288,384]{2,1,0:T(8,128)(2,1)S(1)}, u32[]{:S(2)}, u32[]{:S(2)}) collective-permute-start(bf16[2,288,384]{2,1,0:T(8,128)(2,1)S(1)} %slice_bitcast_fusion.4), channel_id=1, source_target_pairs={{0,2},{1,3},{2,0},{3,1},{4,6},{5,7},{6,4},{7,5},{8,10},{9,11},{10,... | collective-permute-start | bytes 1327112 | tf_op jit(solution)/shard_map/ppermute | solution.py:570
  69.8 6.7 %collective-permute-start.7 = (bf16[288,384]{1,0:T(8,128)(2,1)S(1)}, bf16[288,384]{1,0:T(8,128)(2,1)S(1)}, u32[]{:S(2)}, u32[]{:S(2)}) collective-permute-start(bf16[288,384]{1,0:T(8,128)(2,1)S(1)} %slice_bitcast_fusion.6), channel_id=1, source_target_pairs={{0,2},{1,3},{2,0},{3,1},{4,6},{5,7},{6,4},{7,5},{8,10},{9,11},{10,... | collective-permute-start | bytes 663560 | tf_op jit(solution)/shard_map/ppermute | solution.py:570
  71.0 9.1 %copy-start.11 = (bf16[2,288,384]{2,1,0:T(8,128)(2,1)}, bf16[2,288,384]{2,1,0:T(8,128)(2,1)S(1)}, u32[]{:S(2)}) copy-start(bf16[2,288,384]{2,1,0:T(8,128)(2,1)S(1)} %fusion.3) | copy-start | bytes 1327108
  71.0 6.7 %collective-permute-start.4 = (bf16[288,384]{1,0:T(8,128)(2,1)S(1)}, bf16[288,384]{1,0:T(8,128)(2,1)S(1)}, u32[]{:S(2)}, u32[]{:S(2)}) collective-permute-start(bf16[288,384]{1,0:T(8,128)(2,1)S(1)} %slice_bitcast_fusion.8), channel_id=1, source_target_pairs={{0,4},{1,5},{2,6},{3,7},{4,0},{5,1},{6,2},{7,3},{8,12},{9,13},{10,... | collective-permute-start | bytes 663560 | tf_op jit(solution)/shard_map/ppermute | solution.py:570
  71.9 13.2 %all-to-all-start.1 = ((bf16[8,64,448]{2,1,0:T(8,128)(2,1)}), bf16[8,64,448]{2,1,0:T(8,128)(2,1)S(1)}, u32[]{:S(2)}, u32[]{:S(2)}) async-start(bf16[8,64,448]{2,1,0:T(8,128)(2,1)} %get-tuple-element.17), calls=%async_computation.1 | async-start | bytes 1048576 | tf_op jit(solution)/shard_map/all_to_all | solution.py:637
  76.5 3.7 %copy-start.13 = (bf16[288,384]{1,0:T(8,128)(2,1)}, bf16[288,384]{1,0:T(8,128)(2,1)S(1)}, u32[]{:S(2)}) copy-start(bf16[288,384]{1,0:T(8,128)(2,1)S(1)} %collective-permute-done.7) | copy-start | bytes 663556
  77.7 2.4 %copy-start.14 = (bf16[288,384]{1,0:T(8,128)(2,1)}, bf16[288,384]{1,0:T(8,128)(2,1)S(1)}, u32[]{:S(2)}) copy-start(bf16[288,384]{1,0:T(8,128)(2,1)S(1)} %collective-permute-done.4) | copy-start | bytes 663556
  78.5 23.7 %collective-permute-start.8 = (bf16[288,384]{1,0:T(8,128)(2,1)}, bf16[288,384]{1,0:T(8,128)(2,1)}, u32[]{:S(2)}, u32[]{:S(2)}) collective-permute-start(bf16[288,384]{1,0:T(8,128)(2,1)} %broadcast_select_fusion), channel_id=1, source_target_pairs={{0,8},{8,0},{16,24},{24,16},{1,9},{9,1},{17,25},{25,17},{2,10},{10... | collective-permute-start | bytes 663560 | tf_op jit(solution)/shard_map/ppermute | solution.py:570
  98.1 16.4 %copy-start.8 = (bf16[1536,432]{1,0:T(8,128)(2,1)S(1)}, bf16[1536,432]{1,0:T(8,128)(2,1)}, u32[]{:S(2)}) copy-start(bf16[1536,432]{1,0:T(8,128)(2,1)} %copy-done.7) | copy-start | bytes 3981316
  98.9 9.6 %all-to-all-start.2 = ((bf16[8,96,128]{2,1,0:T(8,128)(2,1)}), bf16[8,96,128]{2,1,0:T(8,128)(2,1)S(1)}, u32[]{:S(2)}, u32[]{:S(2)}) async-start(bf16[8,96,128]{2,1,0:T(8,128)(2,1)} %broadcast_in_dim.22), calls=%async_computation.2 | async-start | bytes 393216 | tf_op jit(solution)/shard_map/all_to_all | solution.py:661
  103.7 0.7 copy-start.12
  104.4 8.8 %collective-permute-start.9 = (bf16[144,384]{1,0:T(8,128)(2,1)S(1)}, bf16[144,384]{1,0:T(8,128)(2,1)S(1)}, u32[]{:S(2)}, u32[]{:S(2)}) collective-permute-start(bf16[144,384]{1,0:T(8,128)(2,1)S(1)} %broadcast_select_fusion.1), channel_id=1, source_target_pairs={{0,16},{8,24},{16,0},{24,8},{1,17},{9,25},{17,1},{25,9},{2,18},{10... | collective-permute-start | bytes 331784 | tf_op jit(solution)/shard_map/ppermute | solution.py:570
  108.5 14.6 %collective-permute-start = (f32[96,128]{1,0:T(8,128)S(1)}, f32[96,128]{1,0:T(8,128)S(1)}, u32[]{:S(2)}, u32[]{:S(2)}) collective-permute-start(f32[96,128]{1,0:T(8,128)S(1)} %convert_reduce_fusion), channel_id=1, source_target_pairs={{0,8},{8,0},{16,24},{24,16},{1,9},{9,1},{17,25},{25,17},{2,10},{10... | collective-permute-start | bytes 147464 | tf_op jit(solution)/shard_map/ppermute | solution.py:570
  114.2 11.6 %collective-permute-start.10 = (bf16[144,384]{1,0:T(8,128)(2,1)S(1)}, bf16[144,384]{1,0:T(8,128)(2,1)S(1)}, u32[]{:S(2)}, u32[]{:S(2)}) collective-permute-start(bf16[144,384]{1,0:T(8,128)(2,1)S(1)} %add_convert_fusion.1), channel_id=1, source_target_pairs={{0,16},{8,24},{16,0},{24,8},{1,17},{9,25},{17,1},{25,9},{2,18},{10... | collective-permute-start | bytes 331784 | tf_op jit(solution)/shard_map/ppermute | solution.py:570
  123.1 5.1 %collective-permute-start.1 = (f32[96,128]{1,0:T(8,128)S(1)}, f32[96,128]{1,0:T(8,128)S(1)}, u32[]{:S(2)}, u32[]{:S(2)}) collective-permute-start(f32[96,128]{1,0:T(8,128)S(1)} %add.30), channel_id=1, source_target_pairs={{0,16},{8,24},{16,0},{24,8},{1,17},{9,25},{17,1},{25,9},{2,18},{10... | collective-permute-start | bytes 147464 | tf_op jit(solution)/shard_map/ppermute | solution.py:570
  125.8 7.0 %collective-permute-start.11 = (bf16[288,384]{1,0:T(8,128)(2,1)S(1)}, bf16[288,384]{1,0:T(8,128)(2,1)S(1)}, u32[]{:S(2)}, u32[]{:S(2)}) collective-permute-start(bf16[288,384]{1,0:T(8,128)(2,1)S(1)} %maximum_select_fusion.1), channel_id=1, source_target_pairs={{0,8},{8,0},{16,24},{24,16},{1,9},{9,1},{17,25},{25,17},{2,10},{10... | collective-permute-start | bytes 663560 | tf_op jit(solution)/shard_map/ppermute | solution.py:570
where the time goes:
time: 137 us; the launch traced here: 136 us
  Pallas kernels  56.9 us (42%)
  waiting for transfers between devices  33.4 us (24%)
  starting transfers between devices  25.7 us (19%)
  local copies, waits for them, and re-layouts  13.3 us (10%)
  other arithmetic  5.55 us (4%)
    ppermute x12, waiting for transfers between devices, swap(): lax.ppermute(values, axis, [(i, i ^ 1 << bit) for i in range(lax.axis_siz...  23.3 us
    pallas_call x1, Pallas kernels, transformer(): pl.pallas_call(functools.partial(block_kernel, sizes), in_specs=[pl.Block...  18.5 us
    ppermute x12, starting transfers between devices, swap(): lax.ppermute(values, axis, [(i, i ^ 1 << bit) for i in range(lax.axis_siz...  13.6 us
    pallas_call x1, Pallas kernels, conv_weight_grad(): pl.pallas_call(functools.partial(conv_weight_kernel, sizes), grid=(sizes....  13 us
    pallas_call x1, Pallas kernels, conv_forward(): pl.pallas_call(functools.partial(conv_forward_kernel, sizes), grid=(sizes...  13 us
    pallas_call x1, Pallas kernels, feature_gradient(): pl.pallas_call(functools.partial(feature_kernel, sizes), grid=(sizes.rows...  8.48 us
    unnamed x35, local copies, waits for them, and re-layouts  7.01 us
    all_to_all x1, starting transfers between devices, shards(): lax.all_to_all(wire, 'space', split_axis=0, concat_axis=0, tiled=True)  5.17 us
  transfers between devices with their start and end apart: 15, of which 12 were waited for; matrix products, arithmetic and copies ran while one was open for 4% of the time, Pallas kernels for 19%

commit v1 on v0

v1 whole, which is shorter than its diff:
```python
import functools
import math

import jax
import jax.numpy as jnp
from jax import lax
from jax.experimental import pallas as pl
from jax.experimental.pallas import tpu as pltpu
from jax.sharding import PartitionSpec as P

HEADS = 6
PATCH = 14
COLOURS = 3
TAPS = 3
F32 = jnp.float32
BF16 = jnp.bfloat16
MIB = 1 << 20
VMEM = pl.BlockSpec(memory_space=pltpu.VMEM)
SMEM = pl.BlockSpec(memory_space=pltpu.SMEM)
HBM = pl.BlockSpec(memory_space=pltpu.HBM)


def in_hbm(array):
    return pltpu.with_memory_space_constraint(array, pltpu.HBM)


def dot(a, b):
    return jnp.dot(a, b, preferred_element_type=F32)


def dot_nt(a, b):
    return lax.dot_general(a, b, (((1,), (1,)), ((), ())), preferred_element_type=F32)


def dot_tn(a, b):
    return lax.dot_general(a, b, (((0,), (0,)), ((), ())), preferred_element_type=F32)


def split(index, size):
    if size & (size - 1) == 0:
        shift = size.bit_length() - 1
        return index >> shift, index & (size - 1)
    high = jnp.floor((index.astype(F32) + 0.5) * (1.0 / size)).astype(jnp.int32)
    return high, index - high * size


def rows_of(count):
    return lax.broadcasted_iota(jnp.int32, (count, 1), 0)


def cols_of(count):
    return lax.broadcasted_iota(jnp.int32, (1, count), 1)


def match(left, right):
    return jnp.where(left == right, 1.0, 0.0).astype(BF16)


def round_up(value, unit):
    return -(-value // unit) * unit


class Sizes:
    def __init__(self, features, space):
        self.space = space
        self.channels, self.frames, self.rows, self.cols = features.shape[1:]
        self.per_dev = self.frames // space
        self.ext = self.rows + 2
        self.height = self.rows * space
        self.patch_rows = self.height // PATCH
        self.patch_cols = self.cols // PATCH
        self.tokens = self.patch_rows * self.patch_cols
        self.block = round_up(self.ext * COLOURS * self.per_dev, 16)
        self.q_used = COLOURS * PATCH
        self.q_pad = round_up(self.q_used, 64)
        self.plane = COLOURS * self.frames
        self.group = TAPS * self.plane
        self.window = TAPS * self.group
        self.depth = self.channels * self.frames


def wire_keys(sizes, index):
    peer, rest = split(index, sizes.block)
    plane, frame = split(rest, sizes.per_dev)
    ext, colour = split(plane, COLOURS)
    key = (frame * COLOURS + colour) * 4096 + peer * sizes.rows + ext
    return jnp.where(plane < sizes.ext * COLOURS, key, -2)


def patch_keys(sizes, index):
    lead, q = split(index, sizes.q_pad)
    frame, patch_row = split(lead, sizes.patch_rows)
    colour, row = split(q, PATCH)
    key = (frame * COLOURS + colour) * 4096 + patch_row * PATCH + row + 1
    return jnp.where(q < sizes.q_used, key, -1)


def tile_keys(sizes, index):
    return index


def tile_wire_keys(sizes, index):
    peer, rest = split(index, sizes.block)
    plane, frame = split(rest, sizes.per_dev)
    key = plane * sizes.frames + peer * sizes.per_dev + frame
    return jnp.where(plane < sizes.ext * COLOURS, key, -2)


def flipped(tap):
    row, _ = split(tap, TAPS * COLOURS)
    return tap + (TAPS - 1 - 2 * row) * (TAPS * COLOURS)


def column_order(sizes):
    inner, patch = split(rows_of(sizes.cols), sizes.patch_cols)
    return match(patch * PATCH + inner, cols_of(sizes.cols))


def conv_forward_kernel(
    sizes, weight_ref, x_hbm, out_ref, x_ref, band_ref, acc_ref, plane_ref, sems
):
    taps = TAPS * TAPS * COLOURS

    def arrival(row):
        return pltpu.make_async_copy(x_hbm.at[:, row], x_ref.at[row], sems.at[row])

    for row in range(sizes.rows):
        arrival(row).start()

    channel, frame_in = split(cols_of(sizes.depth), sizes.frames)
    spread = match(rows_of(sizes.channels), channel)
    wide = dot(weight_ref[...], spread)
    lag = frame_in - rows_of(sizes.frames) + 2
    here = [lag == a for a in range(TAPS)]
    for tap in range(taps):
        row, rest = divmod(tap, TAPS * COLOURS)
        real = (TAPS - 1 - row) * TAPS * COLOURS + rest
        block = jnp.zeros((sizes.frames, sizes.depth), F32)
        for a in range(TAPS):
            at = a * taps + real
            block = jnp.where(here[a], wide[at : at + 1, :], block)
        band_ref[tap * sizes.frames : (tap + 1) * sizes.frames, :] = block.astype(BF16)
    acc_ref[...] = jnp.zeros(acc_ref.shape, F32)

    def step(row, carry):
        arrival(row).wait()
        x = x_ref[row].reshape(sizes.depth, sizes.cols)
        at = pl.ds(pl.multiple_of(row * sizes.group, 16), sizes.window)
        acc_ref[at, :] += dot(band_ref[...], x)
        return carry

    lax.fori_loop(0, sizes.rows, step, 0)

    zero = jnp.zeros((sizes.plane, 1), F32)
    for ext in range(sizes.ext):
        at = ext * sizes.group
        first = acc_ref[at : at + sizes.plane, :]
        second = acc_ref[at + sizes.plane : at + 2 * sizes.plane, :]
        third = acc_ref[at + 2 * sizes.plane : at + 3 * sizes.plane, :]
        first = jnp.concatenate([zero, first[:, : sizes.cols - 1]], axis=1)
        third = jnp.concatenate([third[:, 1:], zero], axis=1)
        plane_ref[ext * sizes.plane : (ext + 1) * sizes.plane, :] = (
            first + second + third
        ).astype(BF16)
    wire = tile_wire_keys(sizes, rows_of(sizes.space * sizes.block))
    order = match(wire, cols_of(sizes.ext * sizes.plane))
    moved = dot(order, plane_ref[...]).astype(BF16)
    out_ref[...] = moved.reshape(sizes.space, sizes.block, sizes.cols)


def conv_forward(sizes, weight, x):
    return pl.pallas_call(
        functools.partial(conv_forward_kernel, sizes),
        in_specs=[VMEM, HBM],
        out_specs=VMEM,
        out_shape=jax.ShapeDtypeStruct((sizes.space, sizes.block, sizes.cols), BF16),
        scratch_shapes=[
            pltpu.VMEM((sizes.rows, sizes.channels, sizes.frames, sizes.cols), BF16),
            pltpu.VMEM((sizes.window, sizes.depth), BF16),
            pltpu.VMEM((sizes.ext * sizes.group, sizes.cols), F32),
            pltpu.VMEM((sizes.ext * sizes.plane, sizes.cols), BF16),
            pltpu.SemaphoreType.DMA((sizes.rows,)),
        ],
        compiler_params=pltpu.CompilerParams(vmem_limit_bytes=32 * MIB),
        cost_estimate=pl.CostEstimate(
            flops=2 * sizes.rows * sizes.window * sizes.depth * sizes.cols,
            bytes_accessed=2 * x.size,
            transcendentals=0,
        ),
        name="conv_forward",
    )(weight, x)


def prepare_kernel(sizes, weight_ref, patch_ref, patch_out_ref, band_ref):
    step = pl.program_id(0)
    taps = TAPS * TAPS * COLOURS

    @pl.when(step == 0)
    def _():
        inner, q = split(rows_of(PATCH * sizes.q_pad), sizes.q_pad)
        source = jnp.where(q < sizes.q_used, q * PATCH + inner, -1)
        order = match(source, cols_of(patch_ref.shape[0]))
        patch_out_ref[...] = dot(order, patch_ref[...]).astype(BF16)

    chunk = band_ref.shape[0]
    tap, frame_in = split(cols_of(sizes.window), sizes.frames)
    pick = match(rows_of(taps), flipped(tap))
    channel, frame_out = split(rows_of(chunk) + step * chunk, sizes.frames)
    spread = match(channel, cols_of(sizes.channels))
    lag = frame_out - frame_in + 2
    total = None
    for a in range(TAPS):
        weight = weight_ref[a * taps : (a + 1) * taps, :]
        wide = dot(spread, dot_tn(weight, pick).astype(BF16))
        wide = jnp.where(lag == a, wide, 0.0)
        total = wide if total is None else total + wide
    band_ref[...] = total.astype(BF16)


def prepare(sizes, weight, patch_weight):
    width = patch_weight.shape[1]
    steps = 4
    patch_shape = (PATCH * sizes.q_pad, width)
    return pl.pallas_call(
        functools.partial(prepare_kernel, sizes),
        grid=(steps,),
        in_specs=[
            pl.BlockSpec(weight.shape, lambda i: (0, 0)),
            pl.BlockSpec(patch_weight.shape, lambda i: (0, 0)),
        ],
        out_specs=(
            pl.BlockSpec(patch_shape, lambda i: (0, 0)),
            pl.BlockSpec((sizes.depth // steps, sizes.window), lambda i: (i, 0)),
        ),
        out_shape=(
            pltpu.HBM(patch_shape, BF16),
            pltpu.HBM((sizes.depth, sizes.window), BF16),
        ),
        compiler_params=pltpu.CompilerParams(vmem_limit_bytes=24 * MIB),
        cost_estimate=pl.CostEstimate(
            flops=4 * 10**9, bytes_accessed=4 * MIB, transcendentals=0
        ),
        name="prepare",
    )(weight, patch_weight)


def normalise(values):
    average = jnp.mean(values, axis=-1, keepdims=True)
    centered = values - average
    variance = jnp.mean(centered * centered, axis=-1, keepdims=True)
    scale = lax.rsqrt(variance + 1e-06)
    return centered * scale, scale


def normalise_back(grad, unit, scale):
    mean_grad = jnp.mean(grad, axis=-1, keepdims=True)
    mean_both = jnp.mean(grad * unit, axis=-1, keepdims=True)
    return scale * (grad - mean_grad - unit * mean_both)


def fetch(pairs, sems):
    copies = [pltpu.make_async_copy(src, dst, sems.at[i]) for i, (src, dst) in enumerate(pairs)]
    for copy in copies:
        copy.start()
    return copies


def first_kernel(
    sizes,
    wire_ref,
    norm1_ref,
    norm2_ref,
    patch_hbm,
    pos_hbm,
    cotangent_hbm,
    qkv_hbm,
    proj_hbm,
    fc1_hbm,
    fc2_hbm,
    out_ref,
    normed_ref,
    packed_ref,
    probs_ref,
    attended_ref,
    unit_ref,
    scale_ref,
    grad_ref,
    normed2_ref,
    hidden_ref,
    grad_before_ref,
    pixels_ref,
    patches_ref,
    *held,
):
    fixed = (patch_hbm, pos_hbm, cotangent_hbm, qkv_hbm, proj_hbm, fc1_hbm, fc2_hbm)
    arrivals = fetch(tuple(zip(fixed, held[:-1])), held[-1])
    patch_ref, pos_ref, cotangent_ref, qkv_ref, proj_ref, fc1_ref, fc2_ref = held[:-1]
    tokens, width = pos_ref.shape
    frames = sizes.per_dev
    count = frames * tokens
    hidden_width = fc1_ref.shape[1]
    head = width // HEADS
    wire_rows = sizes.space * sizes.block
    leads = frames * sizes.patch_rows
    q_pad = sizes.q_pad
    pc = sizes.patch_cols

    order = match(patch_keys(sizes, rows_of(leads * q_pad)), wire_keys(sizes, cols_of(wire_rows)))
    pixels_ref[...] = dot(order, wire_ref[...].reshape(wire_rows, sizes.cols)).astype(BF16)
    columns = column_order(sizes)
    for lead in range(leads):
        turned = dot_nt(columns, pixels_ref[lead * q_pad : (lead + 1) * q_pad, :])
        for inner in range(PATCH):
            patches_ref[lead * pc : (lead + 1) * pc, inner * q_pad : (inner + 1) * q_pad] = turned[
                inner * pc : (inner + 1) * pc, :
            ].astype(BF16)

    for arrival in arrivals:
        arrival.wait()
    pos = pos_ref[...].astype(F32)
    embedded = dot(patches_ref[...], patch_ref[...])
    embedded = embedded + (pos if frames == 1 else jnp.concatenate([pos] * frames, axis=0))
    unit1, scale1 = normalise(embedded)
    unit_ref[...] = unit1
    scale_ref[...] = scale1
    normed = (unit1 * norm1_ref[...]).astype(BF16)
    normed_ref[...] = normed
    packed_ref[...] = dot(normed, qkv_ref[...]).astype(BF16)

    lanes = min(128, width)
    per_group = lanes // head
    lane_head, _ = split(cols_of(lanes), head)
    inv = 1.0 / float(head) ** 0.5
    for frame in range(frames):
        at = slice(frame * tokens, (frame + 1) * tokens)
        for group in range(width // lanes):
            cut = slice(group * lanes, (group + 1) * lanes)
            queries = packed_ref[at, cut]
            keys_in = packed_ref[at, width + group * lanes : width + (group + 1) * lanes]
            values_in = packed_ref[at, 2 * width + group * lanes : 2 * width + (group + 1) * lanes]
            joined = None
            for sub in range(per_group):
                mine = lane_head == sub
                masked = queries * jnp.where(mine, 1.0, 0.0).astype(BF16)
                scores = dot_nt(masked, keys_in) * inv
                scores = jnp.exp(scores - jnp.max(scores, axis=-1, keepdims=True))
                probs = scores / jnp.sum(scores, axis=-1, keepdims=True)
                probs_ref[(frame * HEADS) + group * per_group + sub] = probs
                value = dot(probs.astype(BF16), values_in)
                joined = value if joined is None else jnp.where(mine, value, joined)
            attended_ref[at, cut] = joined.astype(BF16)

    residual = embedded + dot(attended_ref[...], proj_ref[...])
    unit2, scale2 = normalise(residual)
    gain2 = norm2_ref[...]
    normed2 = (unit2 * gain2).astype(BF16)
    normed2_ref[...] = normed2
    cotangent = cotangent_ref[...].reshape(count, width)

    chunk = width
    result = residual
    grad_normed2 = None
    for part in range(hidden_width // chunk):
        cut = slice(part * chunk, (part + 1) * chunk)
        before = dot(normed2, fc1_ref[:, cut])
        cdf = 0.5 + 0.5 * lax.erf(before * math.sqrt(0.5))
        hidden = (before * cdf).astype(BF16)
        result = result + dot(hidden, fc2_ref[cut, :])
        slope = cdf + before * (jnp.exp(-0.5 * before * before) * (1.0 / math.sqrt(2.0 * math.pi)))
        grad_hidden = dot_nt(cotangent, fc2_ref[cut, :]).astype(BF16)
        grad_before = (grad_hidden.astype(F32) * slope).astype(BF16)
        hidden_ref[:, cut] = hidden
        grad_before_ref[:, cut] = grad_before
        piece = dot_nt(grad_before, fc1_ref[:, cut])
        grad_normed2 = piece if grad_normed2 is None else grad_normed2 + piece
    out_ref[...] = result.astype(BF16).reshape(frames, tokens, width)

    grad_normed2 = grad_normed2.astype(BF16).astype(F32) * gain2
    grad_ref[...] = cotangent.astype(F32) + normalise_back(grad_normed2, unit2, scale2)


def second_kernel(
    sizes,
    packed_ref,
    probs_ref,
    grad_ref,
    unit_ref,
    scale_ref,
    norm1_ref,
    patch_hbm,
    qkv_hbm,
    proj_hbm,
    wire_hbm,
    grad_packed_ref,
    grad_att_ref,
    pixels_ref,
    patches_ref,
    wire_out_ref,
    patch_ref,
    qkv_ref,
    proj_ref,
    sems,
    wire_sem,
):
    pairs = ((proj_hbm, proj_ref), (qkv_hbm, qkv_ref), (patch_hbm, patch_ref))
    arrivals = fetch(pairs, sems)
    arrivals[0].wait()
    count, width = grad_ref.shape
    frames = sizes.per_dev
    tokens = count // frames
    head = width // HEADS
    wire_rows = sizes.space * sizes.block
    leads = frames * sizes.patch_rows
    q_pad = sizes.q_pad
    pc = sizes.patch_cols
    lanes = min(128, width)
    per_group = lanes // head
    lane_head, _ = split(cols_of(lanes), head)
    inv = 1.0 / float(head) ** 0.5

    grad_residual = grad_ref[...]
    grad_att_ref[...] = dot_nt(grad_residual.astype(BF16), proj_ref[...]).astype(BF16)
    for frame in range(frames):
        at = slice(frame * tokens, (frame + 1) * tokens)
        for group in range(width // lanes):
            cut = slice(group * lanes, (group + 1) * lanes)
            cut_k = slice(width + group * lanes, width + (group + 1) * lanes)
            cut_v = slice(2 * width + group * lanes, 2 * width + (group + 1) * lanes)
            queries = packed_ref[at, cut]
            keys_in = packed_ref[at, cut_k]
            values_in = packed_ref[at, cut_v]
            grad_att = grad_att_ref[at, cut]
            grad_q = grad_k = grad_v = None
            for sub in range(per_group):
                mine = lane_head == sub
                mask = jnp.where(mine, 1.0, 0.0).astype(BF16)
                masked_q = queries * mask
                masked_g = grad_att * mask
                probs = probs_ref[(frame * HEADS) + group * per_group + sub]
                probs_b = probs.astype(BF16)
                grad_probs = dot_nt(masked_g, values_in).astype(BF16).astype(F32)
                inner = jnp.sum(grad_probs * probs, axis=-1, keepdims=True)
                grad_scores = (probs * (grad_probs - inner) * inv).astype(BF16)
                one_q = dot(grad_scores, keys_in)
                one_k = dot_tn(grad_scores, masked_q)
                one_v = dot_tn(probs_b, masked_g)
                grad_q = one_q if grad_q is None else jnp.where(mine, one_q, grad_q)
                grad_k = one_k if grad_k is None else grad_k + one_k
                grad_v = one_v if grad_v is None else grad_v + one_v
            grad_packed_ref[at, cut] = grad_q.astype(BF16)
            grad_packed_ref[at, cut_k] = grad_k.astype(BF16)
            grad_packed_ref[at, cut_v] = grad_v.astype(BF16)

    for arrival in arrivals[1:]:
        arrival.wait()
    grad_normed = dot_nt(grad_packed_ref[...], qkv_ref[...]).astype(BF16).astype(F32) * norm1_ref[...]
    back = normalise_back(grad_normed, unit_ref[...], scale_ref[...])
    grad_embedded = (grad_residual + back).astype(BF16)
    patches_ref[...] = dot_nt(grad_embedded, patch_ref[...]).astype(BF16)
    columns = column_order(sizes)
    for lead in range(leads):
        turned = jnp.concatenate(
            [
                patches_ref[lead * pc : (lead + 1) * pc, inner * q_pad : (inner + 1) * q_pad]
                for inner in range(PATCH)
            ],
            axis=0,
        )
        pixels_ref[lead * q_pad : (lead + 1) * q_pad, :] = dot_tn(turned, columns).astype(BF16)
    order = match(wire_keys(sizes, rows_of(wire_rows)), patch_keys(sizes, cols_of(leads * q_pad)))
    moved = dot(order, pixels_ref[...]).astype(BF16)
    wire_out_ref[...] = moved.reshape(sizes.space, sizes.block, sizes.cols)
    leave = pltpu.make_async_copy(wire_out_ref, wire_hbm, wire_sem)
    leave.start()
    leave.wait()


def third_kernel(
    space,
    me_ref,
    normed_ref,
    grad_packed_ref,
    attended_ref,
    grad_ref,
    normed2_ref,
    grad_before_ref,
    hidden_ref,
    cotangent_ref,
    keep_ref,
    send_ref,
    qkv_grad_ref,
    proj_grad_ref,
    fc1_grad_ref,
    fc2_grad_ref,
):
    count, width = grad_ref.shape
    hidden_width = hidden_ref.shape[1]
    qkv_grad_ref[...] = dot_tn(normed_ref[...], grad_packed_ref[...])
    proj_grad_ref[...] = dot_tn(attended_ref[...], grad_ref[...].astype(BF16))
    fc1_grad_ref[...] = dot_tn(normed2_ref[...], grad_before_ref[...])
    fc2_grad_ref[...] = dot_tn(hidden_ref[...], cotangent_ref[...].reshape(count, width))
    share = width // space
    pieces = [(fc1_grad_ref, share, c) for c in range(0, hidden_width, width)]
    pieces.append((fc2_grad_ref, hidden_width // space, 0))
    pieces += [(qkv_grad_ref, share, c) for c in range(0, 3 * width, width)]
    pieces.append((proj_grad_ref, share, 0))
    spare = keep_ref.shape[1] - sum(rows for _, rows, _ in pieces)
    for chip in range(space // 2):
        for other, target in ((0, keep_ref), (1, send_ref)):
            peer = me_ref[0] ^ (2 * chip + other)
            blocks = [
                ref[pl.ds(pl.multiple_of(peer * rows, 8), rows), column : column + width]
                for ref, rows, column in pieces
            ]
            if spare:
                blocks.append(jnp.zeros((spare, width), F32))
            target[chip] = jnp.concatenate(blocks, axis=0).astype(BF16)


def transformer(sizes, copies, me, wire, cotangent, params):
    pos, patch, norm1, qkv, proj, norm2, fc1, fc2 = params
    tokens, width = pos.shape
    hidden_width = fc1.shape[1]
    count = sizes.per_dev * tokens
    pixel_shape = (sizes.per_dev * sizes.patch_rows * sizes.q_pad, sizes.cols)
    patches_shape = (count, PATCH * sizes.q_pad)
    norm1, norm2 = norm1[None], norm2[None]

    def held(*arrays):
        return [pltpu.VMEM(array.shape, array.dtype) for array in arrays] + [
            pltpu.SemaphoreType.DMA((len(arrays),))
        ]

    tall = jax.ShapeDtypeStruct((count, width), BF16)
    wide = jax.ShapeDtypeStruct((count, hidden_width), BF16)
    (
        block_out,
        normed,
        packed,
        probs,
        attended,
        unit,
        scale,
        grad,
        normed2,
        hidden,
        grad_before,
    ) = pl.pallas_call(
        functools.partial(first_kernel, sizes),
        in_specs=[VMEM] * 3 + [HBM] * 7,
        out_specs=(VMEM,) * 11,
        out_shape=(
            jax.ShapeDtypeStruct(cotangent.shape, BF16),
            tall,
            jax.ShapeDtypeStruct((count, 3 * width), BF16),
            jax.ShapeDtypeStruct((sizes.per_dev * HEADS, tokens, tokens), F32),
            tall,
            jax.ShapeDtypeStruct((count, width), F32),
            jax.ShapeDtypeStruct((count, 1), F32),
            jax.ShapeDtypeStruct((count, width), F32),
            tall,
            wide,
            wide,
        ),
        scratch_shapes=[
            pltpu.VMEM(pixel_shape, BF16),
            pltpu.VMEM(patches_shape, BF16),
        ]
        + held(patch, pos, cotangent, qkv, proj, fc1, fc2),
        compiler_params=pltpu.CompilerParams(vmem_limit_bytes=24 * MIB),
        cost_estimate=pl.CostEstimate(
            flops=4 * count * (patch.size + qkv.size + proj.size + fc1.size + fc2.size),
            bytes_accessed=12 * MIB,
            transcendentals=2 * count * hidden_width,
        ),
        name="block_forward",
    )(wire, norm1, norm2, patch, pos, cotangent, qkv, proj, fc1, fc2)

    wire_grad, grad_packed = pl.pallas_call(
        functools.partial(second_kernel, sizes),
        in_specs=[VMEM] * 6 + [HBM] * 3,
        out_specs=(HBM, VMEM),
        out_shape=(
            pltpu.HBM(wire.shape, BF16),
            jax.ShapeDtypeStruct((count, 3 * width), BF16),
        ),
        scratch_shapes=[
            pltpu.VMEM((count, width), BF16),
            pltpu.VMEM(pixel_shape, BF16),
            pltpu.VMEM(patches_shape, BF16),
            pltpu.VMEM(wire.shape, BF16),
        ]
        + held(patch, qkv, proj)
        + [pltpu.SemaphoreType.DMA(())],
        compiler_params=pltpu.CompilerParams(vmem_limit_bytes=20 * MIB),
        cost_estimate=pl.CostEstimate(
            flops=4 * count * (patch.size + qkv.size + proj.size),
            bytes_accessed=6 * MIB,
            transcendentals=0,
        ),
        name="block_backward",
    )(packed, probs, grad, unit, scale, norm1, patch, qkv, proj)

    total = qkv.size + proj.size + fc1.size + fc2.size
    rows = round_up(total // (width * sizes.space), 16 * copies)
    shares = jax.ShapeDtypeStruct((sizes.space // 2, rows, width), BF16)
    keep, send = pl.pallas_call(
        functools.partial(third_kernel, sizes.space),
        in_specs=[SMEM] + [VMEM] * 8,
        out_specs=(VMEM, VMEM),
        out_shape=(shares, shares),
        scratch_shapes=[pltpu.VMEM(array.shape, F32) for array in (qkv, proj, fc1, fc2)],
        compiler_params=pltpu.CompilerParams(vmem_limit_bytes=24 * MIB),
        cost_estimate=pl.CostEstimate(
            flops=2 * count * total, bytes_accessed=8 * MIB, transcendentals=0
        ),
        name="weight_grads",
    )(me, normed, grad_packed, attended, grad, normed2, grad_before, hidden, cotangent)
    return block_out, wire_grad, keep, send


def conv_weight_kernel(
    sizes, wire_ref, x_hbm, out_ref, taps_hbm, x_ref, taps_ref, cross_ref, diag_ref, sems, sem
):
    wire_rows = sizes.space * sizes.block
    taps = TAPS * TAPS * COLOURS

    def arrival(row):
        return pltpu.make_async_copy(x_hbm.at[:, row], x_ref.at[row], sems.at[row])

    for row in range(sizes.rows):
        arrival(row).start()

    order = match(rows_of(sizes.ext * sizes.plane), tile_wire_keys(sizes, cols_of(wire_rows)))
    tile = dot(order, wire_ref[...].reshape(wire_rows, sizes.cols)).astype(BF16)
    for tap in range(TAPS):
        if tap == 1:
            moved = tile
        else:
            shift = match(rows_of(sizes.cols), cols_of(sizes.cols) + (1 - tap))
            moved = dot(tile, shift).astype(BF16)
        for ext in range(sizes.ext):
            at = ext * sizes.group + tap * sizes.plane
            taps_ref[at : at + sizes.plane, :] = moved[ext * sizes.plane : (ext + 1) * sizes.plane]

    departure = pltpu.make_async_copy(taps_ref, taps_hbm, sem)
    departure.start()
    cross_ref[...] = jnp.zeros(cross_ref.shape, F32)

    def step(row, carry):
        arrival(row).wait()
        x = x_ref[row].reshape(sizes.depth, sizes.cols)
        window = taps_ref[pl.ds(pl.multiple_of(row * sizes.group, 16), sizes.window), :]
        cross_ref[...] += dot_nt(window, x)
        return carry

    lax.fori_loop(0, sizes.rows, step, 0)

    diag_ref[...] = jnp.zeros(diag_ref.shape, F32)
    channel, frame_in = split(cols_of(sizes.depth), sizes.frames)
    lag = frame_in - rows_of(sizes.frames) + 2
    for tap in range(taps):
        cross = cross_ref[tap * sizes.frames : (tap + 1) * sizes.frames, :]
        row, rest = divmod(tap, TAPS * COLOURS)
        real = (TAPS - 1 - row) * TAPS * COLOURS + rest
        for a in range(TAPS):
            at = a * taps + real
            diag_ref[at : at + 1, :] = jnp.sum(
                jnp.where(lag == a, cross, 0.0), axis=0, keepdims=True
            )
    spread = match(rows_of(out_ref.shape[1]), channel)
    left = diag_ref[...]
    total = jnp.zeros(out_ref.shape, F32)
    for _ in range(3):
        part = left.astype(BF16)
        left = left - part.astype(F32)
        total = total + dot_nt(part, spread)
    out_ref[...] = total
    departure.wait()


def conv_weight_grad(sizes, wire, x):
    taps = TAPS * TAPS * TAPS * COLOURS
    taps_pad = round_up(taps, 16)
    lanes = round_up(sizes.channels, 128)
    return pl.pallas_call(
        functools.partial(conv_weight_kernel, sizes),
        in_specs=[VMEM, HBM],
        out_specs=(VMEM, HBM),
        out_shape=(
            jax.ShapeDtypeStruct((taps_pad, lanes), F32),
            pltpu.HBM((sizes.ext * sizes.group, sizes.cols), BF16),
        ),
        scratch_shapes=[
            pltpu.VMEM((sizes.rows, sizes.channels, sizes.frames, sizes.cols), BF16),
            pltpu.VMEM((sizes.ext * sizes.group, sizes.cols), BF16),
            pltpu.VMEM((sizes.window, sizes.depth), F32),
            pltpu.VMEM((taps_pad, sizes.depth), F32),
            pltpu.SemaphoreType.DMA((sizes.rows,)),
            pltpu.SemaphoreType.DMA(()),
        ],
        compiler_params=pltpu.CompilerParams(vmem_limit_bytes=32 * MIB),
        cost_estimate=pl.CostEstimate(
            flops=2 * sizes.rows * sizes.window * sizes.depth * sizes.cols,
            bytes_accessed=2 * x.size,
            transcendentals=0,
        ),
        name="conv_weight_grad",
    )(wire, x)


def feature_kernel(
    sizes, band_hbm, taps_hbm, out_hbm, held_ref, band_ref, taps_ref, sems, fetch_sems
):
    arrivals = fetch(((band_hbm, band_ref), (taps_hbm, taps_ref)), fetch_sems)

    def departure(row):
        return pltpu.make_async_copy(held_ref.at[row], out_hbm.at[:, row], sems.at[row])

    def step(row, carry):
        window = taps_ref[pl.ds(pl.multiple_of(row * sizes.group, 16), sizes.window), :]
        held_ref[row] = dot(band_ref[...], window).astype(BF16).reshape(held_ref.shape[1:])
        departure(row).start()
        return carry

    for arrival in arrivals:
        arrival.wait()

    lax.fori_loop(0, sizes.rows, step, 0)

    def close(row, carry):
        departure(row).wait()
        return carry

    lax.fori_loop(0, sizes.rows, close, 0)


def feature_gradient(sizes, band, taps):
    shape = (sizes.channels, sizes.rows, sizes.frames, sizes.cols)
    return pl.pallas_call(
        functools.partial(feature_kernel, sizes),
        in_specs=[HBM, HBM],
        out_specs=HBM,
        out_shape=pltpu.HBM(shape, BF16),
        scratch_shapes=[
            pltpu.VMEM((sizes.rows, sizes.channels, sizes.frames, sizes.cols), BF16),
            pltpu.VMEM(band.shape, BF16),
            pltpu.VMEM(taps.shape, BF16),
            pltpu.SemaphoreType.DMA((sizes.rows,)),
            pltpu.SemaphoreType.DMA((2,)),
        ],
        compiler_params=pltpu.CompilerParams(vmem_limit_bytes=32 * MIB),
        cost_estimate=pl.CostEstimate(
            flops=2 * sizes.rows * sizes.window * sizes.depth * sizes.cols,
            bytes_accessed=2 * math.prod(shape),
            transcendentals=0,
        ),
        name="feature_grad",
    )(band, taps)


def scatter(values, axis):
    return lax.all_to_all(values, axis, split_axis=0, concat_axis=0, tiled=True)


def exchange(values, axis, relative):
    return lax.ppermute(values, axis, [(i, i ^ relative) for i in range(lax.axis_size(axis))])


def small_call(kernel, inputs, specs, outputs, name):
    return pl.pallas_call(
        kernel,
        in_specs=specs,
        out_specs=jax.tree.map(lambda _: VMEM, outputs),
        out_shape=outputs,
        compiler_params=pltpu.CompilerParams(vmem_limit_bytes=8 * MIB),
        name=name,
    )(*inputs)


def add_pair_kernel(keep_ref, got_ref, *out_refs):
    for place, out_ref in enumerate(out_refs):
        total = keep_ref[place].astype(F32) + got_ref[place].astype(F32)
        out_ref[...] = total.astype(BF16)


def add_pair(keep, got):
    outs = (jax.ShapeDtypeStruct(keep.shape[1:], BF16),) * keep.shape[0]
    return small_call(add_pair_kernel, (keep, got), [VMEM, VMEM], outs, "add_pair")


def add_cut_kernel(copies, me_ref, *refs):
    terms, outs = refs[:-copies], refs[-copies:]
    rows = outs[0].shape[0]
    for relative, out_ref in enumerate(outs):
        at = pl.ds(pl.multiple_of((me_ref[0] ^ relative) * rows, 16), rows)
        total = terms[0][at, :].astype(F32)
        for term in terms[1:]:
            total = total + term[at, :].astype(F32)
        out_ref[...] = total.astype(BF16)


def add_cut(me, copies, terms):
    rows, width = terms[0].shape
    outs = (jax.ShapeDtypeStruct((rows // copies, width), BF16),) * copies
    return small_call(
        functools.partial(add_cut_kernel, copies),
        (me,) + tuple(terms),
        [SMEM] + [VMEM] * len(terms),
        outs,
        "add_cut",
    )


def join_kernel(conv_ref, *refs):
    terms, out_ref = refs[:-1], refs[-1]
    rows = terms[0].shape[0]
    total = terms[0][...].astype(F32)
    for term in terms[1:]:
        total = total + term[...].astype(F32)
    out_ref[:rows, :] = total.astype(BF16)
    conv = conv_ref[0].astype(F32)
    for place in range(1, conv_ref.shape[0]):
        conv = conv + conv_ref[place].astype(F32)
    strips = out_ref.shape[1] // conv.shape[1]
    tall = conv.shape[0] // strips
    conv = [conv[strip * tall : (strip + 1) * tall] for strip in range(strips)]
    out_ref[rows:, :] = jnp.concatenate(conv, axis=1).astype(BF16)


def join(terms, conv_all):
    rows, width = terms[0].shape
    more = conv_all.shape[1] * conv_all.shape[2] // width
    out = jax.ShapeDtypeStruct((rows + more, width), BF16)
    return small_call(
        join_kernel, (conv_all,) + tuple(terms), [VMEM] * (1 + len(terms)), out, "join"
    )


def finish_kernel(copies, lanes, me_ref, *refs):
    pieces = refs[:copies]
    qkv_ref, proj_ref, fc1_ref, fc2_ref, conv_ref, whole = refs[copies:]
    width = proj_ref.shape[1]
    rows = whole.shape[0] // copies
    total = None
    for relative, piece in enumerate(pieces):
        at = pl.ds(pl.multiple_of((me_ref[0] ^ relative) * rows, 16), rows)
        whole[at, :] = piece[:rows, :].astype(F32)
        conv = piece[rows:, :].astype(F32)
        total = conv if total is None else total + conv
    share = proj_ref.shape[0]
    at = 0
    for part in range(0, fc1_ref.shape[1], width):
        fc1_ref[:, part : part + width] = whole[at : at + share, :]
        at += share
    fc2_ref[...] = whole[at : at + fc2_ref.shape[0], :]
    at += fc2_ref.shape[0]
    for part in range(0, qkv_ref.shape[1], width):
        qkv_ref[:, part : part + width] = whole[at : at + share, :]
        at += share
    proj_ref[...] = whole[at : at + share, :]
    total = jnp.concatenate(
        [total[:, strip : strip + lanes] for strip in range(0, width, lanes)], axis=0
    )
    time_taps, row_taps, col_taps, colours, channels = conv_ref.shape
    for a in range(time_taps):
        for b in range(row_taps):
            for e in range(col_taps):
                at = ((a * row_taps + b) * col_taps + e) * colours
                conv_ref[a, b, e] = total[at : at + colours, :channels]


def finish(me, pieces, rows, lanes, shapes):
    copies, width = len(pieces), pieces[0].shape[1]
    return pl.pallas_call(
        functools.partial(finish_kernel, copies, lanes),
        in_specs=[SMEM] + [VMEM] * copies,
        out_specs=(VMEM,) * 5,
        out_shape=tuple(jax.ShapeDtypeStruct(shape, F32) for shape in shapes),
        scratch_shapes=[pltpu.VMEM((copies * rows, width), F32)],
        compiler_params=pltpu.CompilerParams(vmem_limit_bytes=12 * MIB),
        name="finish",
    )(me, *pieces)


def shards(
    features,
    conv_weight,
    out_grad,
    pos_embed,
    patch_weight,
    norm1,
    qkv_weight,
    proj_weight,
    norm2,
    fc1_weight,
    fc2_weight,
):
    space = lax.axis_size("space")
    copies = lax.axis_size("dp")
    sizes = Sizes(features, space)
    width = pos_embed.shape[1]
    hidden_width = fc1_weight.shape[1]
    me = lax.axis_index("space").astype(jnp.int32).reshape(1)
    me_dp = lax.axis_index("dp").astype(jnp.int32).reshape(1)
    x = in_hbm(features[0].transpose(0, 2, 1, 3))
    taps = conv_weight.reshape(-1, sizes.channels)

    wire = conv_forward(sizes, taps, x)
    wire = scatter(wire, "space")
    patch, band = prepare(sizes, taps, patch_weight)
    patch = in_hbm(patch)
    pos, qkv, proj, fc1, fc2, cotangent = (
        in_hbm(array)
        for array in (pos_embed, qkv_weight, proj_weight, fc1_weight, fc2_weight, out_grad[0])
    )
    params = (pos, patch, norm1, qkv, proj, norm2, fc1, fc2)
    block_out, wire_grad, keep, send = transformer(sizes, copies, me, wire, cotangent, params)

    wire_grad = scatter(wire_grad, "space")
    conv_part, tap_rows = conv_weight_grad(sizes, wire_grad, x)
    feature_grad = feature_gradient(sizes, in_hbm(band), in_hbm(tap_rows))

    conv_all = scatter(
        jnp.broadcast_to(conv_part.astype(BF16)[None], (space,) + conv_part.shape), "space"
    )

    chips = add_pair(keep, exchange(send, "space", 1))
    terms = [exchange(chips[r], "space", 2 * r) for r in range(1, len(chips))]
    cuts = add_cut(me_dp, copies, [chips[0]] + terms)
    terms = [exchange(cuts[r], "dp", r) for r in range(1, copies)]
    conv_all, feature_grad = lax.optimization_barrier((conv_all, feature_grad))
    piece = join([cuts[0]] + terms, conv_all)
    pieces = [piece] + [exchange(piece, "dp", r) for r in range(1, copies)]
    share = width // space
    shapes = (
        (share, 3 * width),
        (share, width),
        (share, hidden_width),
        (hidden_width // space, width),
        conv_weight.shape,
    )
    qkv_grad, proj_grad, fc1_grad, fc2_grad, conv_grad = finish(
        me_dp, pieces, cuts[0].shape[0], conv_part.shape[1], shapes
    )

    return (
        block_out[None],
        feature_grad.transpose(0, 2, 1, 3)[None],
        conv_grad,
        qkv_grad,
        proj_grad,
        fc1_grad,
        fc2_grad,
    )


def solution(mesh):
    placed = (
        P("dp", None, None, "space", None),
        P(),
        P("dp", "space", None, None),
        P(),
        P(),
        P(),
        P(),
        P(),
        P(),
        P(),
        P(),
    )
    return jax.shard_map(
        shards,
        mesh=mesh,
        in_specs=placed,
        out_specs=(
            P("dp", "space", None, None),
            P("dp", None, None, "space", None),
            P(),
            P("space", None),
            P("space", None),
            P("space", None),
            P("space", None),
        ),
        check_vma=False,
    )
```

time: 137 us -> 111 us (0.81)
  waiting for transfers between devices: 33.4 us -> 21.6 us
  local copies, waits for them, and re-layouts: 13.3 us -> 2.3 us
  other arithmetic: 5.55 us -> 0.01 us
  Pallas kernels: 56.9 us -> 60.7 us
    ppermute x12 -> x10, waiting for transfers between devices: 23.3 us -> 12.8 us  [exchange(): lax.ppermute(values, axis, [(i, i ^ relative) for i in range(lax.axis_siz...]
    unnamed x35 -> x10, local copies, waits for them, and re-layouts: 7.01 us -> 0.82 us
    slice x4 -> x0, local copies, waits for them, and re-layouts: 3.95 us -> none  [the longest x1 2.36 us: shards(): second = reduce_blocks(grads[:, half:], bits[:1] + bits[2:] + bits[1:2])]
    pallas_call x5 -> x11, Pallas kernels: 56.9 us -> 60.7 us  [the longest x1 11.3 us: transformer(): pl.pallas_call(functools.partial(first_kernel, sizes), in_specs=[VMEM] *...]
    convert_element_type x7 -> x0, other arithmetic: 3.19 us -> none  [the longest x6 3.12 us: add(): return (left.astype(F32) + right.astype(F32)).astype(BF16)]
    concatenate x2 -> x0, other arithmetic: 1.43 us -> none  [the longest x1 0.73 us: shards(): jnp.concatenate([total[i * share:(i + 1) * share] for i in range(parts)],...]
    ppermute x12 -> x10, starting transfers between devices: 13.6 us -> 12.4 us  [exchange(): lax.ppermute(values, axis, [(i, i ^ relative) for i in range(lax.axis_siz...]
  transfers between devices with their start and end apart: 15 -> 13, of which waited for: 12 -> 5; matrix products, arithmetic and copies ran while one was open for 4% -> 1% of each run, Pallas kernels for 19% -> 25%
where the time goes in v1:
time: 111 us
  Pallas kernels  60.7 us (55%)
  starting transfers between devices  25.3 us (23%)
  waiting for transfers between devices  21.6 us (19%)
  local copies, waits for them, and re-layouts  2.3 us (2%)
    all_to_all x3, starting transfers between devices, scatter(): return lax.all_to_all(values, axis, split_axis=0, concat_axis=0, tiled=True)  12.9 us
    ppermute x10, waiting for transfers between devices, exchange(): lax.ppermute(values, axis, [(i, i ^ relative) for i in range(lax.axis_siz...  12.8 us
    ppermute x10, starting transfers between devices, exchange(): lax.ppermute(values, axis, [(i, i ^ relative) for i in range(lax.axis_siz...  12.4 us
    pallas_call x1, Pallas kernels, transformer(): pl.pallas_call(functools.partial(first_kernel, sizes), in_specs=[VMEM] *...  11.3 us
    pallas_call x1, Pallas kernels, conv_weight_grad(): pl.pallas_call(functools.partial(conv_weight_kernel, sizes), in_specs=[VM...  10.7 us
    pallas_call x1, Pallas kernels, feature_gradient(): pl.pallas_call(functools.partial(feature_kernel, sizes), in_specs=[HBM, H...  9.87 us
    pallas_call x1, Pallas kernels, conv_forward(): pl.pallas_call(functools.partial(conv_forward_kernel, sizes), in_specs=[V...  9.17 us
    all_to_all x3, waiting for transfers between devices, scatter(): return lax.all_to_all(values, axis, split_axis=0, concat_axis=0, tiled=True)  8.79 us
  transfers between devices with their start and end apart: 13, of which 5 were waited for; matrix products, arithmetic and copies ran while one was open for 1% of the time, Pallas kernels for 25%

profile of v1, /device:TPU:0, one launch (start us, length us, event | category | flops | bytes accessed | tf_op | source)
XLA Modules:
  0.0 110.8 jit_solution(9611747782764732820)
XLA Ops:
  0.6 0.8 reshape.24.weight_ref
  1.4 0.0 copy-start.3
  1.4 0.0 copy-start.4
  1.4 0.0 copy-start.2
  1.4 9.2 %conv_forward.1 = bf16[8,64,448]{2,1,0:T(8,128)(2,1)} custom-call(bf16[81,96]{1,0:T(8,128)(2,1)S(1)} %reshape.24.weight_ref, bf16[96,7,16,448]{3,2,1,0:T(8,128)(2,1)} %bitcast.10), custom_call_target="tpu_custom_call" | custom-call | flops 4161798144 | bytes 9633792 | tf_op jit(solution)/shard_map/conv_forward/pallas_call | solution.py:172
  10.6 5.2 %all-to-all-start = ((bf16[8,64,448]{2,1,0:T(8,128)(2,1)}), bf16[8,64,448]{2,1,0:T(8,128)(2,1)S(1)}, u32[]{:S(2)}, u32[]{:S(2)}) async-start(bf16[8,64,448]{2,1,0:T(8,128)(2,1)} %conv_forward.1), calls=%async_computation | async-start | bytes 1048576 | tf_op jit(solution)/shard_map/all_to_all | solution.py:763
  15.8 0.0 copy-done.3
  15.8 0.0 copy-done.4
  15.8 0.0 copy-done.2
  15.8 5.4 %prepare.1 = (bf16[896,384]{1,0:T(8,128)(2,1)}, bf16[1536,432]{1,0:T(8,128)(2,1)}) custom-call(bf16[81,96]{1,0:T(8,128)(2,1)S(1)} %reshape.24.weight_ref, bf16[588,384]{1,0:T(8,128)(2,1)S(1)} %copy-done.2), custom_call_target="tpu_custom_call" | custom-call | flops 4000000000 | bytes 4194304 | tf_op jit(solution)/shard_map/prepare/pallas_call | solution.py:224
  21.3 4.3 %all-to-all-done.wire_ref = bf16[8,64,448]{2,1,0:T(8,128)(2,1)S(1)} async-done(((bf16[8,64,448]{2,1,0:T(8,128)(2,1)}), bf16[8,64,448]{2,1,0:T(8,128)(2,1)S(1)}, u32[]{:S(2)}, u32[]{:S(2)}) %all-to-all-start) | async-done | bytes 458784 | tf_op jit(solution)/shard_map/all_to_all | solution.py:763
  25.5 11.3 %block_forward.1 = (bf16[2,128,384]{2,1,0:T(8,128)(2,1)}, bf16[256,384]{1,0:T(8,128)(2,1)S(1)}, bf16[256,1152]{1,0:T(8,128)(2,1)S(1)}, f32[12,128,128]{2,1,0:T(8...) custom-call(bf16[8,64,448]{2,1,0:T(8,128)(2,1)S(1)} %all-to-all-done, ...), custom_call_target="tpu_custom_call" | custom-call | flops 2164260864 | bytes 12582912 | tf_op jit(solution)/shard_map/block_forward/pallas_call | solution.py:548
  36.9 8.1 %block_backward.1 = (bf16[8,64,448]{2,1,0:T(8,128)(2,1)}, bf16[256,1152]{1,0:T(8,128)(2,1)S(1)}) custom-call(bf16[256,1152]{1,0:T(8,128)(2,1)S(1)} %get-tuple-element.43.packed_ref, f32[12,128,128]{2,1,0:T(8,128)S(1)} %get-tuple-element.44.probs_ref, f32[256,384]{1,0:T(8,128)S(1)} %get-tuple-element.45.grad_ref, f32[256,384]{1,0:T(8,128)S(1)} %get-tuple-element.46.unit_ref, ...), custom_call_target="tpu_custom_call" | custom-call | flops 956301312 | bytes 6291456 | tf_op jit(solution)/shard_map/block_backward/pallas_call | solution.py:579
  45.0 3.6 %weight_grads.1 = (bf16[4,576,384]{2,1,0:T(8,128)(2,1)S(1)}, bf16[4,576,384]{2,1,0:T(8,128)(2,1)}) custom-call(s32[1]{0:T(128)} %bitcast.8.me_ref, bf16[256,384]{1,0:T(8,128)(2,1)S(1)} %get-tuple-element.54.normed_ref, bf16[256,1152]{1,0:T(8,128)(2,1)S(1)} %get-tuple-element.55.grad_packed_ref, bf16[256,384]{1,0:T(8,128)(2,1)S(1)} %get-tuple-element.56.attended_ref, ...), custom_call_target="tpu_custom_call" | custom-call | flops 905969664 | bytes 8388608 | tf_op jit(solution)/shard_map/weight_grads/pallas_call | solution.py:607
  48.6 0.0 collective-permute-start
  48.6 4.4 %all-to-all-start.1 = ((bf16[8,64,448]{2,1,0:T(8,128)(2,1)}), bf16[8,64,448]{2,1,0:T(8,128)(2,1)}, u32[]{:S(2)}, u32[]{:S(2)}) async-start(bf16[8,64,448]{2,1,0:T(8,128)(2,1)} %get-tuple-element.48), calls=%async_computation.1 | async-start | bytes 1048576 | tf_op jit(solution)/shard_map/all_to_all | solution.py:763
  53.0 0.0 collective-permute-done.got_ref
  53.0 1.2 %add_pair.1 = (bf16[576,384]{1,0:T(8,128)(2,1)S(1)}, bf16[576,384]{1,0:T(8,128)(2,1)}, bf16[576,384]{1,0:T(8,128)(2,1)}, bf16[576,384]{1,0:T(8,128)(2,1)}) custom-call(bf16[4,576,384]{2,1,0:T(8,128)(2,1)S(1)} %get-tuple-element.60.keep_ref, bf16[4,576,384]{2,1,0:T(8,128)(2,1)S(1)} %collective-permute-done.got_ref), custom_call_target="tpu_custom_call" | custom-call | tf_op jit(solution)/shard_map/add_pair/pallas_call | solution.py:771
  54.2 0.0 copy-start
  54.2 0.8 copy-done
  55.0 1.7 %collective-permute-start.1 = (bf16[576,384]{1,0:T(8,128)(2,1)}, bf16[576,384]{1,0:T(8,128)(2,1)S(1)}, u32[]{:S(2)}, u32[]{:S(2)}) collective-permute-start(bf16[576,384]{1,0:T(8,128)(2,1)} %get-tuple-element.63), channel_id=1, source_target_pairs={{0,2},{1,3},{2,0},{3,1},{4,6},{5,7},{6,4},{7,5},{8,10},{9,11},{10,... | collective-permute-start | bytes 1327112 | tf_op jit(solution)/shard_map/ppermute | solution.py:767
  56.6 1.5 %collective-permute-start.2 = (bf16[576,384]{1,0:T(8,128)(2,1)}, bf16[576,384]{1,0:T(8,128)(2,1)S(1)}, u32[]{:S(2)}, u32[]{:S(2)}) collective-permute-start(bf16[576,384]{1,0:T(8,128)(2,1)} %get-tuple-element.64), channel_id=1, source_target_pairs={{0,4},{1,5},{2,6},{3,7},{4,0},{5,1},{6,2},{7,3},{8,12},{9,13},{10,... | collective-permute-start | bytes 1327112 | tf_op jit(solution)/shard_map/ppermute | solution.py:767
  58.1 0.3 collective-permute-start.3
  58.4 0.0 copy-start.1
  58.4 4.5 %all-to-all-done.1.wire_ref = bf16[8,64,448]{2,1,0:T(8,128)(2,1)} async-done(((bf16[8,64,448]{2,1,0:T(8,128)(2,1)}), bf16[8,64,448]{2,1,0:T(8,128)(2,1)}, u32[]{:S(2)}, u32[]{:S(2)}) %all-to-all-start.1) | async-done | bytes 458784 | tf_op jit(solution)/shard_map/all_to_all | solution.py:763
  63.0 10.7 %conv_weight_grad.1 = (f32[96,128]{1,0:T(8,128)S(1)}, bf16[1296,448]{1,0:T(8,128)(2,1)}) custom-call(bf16[8,64,448]{2,1,0:T(8,128)(2,1)} %all-to-all-done.1.wire_ref, bf16[96,7,16,448]{3,2,1,0:T(8,128)(2,1)} %bitcast.11), custom_call_target="tpu_custom_call" | custom-call | flops 4161798144 | bytes 9633792 | tf_op jit(solution)/shard_map/conv_weight_grad/pallas_call | solution.py:686
  73.7 0.7 broadcast_in_dim.21
  74.4 3.4 %all-to-all-start.2 = ((bf16[8,96,128]{2,1,0:T(8,128)(2,1)}), bf16[8,96,128]{2,1,0:T(8,128)(2,1)S(1)}, u32[]{:S(2)}, u32[]{:S(2)}) async-start(bf16[8,96,128]{2,1,0:T(8,128)(2,1)} %broadcast_in_dim.21), calls=%async_computation.2 | async-start | bytes 393216 | tf_op jit(solution)/shard_map/all_to_all | solution.py:763
  77.8 0.0 collective-permute-done.1.refs_1_
  77.8 0.0 collective-permute-done.2.refs_2_
  77.8 3.6 %collective-permute-done.3.refs_3_ = bf16[576,384]{1,0:T(8,128)(2,1)S(1)} collective-permute-done((bf16[576,384]{1,0:T(8,128)(2,1)}, bf16[576,384]{1,0:T(8,128)(2,1)S(1)}, u32[]{:S(2)}, u32[]{:S(2)}) %collective-permute-start.3) | collective-permute-done | bytes 442400 | tf_op jit(solution)/shard_map/ppermute | solution.py:767
  81.4 0.0 copy-done.1
  81.4 0.2 add_cut.1
  81.6 1.6 %collective-permute-start.4 = (bf16[144,384]{1,0:T(8,128)(2,1)S(1)}, bf16[144,384]{1,0:T(8,128)(2,1)S(1)}, u32[]{:S(2)}, u32[]{:S(2)}) collective-permute-start(bf16[144,384]{1,0:T(8,128)(2,1)S(1)} %get-tuple-element.67), channel_id=1, source_target_pairs={{0,8},{8,0},{16,24},{24,16},{1,9},{9,1},{17,25},{25,17},{2,10},{10... | collective-permute-start | bytes 331784 | tf_op jit(solution)/shard_map/ppermute | solution.py:767
  83.3 2.6 %collective-permute-start.5 = (bf16[144,384]{1,0:T(8,128)(2,1)S(1)}, bf16[144,384]{1,0:T(8,128)(2,1)S(1)}, u32[]{:S(2)}, u32[]{:S(2)}) collective-permute-start(bf16[144,384]{1,0:T(8,128)(2,1)S(1)} %get-tuple-element.68), channel_id=1, source_target_pairs={{0,16},{8,24},{16,0},{24,8},{1,17},{9,25},{17,1},{25,9},{2,18},{10... | collective-permute-start | bytes 331784 | tf_op jit(solution)/shard_map/ppermute | solution.py:767
  85.9 0.2 collective-permute-start.6
  86.1 9.9 %feature_grad.1 = bf16[96,7,16,448]{3,2,1,0:T(8,128)(2,1)} custom-call(bf16[1536,432]{1,0:T(8,128)(2,1)} %get-tuple-element.50.band_hbm, bf16[1296,448]{1,0:T(8,128)(2,1)} %get-tuple-element.51.taps_hbm), custom_call_target="tpu_custom_call" | custom-call | flops 4161798144 | bytes 9633792 | tf_op jit(solution)/shard_map/feature_grad/pallas_call | solution.py:740
  96.0 0.0 all-to-all-done.2.conv_ref
  96.0 0.0 collective-permute-done.4.refs_1_
  96.0 0.0 collective-permute-done.5.refs_2_
  96.0 0.0 collective-permute-done.6.refs_3_
  96.0 0.1 join.1.refs_0_
  96.1 0.7 collective-permute-start.7
  96.9 3.5 %collective-permute-start.8 = (bf16[176,384]{1,0:T(8,128)(2,1)S(1)}, bf16[176,384]{1,0:T(8,128)(2,1)S(1)}, u32[]{:S(2)}, u32[]{:S(2)}) collective-permute-start(bf16[176,384]{1,0:T(8,128)(2,1)S(1)} %join.1.refs_0_), channel_id=1, source_target_pairs={{0,16},{8,24},{16,0},{24,8},{1,17},{9,25},{17,1},{25,9},{2,18},{10... | collective-permute-start | bytes 405512 | tf_op jit(solution)/shard_map/ppermute | solution.py:767
  100.4 0.2 collective-permute-start.9
  100.6 2.2 %collective-permute-done.7.refs_1_ = bf16[176,384]{1,0:T(8,128)(2,1)S(1)} collective-permute-done((bf16[176,384]{1,0:T(8,128)(2,1)S(1)}, bf16[176,384]{1,0:T(8,128)(2,1)S(1)}, u32[]{:S(2)}, u32[]{:S(2)}) %collective-permute-start.7) | collective-permute-done | bytes 135200 | tf_op jit(solution)/shard_map/ppermute | solution.py:767
  102.8 7.1 %collective-permute-done.8.refs_2_ = bf16[176,384]{1,0:T(8,128)(2,1)S(1)} collective-permute-done((bf16[176,384]{1,0:T(8,128)(2,1)S(1)}, bf16[176,384]{1,0:T(8,128)(2,1)S(1)}, u32[]{:S(2)}, u32[]{:S(2)}) %collective-permute-start.8) | collective-permute-done | bytes 135200 | tf_op jit(solution)/shard_map/ppermute | solution.py:767
  109.8 0.0 collective-permute-done.9.refs_3_
  109.8 1.0 finish.1
  (3 shorter events, 0.0 us)
Async XLA Ops:
  1.4 14.4 %copy-start.3 = (f32[384]{0:T(512)S(1)}, f32[384]{0:T(512)}, u32[]{:S(2)}) copy-start(f32[384]{0:T(512)} %param.16) | copy-start | bytes 4612
  1.4 14.4 %copy-start.4 = (f32[384]{0:T(512)S(1)}, f32[384]{0:T(512)}, u32[]{:S(2)}) copy-start(f32[384]{0:T(512)} %param.19) | copy-start | bytes 4612
  1.4 14.4 %copy-start.2 = (bf16[588,384]{1,0:T(8,128)(2,1)S(1)}, bf16[588,384]{1,0:T(8,128)(2,1)}, u32[]{:S(2)}) copy-start(bf16[588,384]{1,0:T(8,128)(2,1)} %patch_ref.1) | copy-start | bytes 1354756
  10.6 14.9 %all-to-all-start = ((bf16[8,64,448]{2,1,0:T(8,128)(2,1)}), bf16[8,64,448]{2,1,0:T(8,128)(2,1)S(1)}, u32[]{:S(2)}, u32[]{:S(2)}) async-start(bf16[8,64,448]{2,1,0:T(8,128)(2,1)} %conv_forward.1), calls=%async_computation | async-start | bytes 1048576 | tf_op jit(solution)/shard_map/all_to_all | solution.py:763
  48.6 4.4 %collective-permute-start = (bf16[4,576,384]{2,1,0:T(8,128)(2,1)}, bf16[4,576,384]{2,1,0:T(8,128)(2,1)S(1)}, u32[]{:S(2)}, u32[]{:S(2)}) collective-permute-start(bf16[4,576,384]{2,1,0:T(8,128)(2,1)} %get-tuple-element.61), channel_id=1, source_target_pairs={{0,1},{1,0},{2,3},{3,2},{4,5},{5,4},{6,7},{7,6},{8,9},{9,8},{10,11... | collective-permute-start | bytes 5308424 | tf_op jit(solution)/shard_map/ppermute | solution.py:767
  48.6 14.4 %all-to-all-start.1 = ((bf16[8,64,448]{2,1,0:T(8,128)(2,1)}), bf16[8,64,448]{2,1,0:T(8,128)(2,1)}, u32[]{:S(2)}, u32[]{:S(2)}) async-start(bf16[8,64,448]{2,1,0:T(8,128)(2,1)} %get-tuple-element.48), calls=%async_computation.1 | async-start | bytes 1048576 | tf_op jit(solution)/shard_map/all_to_all | solution.py:763
  54.2 0.8 copy-start
  55.0 22.8 %collective-permute-start.1 = (bf16[576,384]{1,0:T(8,128)(2,1)}, bf16[576,384]{1,0:T(8,128)(2,1)S(1)}, u32[]{:S(2)}, u32[]{:S(2)}) collective-permute-start(bf16[576,384]{1,0:T(8,128)(2,1)} %get-tuple-element.63), channel_id=1, source_target_pairs={{0,2},{1,3},{2,0},{3,1},{4,6},{5,7},{6,4},{7,5},{8,10},{9,11},{10,... | collective-permute-start | bytes 1327112 | tf_op jit(solution)/shard_map/ppermute | solution.py:767
  56.6 21.2 %collective-permute-start.2 = (bf16[576,384]{1,0:T(8,128)(2,1)}, bf16[576,384]{1,0:T(8,128)(2,1)S(1)}, u32[]{:S(2)}, u32[]{:S(2)}) collective-permute-start(bf16[576,384]{1,0:T(8,128)(2,1)} %get-tuple-element.64), channel_id=1, source_target_pairs={{0,4},{1,5},{2,6},{3,7},{4,0},{5,1},{6,2},{7,3},{8,12},{9,13},{10,... | collective-permute-start | bytes 1327112 | tf_op jit(solution)/shard_map/ppermute | solution.py:767
  58.1 23.3 %collective-permute-start.3 = (bf16[576,384]{1,0:T(8,128)(2,1)}, bf16[576,384]{1,0:T(8,128)(2,1)S(1)}, u32[]{:S(2)}, u32[]{:S(2)}) collective-permute-start(bf16[576,384]{1,0:T(8,128)(2,1)} %get-tuple-element.65), channel_id=1, source_target_pairs={{0,6},{1,7},{2,4},{3,5},{4,2},{5,3},{6,0},{7,1},{8,14},{9,15},{10,... | collective-permute-start | bytes 1327112 | tf_op jit(solution)/shard_map/ppermute | solution.py:767
  58.4 23.0 %copy-start.1 = (bf16[576,384]{1,0:T(8,128)(2,1)S(1)}, bf16[576,384]{1,0:T(8,128)(2,1)}, u32[]{:S(2)}) copy-start(bf16[576,384]{1,0:T(8,128)(2,1)} %copy-done) | copy-start | bytes 1327108
  74.4 21.6 %all-to-all-start.2 = ((bf16[8,96,128]{2,1,0:T(8,128)(2,1)}), bf16[8,96,128]{2,1,0:T(8,128)(2,1)S(1)}, u32[]{:S(2)}, u32[]{:S(2)}) async-start(bf16[8,96,128]{2,1,0:T(8,128)(2,1)} %broadcast_in_dim.21), calls=%async_computation.2 | async-start | bytes 393216 | tf_op jit(solution)/shard_map/all_to_all | solution.py:763
  81.6 14.3 %collective-permute-start.4 = (bf16[144,384]{1,0:T(8,128)(2,1)S(1)}, bf16[144,384]{1,0:T(8,128)(2,1)S(1)}, u32[]{:S(2)}, u32[]{:S(2)}) collective-permute-start(bf16[144,384]{1,0:T(8,128)(2,1)S(1)} %get-tuple-element.67), channel_id=1, source_target_pairs={{0,8},{8,0},{16,24},{24,16},{1,9},{9,1},{17,25},{25,17},{2,10},{10... | collective-permute-start | bytes 331784 | tf_op jit(solution)/shard_map/ppermute | solution.py:767
  83.3 12.7 %collective-permute-start.5 = (bf16[144,384]{1,0:T(8,128)(2,1)S(1)}, bf16[144,384]{1,0:T(8,128)(2,1)S(1)}, u32[]{:S(2)}, u32[]{:S(2)}) collective-permute-start(bf16[144,384]{1,0:T(8,128)(2,1)S(1)} %get-tuple-element.68), channel_id=1, source_target_pairs={{0,16},{8,24},{16,0},{24,8},{1,17},{9,25},{17,1},{25,9},{2,18},{10... | collective-permute-start | bytes 331784 | tf_op jit(solution)/shard_map/ppermute | solution.py:767
  85.9 10.1 %collective-permute-start.6 = (bf16[144,384]{1,0:T(8,128)(2,1)S(1)}, bf16[144,384]{1,0:T(8,128)(2,1)S(1)}, u32[]{:S(2)}, u32[]{:S(2)}) collective-permute-start(bf16[144,384]{1,0:T(8,128)(2,1)S(1)} %get-tuple-element.69), channel_id=1, source_target_pairs={{0,24},{8,16},{16,8},{24,0},{1,25},{9,17},{17,9},{25,1},{2,26},{10... | collective-permute-start | bytes 331784 | tf_op jit(solution)/shard_map/ppermute | solution.py:767
  96.1 6.6 %collective-permute-start.7 = (bf16[176,384]{1,0:T(8,128)(2,1)S(1)}, bf16[176,384]{1,0:T(8,128)(2,1)S(1)}, u32[]{:S(2)}, u32[]{:S(2)}) collective-permute-start(bf16[176,384]{1,0:T(8,128)(2,1)S(1)} %join.1.refs_0_), channel_id=1, source_target_pairs={{0,8},{8,0},{16,24},{24,16},{1,9},{9,1},{17,25},{25,17},{2,10},{10... | collective-permute-start | bytes 405512 | tf_op jit(solution)/shard_map/ppermute | solution.py:767
  96.9 13.0 %collective-permute-start.8 = (bf16[176,384]{1,0:T(8,128)(2,1)S(1)}, bf16[176,384]{1,0:T(8,128)(2,1)S(1)}, u32[]{:S(2)}, u32[]{:S(2)}) collective-permute-start(bf16[176,384]{1,0:T(8,128)(2,1)S(1)} %join.1.refs_0_), channel_id=1, source_target_pairs={{0,16},{8,24},{16,0},{24,8},{1,17},{9,25},{17,1},{25,9},{2,18},{10... | collective-permute-start | bytes 405512 | tf_op jit(solution)/shard_map/ppermute | solution.py:767
  100.4 9.5 %collective-permute-start.9 = (bf16[176,384]{1,0:T(8,128)(2,1)S(1)}, bf16[176,384]{1,0:T(8,128)(2,1)S(1)}, u32[]{:S(2)}, u32[]{:S(2)}) collective-permute-start(bf16[176,384]{1,0:T(8,128)(2,1)S(1)} %join.1.refs_0_), channel_id=1, source_target_pairs={{0,24},{8,16},{16,8},{24,0},{1,25},{9,17},{17,9},{25,1},{2,26},{10... | collective-permute-start | bytes 405512 | tf_op jit(solution)/shard_map/ppermute | solution.py:767

commit v2 on v1

--- a/solution.py
+++ b/solution.py
@@ -70,7 +70,7 @@
         self.patch_rows = self.height // PATCH
         self.patch_cols = self.cols // PATCH
         self.tokens = self.patch_rows * self.patch_cols
-        self.block = round_up(self.ext * COLOURS * self.per_dev, 16)
+        self.block = round_up(self.ext * COLOURS * self.per_dev, 8)
         self.q_used = COLOURS * PATCH
         self.q_pad = round_up(self.q_used, 64)
         self.plane = COLOURS * self.frames
@@ -117,7 +117,7 @@
 
 
 def conv_forward_kernel(
-    sizes, weight_ref, x_hbm, out_ref, x_ref, band_ref, acc_ref, plane_ref, sems
+    sizes, weight_ref, x_hbm, out_ref, weight_out_ref, x_ref, band_ref, acc_ref, plane_ref, rows_ref, sems
 ):
     taps = TAPS * TAPS * COLOURS
 
@@ -129,7 +129,10 @@
 
     channel, frame_in = split(cols_of(sizes.depth), sizes.frames)
     spread = match(rows_of(sizes.channels), channel)
-    wide = dot(weight_ref[...], spread)
+    for at in range(weight_ref.shape[0]):
+        rows_ref[at * COLOURS : (at + 1) * COLOURS, :] = weight_ref[at].astype(F32)
+    weight_out_ref[...] = rows_ref[...].astype(BF16)
+    wide = dot(weight_out_ref[...], spread)
     lag = frame_in - rows_of(sizes.frames) + 2
     here = [lag == a for a in range(TAPS)]
     for tap in range(taps):
@@ -165,20 +168,24 @@
     wire = tile_wire_keys(sizes, rows_of(sizes.space * sizes.block))
     order = match(wire, cols_of(sizes.ext * sizes.plane))
     moved = dot(order, plane_ref[...]).astype(BF16)
-    out_ref[...] = moved.reshape(sizes.space, sizes.block, sizes.cols)
+    out_ref[...] = moved
 
 
 def conv_forward(sizes, weight, x):
     return pl.pallas_call(
         functools.partial(conv_forward_kernel, sizes),
         in_specs=[VMEM, HBM],
-        out_specs=VMEM,
-        out_shape=jax.ShapeDtypeStruct((sizes.space, sizes.block, sizes.cols), BF16),
+        out_specs=(VMEM, VMEM),
+        out_shape=(
+            jax.ShapeDtypeStruct((sizes.space * sizes.block, sizes.cols), BF16),
+            jax.ShapeDtypeStruct((weight.shape[0] * weight.shape[1], sizes.channels), BF16),
+        ),
         scratch_shapes=[
             pltpu.VMEM((sizes.rows, sizes.channels, sizes.frames, sizes.cols), BF16),
             pltpu.VMEM((sizes.window, sizes.depth), BF16),
             pltpu.VMEM((sizes.ext * sizes.group, sizes.cols), F32),
             pltpu.VMEM((sizes.ext * sizes.plane, sizes.cols), BF16),
+            pltpu.VMEM((weight.shape[0] * weight.shape[1], sizes.channels), F32),
             pltpu.SemaphoreType.DMA((sizes.rows,)),
         ],
         compiler_params=pltpu.CompilerParams(vmem_limit_bytes=32 * MIB),
@@ -281,6 +288,7 @@
     normed_ref,
     packed_ref,
     probs_ref,
+    probs_b_ref,
     attended_ref,
     unit_ref,
     scale_ref,
@@ -288,13 +296,27 @@
     normed2_ref,
     hidden_ref,
     grad_before_ref,
+    patch_ref,
+    qkv_ref,
+    proj_ref,
     pixels_ref,
     patches_ref,
-    *held,
+    pos_ref,
+    cotangent_ref,
+    fc1_ref,
+    fc2_ref,
+    sems,
 ):
-    fixed = (patch_hbm, pos_hbm, cotangent_hbm, qkv_hbm, proj_hbm, fc1_hbm, fc2_hbm)
-    arrivals = fetch(tuple(zip(fixed, held[:-1])), held[-1])
-    patch_ref, pos_ref, cotangent_ref, qkv_ref, proj_ref, fc1_ref, fc2_ref = held[:-1]
+    pairs = (
+        (patch_hbm, patch_ref),
+        (pos_hbm, pos_ref),
+        (qkv_hbm, qkv_ref),
+        (proj_hbm, proj_ref),
+        (fc1_hbm, fc1_ref),
+        (cotangent_hbm, cotangent_ref),
+        (fc2_hbm, fc2_ref),
+    )
+    arrivals = fetch(pairs, sems)
     tokens, width = pos_ref.shape
     frames = sizes.per_dev
     count = frames * tokens
@@ -306,7 +328,7 @@
     pc = sizes.patch_cols
 
     order = match(patch_keys(sizes, rows_of(leads * q_pad)), wire_keys(sizes, cols_of(wire_rows)))
-    pixels_ref[...] = dot(order, wire_ref[...].reshape(wire_rows, sizes.cols)).astype(BF16)
+    pixels_ref[...] = dot(order, wire_ref[...]).astype(BF16)
     columns = column_order(sizes)
     for lead in range(leads):
         turned = dot_nt(columns, pixels_ref[lead * q_pad : (lead + 1) * q_pad, :])
@@ -315,7 +337,7 @@
                 inner * pc : (inner + 1) * pc, :
             ].astype(BF16)
 
-    for arrival in arrivals:
+    for arrival in arrivals[:2]:
         arrival.wait()
     pos = pos_ref[...].astype(F32)
     embedded = dot(patches_ref[...], patch_ref[...])
@@ -325,31 +347,41 @@
     scale_ref[...] = scale1
     normed = (unit1 * norm1_ref[...]).astype(BF16)
     normed_ref[...] = normed
+    arrivals[2].wait()
     packed_ref[...] = dot(normed, qkv_ref[...]).astype(BF16)
 
     lanes = min(128, width)
     per_group = lanes // head
     lane_head, _ = split(cols_of(lanes), head)
     inv = 1.0 / float(head) ** 0.5
-    for frame in range(frames):
-        at = slice(frame * tokens, (frame + 1) * tokens)
-        for group in range(width // lanes):
-            cut = slice(group * lanes, (group + 1) * lanes)
-            queries = packed_ref[at, cut]
-            keys_in = packed_ref[at, width + group * lanes : width + (group + 1) * lanes]
-            values_in = packed_ref[at, 2 * width + group * lanes : 2 * width + (group + 1) * lanes]
-            joined = None
-            for sub in range(per_group):
-                mine = lane_head == sub
-                masked = queries * jnp.where(mine, 1.0, 0.0).astype(BF16)
-                scores = dot_nt(masked, keys_in) * inv
-                scores = jnp.exp(scores - jnp.max(scores, axis=-1, keepdims=True))
-                probs = scores / jnp.sum(scores, axis=-1, keepdims=True)
-                probs_ref[(frame * HEADS) + group * per_group + sub] = probs
-                value = dot(probs.astype(BF16), values_in)
-                joined = value if joined is None else jnp.where(mine, value, joined)
-            attended_ref[at, cut] = joined.astype(BF16)
-
+    masks = [jnp.where(lane_head == sub, 1.0, 0.0).astype(BF16) for sub in range(per_group)]
+    places = [
+        (frame, group, slice(frame * tokens, (frame + 1) * tokens))
+        for frame in range(frames)
+        for group in range(width // lanes)
+    ]
+    for frame, group, at in places:
+        queries = packed_ref[at, group * lanes : (group + 1) * lanes]
+        keys_in = packed_ref[at, width + group * lanes : width + (group + 1) * lanes]
+        for sub in range(per_group):
+            probs_ref[frame * HEADS + group * per_group + sub] = dot_nt(
+                queries * masks[sub], keys_in
+            )
+    scores = probs_ref[...] * inv
+    scores = jnp.exp(scores - jnp.max(scores, axis=-1, keepdims=True))
+    probs = scores * (1.0 / jnp.sum(scores, axis=-1, keepdims=True))
+    probs_ref[...] = probs
+    probs_b_ref[...] = probs.astype(BF16)
+    for frame, group, at in places:
+        values_in = packed_ref[at, 2 * width + group * lanes : 2 * width + (group + 1) * lanes]
+        joined = None
+        for sub in range(per_group):
+            value = dot(probs_b_ref[frame * HEADS + group * per_group + sub], values_in)
+            joined = value if joined is None else jnp.where(lane_head == sub, value, joined)
+        attended_ref[at, group * lanes : (group + 1) * lanes] = joined.astype(BF16)
+
+    for arrival in arrivals[3:]:
+        arrival.wait()
     residual = embedded + dot(attended_ref[...], proj_ref[...])
     unit2, scale2 = normalise(residual)
     gain2 = norm2_ref[...]
@@ -383,28 +415,24 @@
     sizes,
     packed_ref,
     probs_ref,
+    probs_b_ref,
     grad_ref,
     unit_ref,
     scale_ref,
     norm1_ref,
-    patch_hbm,
-    qkv_hbm,
-    proj_hbm,
+    patch_ref,
+    qkv_ref,
+    proj_ref,
     wire_hbm,
     grad_packed_ref,
     grad_att_ref,
+    scores_ref,
+    scores_b_ref,
     pixels_ref,
     patches_ref,
     wire_out_ref,
-    patch_ref,
-    qkv_ref,
-    proj_ref,
-    sems,
-    wire_sem,
+    wire_sems,
 ):
-    pairs = ((proj_hbm, proj_ref), (qkv_hbm, qkv_ref), (patch_hbm, patch_ref))
-    arrivals = fetch(pairs, sems)
-    arrivals[0].wait()
     count, width = grad_ref.shape
     frames = sizes.per_dev
     tokens = count // frames
@@ -420,39 +448,44 @@
 
     grad_residual = grad_ref[...]
     grad_att_ref[...] = dot_nt(grad_residual.astype(BF16), proj_ref[...]).astype(BF16)
-    for frame in range(frames):
-        at = slice(frame * tokens, (frame + 1) * tokens)
-        for group in range(width // lanes):
-            cut = slice(group * lanes, (group + 1) * lanes)
-            cut_k = slice(width + group * lanes, width + (group + 1) * lanes)
-            cut_v = slice(2 * width + group * lanes, 2 * width + (group + 1) * lanes)
-            queries = packed_ref[at, cut]
-            keys_in = packed_ref[at, cut_k]
-            values_in = packed_ref[at, cut_v]
-            grad_att = grad_att_ref[at, cut]
-            grad_q = grad_k = grad_v = None
-            for sub in range(per_group):
-                mine = lane_head == sub
-                mask = jnp.where(mine, 1.0, 0.0).astype(BF16)
-                masked_q = queries * mask
-                masked_g = grad_att * mask
-                probs = probs_ref[(frame * HEADS) + group * per_group + sub]
-                probs_b = probs.astype(BF16)
-                grad_probs = dot_nt(masked_g, values_in).astype(BF16).astype(F32)
-                inner = jnp.sum(grad_probs * probs, axis=-1, keepdims=True)
-                grad_scores = (probs * (grad_probs - inner) * inv).astype(BF16)
-                one_q = dot(grad_scores, keys_in)
-                one_k = dot_tn(grad_scores, masked_q)
-                one_v = dot_tn(probs_b, masked_g)
-                grad_q = one_q if grad_q is None else jnp.where(mine, one_q, grad_q)
-                grad_k = one_k if grad_k is None else grad_k + one_k
-                grad_v = one_v if grad_v is None else grad_v + one_v
-            grad_packed_ref[at, cut] = grad_q.astype(BF16)
-            grad_packed_ref[at, cut_k] = grad_k.astype(BF16)
-            grad_packed_ref[at, cut_v] = grad_v.astype(BF16)
-
-    for arrival in arrivals[1:]:
-        arrival.wait()
+    masks = [jnp.where(lane_head == sub, 1.0, 0.0).astype(BF16) for sub in range(per_group)]
+    places = [
+        (frame, group, slice(frame * tokens, (frame + 1) * tokens))
+        for frame in range(frames)
+        for group in range(width // lanes)
+    ]
+    for frame, group, at in places:
+        grad_att = grad_att_ref[at, group * lanes : (group + 1) * lanes]
+        values_in = packed_ref[at, 2 * width + group * lanes : 2 * width + (group + 1) * lanes]
+        for sub in range(per_group):
+            scores_ref[frame * HEADS + group * per_group + sub] = dot_nt(
+                grad_att * masks[sub], values_in
+            )
+    grad_probs = scores_ref[...].astype(BF16).astype(F32)
+    weighted = grad_probs * probs_ref[...]
+    inner = jnp.sum(weighted, axis=-1, keepdims=True)
+    scores_b_ref[...] = ((weighted - probs_ref[...] * inner) * inv).astype(BF16)
+    for frame, group, at in places:
+        cut = slice(group * lanes, (group + 1) * lanes)
+        cut_k = slice(width + group * lanes, width + (group + 1) * lanes)
+        cut_v = slice(2 * width + group * lanes, 2 * width + (group + 1) * lanes)
+        queries = packed_ref[at, cut]
+        keys_in = packed_ref[at, cut_k]
+        grad_att = grad_att_ref[at, cut]
+        grad_q = grad_k = grad_v = None
+        for sub in range(per_group):
+            place = frame * HEADS + group * per_group + sub
+            grad_scores = scores_b_ref[place]
+            one_q = dot(grad_scores, keys_in)
+            one_k = dot_tn(grad_scores, queries * masks[sub])
+            one_v = dot_tn(probs_b_ref[place], grad_att * masks[sub])
+            grad_q = one_q if grad_q is None else jnp.where(lane_head == sub, one_q, grad_q)
+            grad_k = one_k if grad_k is None else grad_k + one_k
+            grad_v = one_v if grad_v is None else grad_v + one_v
+        grad_packed_ref[at, cut] = grad_q.astype(BF16)
+        grad_packed_ref[at, cut_k] = grad_k.astype(BF16)
+        grad_packed_ref[at, cut_v] = grad_v.astype(BF16)
+
     grad_normed = dot_nt(grad_packed_ref[...], qkv_ref[...]).astype(BF16).astype(F32) * norm1_ref[...]
     back = normalise_back(grad_normed, unit_ref[...], scale_ref[...])
     grad_embedded = (grad_residual + back).astype(BF16)
@@ -468,11 +501,18 @@
         )
         pixels_ref[lead * q_pad : (lead + 1) * q_pad, :] = dot_tn(turned, columns).astype(BF16)
     order = match(wire_keys(sizes, rows_of(wire_rows)), patch_keys(sizes, cols_of(leads * q_pad)))
-    moved = dot(order, pixels_ref[...]).astype(BF16)
-    wire_out_ref[...] = moved.reshape(sizes.space, sizes.block, sizes.cols)
-    leave = pltpu.make_async_copy(wire_out_ref, wire_hbm, wire_sem)
-    leave.start()
-    leave.wait()
+    parts = wire_sems.shape[0]
+    tall = wire_rows // parts
+    leaving = []
+    for part in range(parts):
+        at = slice(part * tall, (part + 1) * tall)
+        wire_out_ref[at, :] = dot(order[at], pixels_ref[...]).astype(BF16)
+        leaving.append(
+            pltpu.make_async_copy(wire_out_ref.at[at, :], wire_hbm.at[at, :], wire_sems.at[part])
+        )
+        leaving[-1].start()
+    for copy in leaving:
+        copy.wait()
 
 
 def third_kernel(
@@ -526,11 +566,6 @@
     patches_shape = (count, PATCH * sizes.q_pad)
     norm1, norm2 = norm1[None], norm2[None]
 
-    def held(*arrays):
-        return [pltpu.VMEM(array.shape, array.dtype) for array in arrays] + [
-            pltpu.SemaphoreType.DMA((len(arrays),))
-        ]
-
     tall = jax.ShapeDtypeStruct((count, width), BF16)
     wide = jax.ShapeDtypeStruct((count, hidden_width), BF16)
     (
@@ -538,6 +573,7 @@
         normed,
         packed,
         probs,
+        probs_b,
         attended,
         unit,
         scale,
@@ -545,15 +581,19 @@
         normed2,
         hidden,
         grad_before,
+        patch,
+        qkv,
+        proj,
     ) = pl.pallas_call(
         functools.partial(first_kernel, sizes),
         in_specs=[VMEM] * 3 + [HBM] * 7,
-        out_specs=(VMEM,) * 11,
+        out_specs=(VMEM,) * 15,
         out_shape=(
             jax.ShapeDtypeStruct(cotangent.shape, BF16),
             tall,
             jax.ShapeDtypeStruct((count, 3 * width), BF16),
             jax.ShapeDtypeStruct((sizes.per_dev * HEADS, tokens, tokens), F32),
+            jax.ShapeDtypeStruct((sizes.per_dev * HEADS, tokens, tokens), BF16),
             tall,
             jax.ShapeDtypeStruct((count, width), F32),
             jax.ShapeDtypeStruct((count, 1), F32),
@@ -561,12 +601,16 @@
             tall,
             wide,
             wide,
+            jax.ShapeDtypeStruct(patch.shape, BF16),
+            jax.ShapeDtypeStruct(qkv.shape, BF16),
+            jax.ShapeDtypeStruct(proj.shape, BF16),
         ),
         scratch_shapes=[
             pltpu.VMEM(pixel_shape, BF16),
             pltpu.VMEM(patches_shape, BF16),
         ]
-        + held(patch, pos, cotangent, qkv, proj, fc1, fc2),
+        + [pltpu.VMEM(array.shape, BF16) for array in (pos, cotangent, fc1, fc2)]
+        + [pltpu.SemaphoreType.DMA((7,))],
         compiler_params=pltpu.CompilerParams(vmem_limit_bytes=24 * MIB),
         cost_estimate=pl.CostEstimate(
             flops=4 * count * (patch.size + qkv.size + proj.size + fc1.size + fc2.size),
@@ -578,7 +622,7 @@
 
     wire_grad, grad_packed = pl.pallas_call(
         functools.partial(second_kernel, sizes),
-        in_specs=[VMEM] * 6 + [HBM] * 3,
+        in_specs=[VMEM] * 10,
         out_specs=(HBM, VMEM),
         out_shape=(
             pltpu.HBM(wire.shape, BF16),
@@ -586,12 +630,13 @@
         ),
         scratch_shapes=[
             pltpu.VMEM((count, width), BF16),
+            pltpu.VMEM(probs.shape, F32),
+            pltpu.VMEM(probs.shape, BF16),
             pltpu.VMEM(pixel_shape, BF16),
             pltpu.VMEM(patches_shape, BF16),
             pltpu.VMEM(wire.shape, BF16),
-        ]
-        + held(patch, qkv, proj)
-        + [pltpu.SemaphoreType.DMA(())],
+            pltpu.SemaphoreType.DMA((4,)),
+        ],
         compiler_params=pltpu.CompilerParams(vmem_limit_bytes=20 * MIB),
         cost_estimate=pl.CostEstimate(
             flops=4 * count * (patch.size + qkv.size + proj.size),
@@ -599,7 +644,7 @@
             transcendentals=0,
         ),
         name="block_backward",
-    )(packed, probs, grad, unit, scale, norm1, patch, qkv, proj)
+    )(packed, probs, probs_b, grad, unit, scale, norm1, patch, qkv, proj)
 
     total = qkv.size + proj.size + fc1.size + fc2.size
     rows = round_up(total // (width * sizes.space), 16 * copies)
@@ -632,7 +677,7 @@
         arrival(row).start()
 
     order = match(rows_of(sizes.ext * sizes.plane), tile_wire_keys(sizes, cols_of(wire_rows)))
-    tile = dot(order, wire_ref[...].reshape(wire_rows, sizes.cols)).astype(BF16)
+    tile = dot(order, wire_ref[...]).astype(BF16)
     for tap in range(TAPS):
         if tap == 1:
             moved = tile
@@ -778,15 +823,29 @@
     )(*inputs)
 
 
-def add_pair_kernel(keep_ref, got_ref, *out_refs):
-    for place, out_ref in enumerate(out_refs):
+def add_pair_kernel(keep_ref, got_ref, first_hbm, *refs):
+    out_refs, (first_ref, sem) = refs[:-2], refs[-2:]
+    leave = pltpu.make_async_copy(first_ref, first_hbm, sem)
+    for place, out_ref in enumerate((first_ref,) + tuple(out_refs)):
         total = keep_ref[place].astype(F32) + got_ref[place].astype(F32)
         out_ref[...] = total.astype(BF16)
+        if place == 0:
+            leave.start()
+    leave.wait()
 
 
 def add_pair(keep, got):
-    outs = (jax.ShapeDtypeStruct(keep.shape[1:], BF16),) * keep.shape[0]
-    return small_call(add_pair_kernel, (keep, got), [VMEM, VMEM], outs, "add_pair")
+    shape = keep.shape[1:]
+    outs = (pltpu.HBM(shape, BF16),) + (jax.ShapeDtypeStruct(shape, BF16),) * (keep.shape[0] - 1)
+    return pl.pallas_call(
+        add_pair_kernel,
+        in_specs=[VMEM, VMEM],
+        out_specs=(HBM,) + (VMEM,) * (keep.shape[0] - 1),
+        out_shape=outs,
+        scratch_shapes=[pltpu.VMEM(shape, BF16), pltpu.SemaphoreType.DMA(())],
+        compiler_params=pltpu.CompilerParams(vmem_limit_bytes=8 * MIB),
+        name="add_pair",
+    )(keep, got)
 
 
 def add_cut_kernel(copies, me_ref, *refs):
@@ -904,9 +963,7 @@
     me = lax.axis_index("space").astype(jnp.int32).reshape(1)
     me_dp = lax.axis_index("dp").astype(jnp.int32).reshape(1)
     x = in_hbm(features[0].transpose(0, 2, 1, 3))
-    taps = conv_weight.reshape(-1, sizes.channels)
-
-    wire = conv_forward(sizes, taps, x)
+    wire, taps = conv_forward(sizes, conv_weight.reshape(-1, COLOURS, sizes.channels), x)
     wire = scatter(wire, "space")
     patch, band = prepare(sizes, taps, patch_weight)
     patch = in_hbm(patch)

time: 111 us -> 102 us (0.919)
  Pallas kernels: 60.7 us -> 53.5 us
  waiting for transfers between devices: 21.6 us -> 20.1 us
    pallas_call x1, Pallas kernels: 11.3 us -> 6.97 us  [transformer(): pl.pallas_call(functools.partial(first_kernel, sizes), in_specs=[VMEM] *...]
    pallas_call x1, Pallas kernels: 8.09 us -> 4.41 us  [transformer(): pl.pallas_call(functools.partial(second_kernel, sizes), in_specs=[VMEM] *...]
    pallas_call x0 -> x1, Pallas kernels: none -> 1.96 us  [add_pair(): pl.pallas_call(add_pair_kernel, in_specs=[VMEM, VMEM], out_specs=(HBM,) +...]
    all_to_all x3, waiting for transfers between devices: 8.79 us -> 7.34 us  [scatter(): return lax.all_to_all(values, axis, split_axis=0, concat_axis=0, tiled=True)]
    pallas_call x3 -> x2, Pallas kernels: 1.51 us -> 0.32 us  [small_call(): pl.pallas_call(kernel, in_specs=specs, out_specs=jax.tree.map(lambda _: V...]
  transfers between devices with their start and end apart: 13 -> 13, of which waited for: 5 -> 5; matrix products, arithmetic and copies ran while one was open for 1% -> 1% of each run, Pallas kernels for 25% -> 28%
where the time goes in v2:
time: 102 us; the launch traced here: 101 us
  Pallas kernels  53.5 us (52%)
  starting transfers between devices  25.3 us (25%)
  waiting for transfers between devices  20.1 us (20%)
  local copies, waits for them, and re-layouts  1.46 us (1%)
    all_to_all x3, starting transfers between devices, scatter(): return lax.all_to_all(values, axis, split_axis=0, concat_axis=0, tiled=True)  12.9 us
    ppermute x10, waiting for transfers between devices, exchange(): lax.ppermute(values, axis, [(i, i ^ relative) for i in range(lax.axis_siz...  12.8 us
    ppermute x10, starting transfers between devices, exchange(): lax.ppermute(values, axis, [(i, i ^ relative) for i in range(lax.axis_siz...  12.5 us
    pallas_call x1, Pallas kernels, conv_weight_grad(): pl.pallas_call(functools.partial(conv_weight_kernel, sizes), in_specs=[VM...  10.7 us
    pallas_call x1, Pallas kernels, feature_gradient(): pl.pallas_call(functools.partial(feature_kernel, sizes), in_specs=[HBM, H...  9.87 us
    pallas_call x1, Pallas kernels, conv_forward(): pl.pallas_call(functools.partial(conv_forward_kernel, sizes), in_specs=[V...  9.16 us
    all_to_all x3, waiting for transfers between devices, scatter(): return lax.all_to_all(values, axis, split_axis=0, concat_axis=0, tiled=True)  7.34 us
    pallas_call x1, Pallas kernels, transformer(): pl.pallas_call(functools.partial(first_kernel, sizes), in_specs=[VMEM] *...  6.97 us
  transfers between devices with their start and end apart: 13, of which 5 were waited for; matrix products, arithmetic and copies ran while one was open for 1% of the time, Pallas kernels for 28%

profile of v2, /device:TPU:0, one launch (start us, length us, event | category | flops | bytes accessed | tf_op | source)
XLA Modules:
  0.0 101.3 jit_solution(17168947909285597954)
XLA Ops:
  0.6 0.0 copy-start.2
  0.6 0.7 copy-done.2
  1.4 0.0 copy-start.3
  1.4 0.0 copy-start.4
  1.4 0.0 copy-start.1
  1.4 9.2 %conv_forward.1 = (bf16[448,448]{1,0:T(8,128)(2,1)}, bf16[81,96]{1,0:T(8,128)(2,1)S(1)}) custom-call(bf16[27,3,96]{2,1,0:T(4,128)(2,1)S(1)} %bitcast.16, bf16[96,7,16,448]{3,2,1,0:T(8,128)(2,1)} %bitcast.18), custom_call_target="tpu_custom_call" | custom-call | flops 4161798144 | bytes 9633792 | tf_op jit(solution)/shard_map/conv_forward/pallas_call | solution.py:175
  10.6 5.2 %all-to-all-start = ((bf16[8,56,448]{2,1,0:T(8,128)(2,1)}), bf16[8,56,448]{2,1,0:T(8,128)(2,1)S(1)}, u32[]{:S(2)}, u32[]{:S(2)}) async-start(bf16[8,56,448]{2,1,0:T(8,128)(2,1)} %bitcast.3), calls=%async_computation | async-start | bytes 917504 | tf_op jit(solution)/shard_map/all_to_all | solution.py:808
  15.7 0.0 copy-done.3
  15.8 0.0 copy-done.4
  15.8 0.0 copy-done.1
  15.8 5.5 %prepare.1 = (bf16[896,384]{1,0:T(8,128)(2,1)}, bf16[1536,432]{1,0:T(8,128)(2,1)}) custom-call(bf16[81,96]{1,0:T(8,128)(2,1)S(1)} %get-tuple-element.48.weight_ref, bf16[588,384]{1,0:T(8,128)(2,1)S(1)} %copy-done.1), custom_call_target="tpu_custom_call" | custom-call | flops 4000000000 | bytes 4194304 | tf_op jit(solution)/shard_map/prepare/pallas_call | solution.py:231
  21.3 3.5 %all-to-all-done = bf16[8,56,448]{2,1,0:T(8,128)(2,1)S(1)} async-done(((bf16[8,56,448]{2,1,0:T(8,128)(2,1)}), bf16[8,56,448]{2,1,0:T(8,128)(2,1)S(1)}, u32[]{:S(2)}, u32[]{:S(2)}) %all-to-all-start) | async-done | bytes 401440 | tf_op jit(solution)/shard_map/all_to_all | solution.py:808
  24.8 7.0 %block_forward.1 = (bf16[2,128,384]{2,1,0:T(8,128)(2,1)}, bf16[256,384]{1,0:T(8,128)(2,1)S(1)}, bf16[256,1152]{1,0:T(8,128)(2,1)S(1)}, f32[12,128,128]{2,1,0:T(8...) custom-call(bf16[448,448]{1,0:T(8,128)(2,1)S(1)} %bitcast.15, ...), custom_call_target="tpu_custom_call" | custom-call | flops 2164260864 | bytes 12582912 | tf_op jit(solution)/shard_map/block_forward/pallas_call | solution.py:587
  31.8 4.4 %block_backward.1 = (bf16[448,448]{1,0:T(8,128)(2,1)}, bf16[256,1152]{1,0:T(8,128)(2,1)S(1)}) custom-call(bf16[256,1152]{1,0:T(8,128)(2,1)S(1)} %get-tuple-element.51.packed_ref, f32[12,128,128]{2,1,0:T(8,128)S(1)} %get-tuple-element.52.probs_ref, bf16[12,128,128]{2,1,0:T(8,128)(2,1)S(1)} %get-tuple-element.53.probs_b_ref, ...), custom_call_target="tpu_custom_call" | custom-call | flops 956301312 | bytes 6291456 | tf_op jit(solution)/shard_map/block_backward/pallas_call | solution.py:623
  36.2 3.6 %weight_grads.1 = (bf16[4,576,384]{2,1,0:T(8,128)(2,1)S(1)}, bf16[4,576,384]{2,1,0:T(8,128)(2,1)}) custom-call(s32[1]{0:T(128)} %bitcast.13.me_ref, bf16[256,384]{1,0:T(8,128)(2,1)S(1)} %get-tuple-element.66.normed_ref, bf16[256,1152]{1,0:T(8,128)(2,1)S(1)} %get-tuple-element.67.grad_packed_ref, bf16[256,384]{1,0:T(8,128)(2,1)S(1)} %get-tuple-element.68.attended_ref, ...), custom_call_target="tpu_custom_call" | custom-call | flops 905969664 | bytes 8388608 | tf_op jit(solution)/shard_map/weight_grads/pallas_call | solution.py:652
  39.8 0.0 collective-permute-start
  39.8 4.3 %all-to-all-start.1 = ((bf16[8,56,448]{2,1,0:T(8,128)(2,1)}), bf16[8,56,448]{2,1,0:T(8,128)(2,1)}, u32[]{:S(2)}, u32[]{:S(2)}) async-start(bf16[8,56,448]{2,1,0:T(8,128)(2,1)} %bitcast.17), calls=%async_computation.1 | async-start | bytes 917504 | tf_op jit(solution)/shard_map/all_to_all | solution.py:808
  44.1 0.0 collective-permute-done.got_ref
  44.1 2.0 %add_pair.1 = (bf16[576,384]{1,0:T(8,128)(2,1)}, bf16[576,384]{1,0:T(8,128)(2,1)}, bf16[576,384]{1,0:T(8,128)(2,1)}, bf16[576,384]{1,0:T(8,128)(2,1)}) custom-call(bf16[4,576,384]{2,1,0:T(8,128)(2,1)S(1)} %get-tuple-element.72.keep_ref, bf16[4,576,384]{2,1,0:T(8,128)(2,1)S(1)} %collective-permute-done.got_ref), custom_call_target="tpu_custom_call" | custom-call | tf_op jit(solution)/shard_map/add_pair/pallas_call | solution.py:840
  46.1 1.8 %collective-permute-start.1 = (bf16[576,384]{1,0:T(8,128)(2,1)}, bf16[576,384]{1,0:T(8,128)(2,1)S(1)}, u32[]{:S(2)}, u32[]{:S(2)}) collective-permute-start(bf16[576,384]{1,0:T(8,128)(2,1)} %get-tuple-element.75), channel_id=1, source_target_pairs={{0,2},{1,3},{2,0},{3,1},{4,6},{5,7},{6,4},{7,5},{8,10},{9,11},{10,... | collective-permute-start | bytes 1327112 | tf_op jit(solution)/shard_map/ppermute | solution.py:812
  47.9 1.5 %collective-permute-start.2 = (bf16[576,384]{1,0:T(8,128)(2,1)}, bf16[576,384]{1,0:T(8,128)(2,1)S(1)}, u32[]{:S(2)}, u32[]{:S(2)}) collective-permute-start(bf16[576,384]{1,0:T(8,128)(2,1)} %get-tuple-element.76), channel_id=1, source_target_pairs={{0,4},{1,5},{2,6},{3,7},{4,0},{5,1},{6,2},{7,3},{8,12},{9,13},{10,... | collective-permute-start | bytes 1327112 | tf_op jit(solution)/shard_map/ppermute | solution.py:812
  49.4 0.3 collective-permute-start.3
  49.7 3.8 %all-to-all-done.1 = bf16[8,56,448]{2,1,0:T(8,128)(2,1)} async-done(((bf16[8,56,448]{2,1,0:T(8,128)(2,1)}), bf16[8,56,448]{2,1,0:T(8,128)(2,1)}, u32[]{:S(2)}, u32[]{:S(2)}) %all-to-all-start.1) | async-done | bytes 401440 | tf_op jit(solution)/shard_map/all_to_all | solution.py:808
  53.5 0.0 copy-start
  53.5 10.7 %conv_weight_grad.1 = (f32[96,128]{1,0:T(8,128)S(1)}, bf16[1296,448]{1,0:T(8,128)(2,1)}) custom-call(bf16[448,448]{1,0:T(8,128)(2,1)} %bitcast.8.wire_ref, bf16[96,7,16,448]{3,2,1,0:T(8,128)(2,1)} %bitcast.19), custom_call_target="tpu_custom_call" | custom-call | flops 4161798144 | bytes 9633792 | tf_op jit(solution)/shard_map/conv_weight_grad/pallas_call | solution.py:731
  64.2 0.7 broadcast_in_dim.21
  64.9 3.4 %all-to-all-start.2 = ((bf16[8,96,128]{2,1,0:T(8,128)(2,1)}), bf16[8,96,128]{2,1,0:T(8,128)(2,1)S(1)}, u32[]{:S(2)}, u32[]{:S(2)}) async-start(bf16[8,96,128]{2,1,0:T(8,128)(2,1)} %broadcast_in_dim.21), calls=%async_computation.2 | async-start | bytes 393216 | tf_op jit(solution)/shard_map/all_to_all | solution.py:808
  68.3 0.0 collective-permute-done.1.refs_1_
  68.3 0.0 collective-permute-done.2.refs_2_
  68.4 3.5 %collective-permute-done.3.refs_3_ = bf16[576,384]{1,0:T(8,128)(2,1)S(1)} collective-permute-done((bf16[576,384]{1,0:T(8,128)(2,1)}, bf16[576,384]{1,0:T(8,128)(2,1)S(1)}, u32[]{:S(2)}, u32[]{:S(2)}) %collective-permute-start.3) | collective-permute-done | bytes 442400 | tf_op jit(solution)/shard_map/ppermute | solution.py:812
  71.9 0.0 copy-done
  71.9 0.2 add_cut.1
  72.1 1.6 %collective-permute-start.4 = (bf16[144,384]{1,0:T(8,128)(2,1)S(1)}, bf16[144,384]{1,0:T(8,128)(2,1)S(1)}, u32[]{:S(2)}, u32[]{:S(2)}) collective-permute-start(bf16[144,384]{1,0:T(8,128)(2,1)S(1)} %get-tuple-element.79), channel_id=1, source_target_pairs={{0,8},{8,0},{16,24},{24,16},{1,9},{9,1},{17,25},{25,17},{2,10},{10... | collective-permute-start | bytes 331784 | tf_op jit(solution)/shard_map/ppermute | solution.py:812
  73.8 2.6 %collective-permute-start.5 = (bf16[144,384]{1,0:T(8,128)(2,1)S(1)}, bf16[144,384]{1,0:T(8,128)(2,1)S(1)}, u32[]{:S(2)}, u32[]{:S(2)}) collective-permute-start(bf16[144,384]{1,0:T(8,128)(2,1)S(1)} %get-tuple-element.80), channel_id=1, source_target_pairs={{0,16},{8,24},{16,0},{24,8},{1,17},{9,25},{17,1},{25,9},{2,18},{10... | collective-permute-start | bytes 331784 | tf_op jit(solution)/shard_map/ppermute | solution.py:812
  76.3 0.2 collective-permute-start.6
  76.6 9.9 %feature_grad.1 = bf16[96,7,16,448]{3,2,1,0:T(8,128)(2,1)} custom-call(bf16[1536,432]{1,0:T(8,128)(2,1)} %get-tuple-element.62.band_hbm, bf16[1296,448]{1,0:T(8,128)(2,1)} %get-tuple-element.63.taps_hbm), custom_call_target="tpu_custom_call" | custom-call | flops 4161798144 | bytes 9633792 | tf_op jit(solution)/shard_map/feature_grad/pallas_call | solution.py:785
  86.5 0.0 all-to-all-done.2.conv_ref
  86.5 0.0 collective-permute-done.4.refs_1_
  86.5 0.0 collective-permute-done.5.refs_2_
  86.5 0.0 collective-permute-done.6.refs_3_
  86.5 0.1 join.1.refs_0_
  86.6 0.7 collective-permute-start.7
  87.3 3.5 %collective-permute-start.8 = (bf16[176,384]{1,0:T(8,128)(2,1)S(1)}, bf16[176,384]{1,0:T(8,128)(2,1)S(1)}, u32[]{:S(2)}, u32[]{:S(2)}) collective-permute-start(bf16[176,384]{1,0:T(8,128)(2,1)S(1)} %join.1.refs_0_), channel_id=1, source_target_pairs={{0,16},{8,24},{16,0},{24,8},{1,17},{9,25},{17,1},{25,9},{2,18},{10... | collective-permute-start | bytes 405512 | tf_op jit(solution)/shard_map/ppermute | solution.py:812
  90.8 0.2 collective-permute-start.9
  91.0 2.2 %collective-permute-done.7.refs_1_ = bf16[176,384]{1,0:T(8,128)(2,1)S(1)} collective-permute-done((bf16[176,384]{1,0:T(8,128)(2,1)S(1)}, bf16[176,384]{1,0:T(8,128)(2,1)S(1)}, u32[]{:S(2)}, u32[]{:S(2)}) %collective-permute-start.7) | collective-permute-done | bytes 135200 | tf_op jit(solution)/shard_map/ppermute | solution.py:812
  93.2 7.1 %collective-permute-done.8.refs_2_ = bf16[176,384]{1,0:T(8,128)(2,1)S(1)} collective-permute-done((bf16[176,384]{1,0:T(8,128)(2,1)S(1)}, bf16[176,384]{1,0:T(8,128)(2,1)S(1)}, u32[]{:S(2)}, u32[]{:S(2)}) %collective-permute-start.8) | collective-permute-done | bytes 135200 | tf_op jit(solution)/shard_map/ppermute | solution.py:812
  100.3 0.0 collective-permute-done.9.refs_3_
  100.3 1.0 finish.1
  (3 shorter events, 0.0 us)
Async XLA Ops:
  0.6 0.7 copy-start.2
  1.4 14.4 %copy-start.3 = (f32[384]{0:T(512)S(1)}, f32[384]{0:T(512)}, u32[]{:S(2)}) copy-start(f32[384]{0:T(512)} %param.16) | copy-start | bytes 4612
  1.4 14.4 %copy-start.4 = (f32[384]{0:T(512)S(1)}, f32[384]{0:T(512)}, u32[]{:S(2)}) copy-start(f32[384]{0:T(512)} %param.19) | copy-start | bytes 4612
  1.4 14.4 %copy-start.1 = (bf16[588,384]{1,0:T(8,128)(2,1)S(1)}, bf16[588,384]{1,0:T(8,128)(2,1)}, u32[]{:S(2)}) copy-start(bf16[588,384]{1,0:T(8,128)(2,1)} %patch_ref.1) | copy-start | bytes 1354756
  10.6 14.2 %all-to-all-start = ((bf16[8,56,448]{2,1,0:T(8,128)(2,1)}), bf16[8,56,448]{2,1,0:T(8,128)(2,1)S(1)}, u32[]{:S(2)}, u32[]{:S(2)}) async-start(bf16[8,56,448]{2,1,0:T(8,128)(2,1)} %bitcast.3), calls=%async_computation | async-start | bytes 917504 | tf_op jit(solution)/shard_map/all_to_all | solution.py:808
  39.8 4.3 %collective-permute-start = (bf16[4,576,384]{2,1,0:T(8,128)(2,1)}, bf16[4,576,384]{2,1,0:T(8,128)(2,1)S(1)}, u32[]{:S(2)}, u32[]{:S(2)}) collective-permute-start(bf16[4,576,384]{2,1,0:T(8,128)(2,1)} %get-tuple-element.73), channel_id=1, source_target_pairs={{0,1},{1,0},{2,3},{3,2},{4,5},{5,4},{6,7},{7,6},{8,9},{9,8},{10,11... | collective-permute-start | bytes 5308424 | tf_op jit(solution)/shard_map/ppermute | solution.py:812
  39.8 13.7 %all-to-all-start.1 = ((bf16[8,56,448]{2,1,0:T(8,128)(2,1)}), bf16[8,56,448]{2,1,0:T(8,128)(2,1)}, u32[]{:S(2)}, u32[]{:S(2)}) async-start(bf16[8,56,448]{2,1,0:T(8,128)(2,1)} %bitcast.17), calls=%async_computation.1 | async-start | bytes 917504 | tf_op jit(solution)/shard_map/all_to_all | solution.py:808
  46.1 22.2 %collective-permute-start.1 = (bf16[576,384]{1,0:T(8,128)(2,1)}, bf16[576,384]{1,0:T(8,128)(2,1)S(1)}, u32[]{:S(2)}, u32[]{:S(2)}) collective-permute-start(bf16[576,384]{1,0:T(8,128)(2,1)} %get-tuple-element.75), channel_id=1, source_target_pairs={{0,2},{1,3},{2,0},{3,1},{4,6},{5,7},{6,4},{7,5},{8,10},{9,11},{10,... | collective-permute-start | bytes 1327112 | tf_op jit(solution)/shard_map/ppermute | solution.py:812
  47.9 20.5 %collective-permute-start.2 = (bf16[576,384]{1,0:T(8,128)(2,1)}, bf16[576,384]{1,0:T(8,128)(2,1)S(1)}, u32[]{:S(2)}, u32[]{:S(2)}) collective-permute-start(bf16[576,384]{1,0:T(8,128)(2,1)} %get-tuple-element.76), channel_id=1, source_target_pairs={{0,4},{1,5},{2,6},{3,7},{4,0},{5,1},{6,2},{7,3},{8,12},{9,13},{10,... | collective-permute-start | bytes 1327112 | tf_op jit(solution)/shard_map/ppermute | solution.py:812
  49.4 22.5 %collective-permute-start.3 = (bf16[576,384]{1,0:T(8,128)(2,1)}, bf16[576,384]{1,0:T(8,128)(2,1)S(1)}, u32[]{:S(2)}, u32[]{:S(2)}) collective-permute-start(bf16[576,384]{1,0:T(8,128)(2,1)} %get-tuple-element.77), channel_id=1, source_target_pairs={{0,6},{1,7},{2,4},{3,5},{4,2},{5,3},{6,0},{7,1},{8,14},{9,15},{10,... | collective-permute-start | bytes 1327112 | tf_op jit(solution)/shard_map/ppermute | solution.py:812
  53.5 18.4 %copy-start = (bf16[576,384]{1,0:T(8,128)(2,1)S(1)}, bf16[576,384]{1,0:T(8,128)(2,1)}, u32[]{:S(2)}) copy-start(bf16[576,384]{1,0:T(8,128)(2,1)} %get-tuple-element.74.refs_0_) | copy-start | bytes 1327108
  64.9 21.5 %all-to-all-start.2 = ((bf16[8,96,128]{2,1,0:T(8,128)(2,1)}), bf16[8,96,128]{2,1,0:T(8,128)(2,1)S(1)}, u32[]{:S(2)}, u32[]{:S(2)}) async-start(bf16[8,96,128]{2,1,0:T(8,128)(2,1)} %broadcast_in_dim.21), calls=%async_computation.2 | async-start | bytes 393216 | tf_op jit(solution)/shard_map/all_to_all | solution.py:808
  72.1 14.3 %collective-permute-start.4 = (bf16[144,384]{1,0:T(8,128)(2,1)S(1)}, bf16[144,384]{1,0:T(8,128)(2,1)S(1)}, u32[]{:S(2)}, u32[]{:S(2)}) collective-permute-start(bf16[144,384]{1,0:T(8,128)(2,1)S(1)} %get-tuple-element.79), channel_id=1, source_target_pairs={{0,8},{8,0},{16,24},{24,16},{1,9},{9,1},{17,25},{25,17},{2,10},{10... | collective-permute-start | bytes 331784 | tf_op jit(solution)/shard_map/ppermute | solution.py:812
  73.8 12.7 %collective-permute-start.5 = (bf16[144,384]{1,0:T(8,128)(2,1)S(1)}, bf16[144,384]{1,0:T(8,128)(2,1)S(1)}, u32[]{:S(2)}, u32[]{:S(2)}) collective-permute-start(bf16[144,384]{1,0:T(8,128)(2,1)S(1)} %get-tuple-element.80), channel_id=1, source_target_pairs={{0,16},{8,24},{16,0},{24,8},{1,17},{9,25},{17,1},{25,9},{2,18},{10... | collective-permute-start | bytes 331784 | tf_op jit(solution)/shard_map/ppermute | solution.py:812
  76.3 10.1 %collective-permute-start.6 = (bf16[144,384]{1,0:T(8,128)(2,1)S(1)}, bf16[144,384]{1,0:T(8,128)(2,1)S(1)}, u32[]{:S(2)}, u32[]{:S(2)}) collective-permute-start(bf16[144,384]{1,0:T(8,128)(2,1)S(1)} %get-tuple-element.81), channel_id=1, source_target_pairs={{0,24},{8,16},{16,8},{24,0},{1,25},{9,17},{17,9},{25,1},{2,26},{10... | collective-permute-start | bytes 331784 | tf_op jit(solution)/shard_map/ppermute | solution.py:812
  86.6 6.6 %collective-permute-start.7 = (bf16[176,384]{1,0:T(8,128)(2,1)S(1)}, bf16[176,384]{1,0:T(8,128)(2,1)S(1)}, u32[]{:S(2)}, u32[]{:S(2)}) collective-permute-start(bf16[176,384]{1,0:T(8,128)(2,1)S(1)} %join.1.refs_0_), channel_id=1, source_target_pairs={{0,8},{8,0},{16,24},{24,16},{1,9},{9,1},{17,25},{25,17},{2,10},{10... | collective-permute-start | bytes 405512 | tf_op jit(solution)/shard_map/ppermute | solution.py:812
  87.3 13.0 %collective-permute-start.8 = (bf16[176,384]{1,0:T(8,128)(2,1)S(1)}, bf16[176,384]{1,0:T(8,128)(2,1)S(1)}, u32[]{:S(2)}, u32[]{:S(2)}) collective-permute-start(bf16[176,384]{1,0:T(8,128)(2,1)S(1)} %join.1.refs_0_), channel_id=1, source_target_pairs={{0,16},{8,24},{16,0},{24,8},{1,17},{9,25},{17,1},{25,9},{2,18},{10... | collective-permute-start | bytes 405512 | tf_op jit(solution)/shard_map/ppermute | solution.py:812
  90.8 9.5 %collective-permute-start.9 = (bf16[176,384]{1,0:T(8,128)(2,1)S(1)}, bf16[176,384]{1,0:T(8,128)(2,1)S(1)}, u32[]{:S(2)}, u32[]{:S(2)}) collective-permute-start(bf16[176,384]{1,0:T(8,128)(2,1)S(1)} %join.1.refs_0_), channel_id=1, source_target_pairs={{0,24},{8,16},{16,8},{24,0},{1,25},{9,17},{17,9},{25,1},{2,26},{10... | collective-permute-start | bytes 405512 | tf_op jit(solution)/shard_map/ppermute | solution.py:812

commit v3 on v2

--- a/solution.py
+++ b/solution.py
@@ -517,6 +517,7 @@
 
 def third_kernel(
     space,
+    fc_rows,
     me_ref,
     normed_ref,
     grad_packed_ref,
@@ -540,20 +541,22 @@
     fc1_grad_ref[...] = dot_tn(normed2_ref[...], grad_before_ref[...])
     fc2_grad_ref[...] = dot_tn(hidden_ref[...], cotangent_ref[...].reshape(count, width))
     share = width // space
-    pieces = [(fc1_grad_ref, share, c) for c in range(0, hidden_width, width)]
-    pieces.append((fc2_grad_ref, hidden_width // space, 0))
-    pieces += [(qkv_grad_ref, share, c) for c in range(0, 3 * width, width)]
-    pieces.append((proj_grad_ref, share, 0))
-    spare = keep_ref.shape[1] - sum(rows for _, rows, _ in pieces)
+    fc = [(fc1_grad_ref, share, c) for c in range(0, hidden_width, width)]
+    fc.append((fc2_grad_ref, hidden_width // space, 0))
+    att = [(qkv_grad_ref, share, c) for c in range(0, 3 * width, width)]
+    att.append((proj_grad_ref, share, 0))
     for chip in range(space // 2):
         for other, target in ((0, keep_ref), (1, send_ref)):
             peer = me_ref[0] ^ (2 * chip + other)
-            blocks = [
-                ref[pl.ds(pl.multiple_of(peer * rows, 8), rows), column : column + width]
-                for ref, rows, column in pieces
-            ]
-            if spare:
-                blocks.append(jnp.zeros((spare, width), F32))
+            blocks = []
+            for pieces, held in ((fc, fc_rows), (att, keep_ref.shape[1] - fc_rows)):
+                blocks += [
+                    ref[pl.ds(pl.multiple_of(peer * rows, 8), rows), column : column + width]
+                    for ref, rows, column in pieces
+                ]
+                spare = held - sum(rows for _, rows, _ in pieces)
+                if spare:
+                    blocks.append(jnp.zeros((spare, width), F32))
             target[chip] = jnp.concatenate(blocks, axis=0).astype(BF16)
 
 
@@ -647,10 +650,11 @@
     )(packed, probs, probs_b, grad, unit, scale, norm1, patch, qkv, proj)
 
     total = qkv.size + proj.size + fc1.size + fc2.size
-    rows = round_up(total // (width * sizes.space), 16 * copies)
-    shares = jax.ShapeDtypeStruct((sizes.space // 2, rows, width), BF16)
+    fc_rows = round_up((fc1.size + fc2.size) // (width * sizes.space), 16 * copies)
+    att_rows = round_up((qkv.size + proj.size) // (width * sizes.space), 16 * copies)
+    shares = jax.ShapeDtypeStruct((sizes.space // 2, fc_rows + att_rows, width), BF16)
     keep, send = pl.pallas_call(
-        functools.partial(third_kernel, sizes.space),
+        functools.partial(third_kernel, sizes.space, fc_rows),
         in_specs=[SMEM] + [VMEM] * 8,
         out_specs=(VMEM, VMEM),
         out_shape=(shares, shares),
@@ -661,7 +665,7 @@
         ),
         name="weight_grads",
     )(me, normed, grad_packed, attended, grad, normed2, grad_before, hidden, cotangent)
-    return block_out, wire_grad, keep, send
+    return block_out, wire_grad, keep, send, fc_rows
 
 
 def conv_weight_kernel(
@@ -755,7 +759,7 @@
 
 
 def feature_kernel(
-    sizes, band_hbm, taps_hbm, out_hbm, held_ref, band_ref, taps_ref, sems, fetch_sems
+    sizes, band_hbm, taps_hbm, _, out_hbm, held_ref, band_ref, taps_ref, sems, fetch_sems
 ):
     arrivals = fetch(((band_hbm, band_ref), (taps_hbm, taps_ref)), fetch_sems)
 
@@ -780,11 +784,11 @@
     lax.fori_loop(0, sizes.rows, close, 0)
 
 
-def feature_gradient(sizes, band, taps):
+def feature_gradient(sizes, band, taps, after):
     shape = (sizes.channels, sizes.rows, sizes.frames, sizes.cols)
     return pl.pallas_call(
         functools.partial(feature_kernel, sizes),
-        in_specs=[HBM, HBM],
+        in_specs=[HBM, HBM, VMEM],
         out_specs=HBM,
         out_shape=pltpu.HBM(shape, BF16),
         scratch_shapes=[
@@ -801,7 +805,7 @@
             transcendentals=0,
         ),
         name="feature_grad",
-    )(band, taps)
+    )(band, taps, after)
 
 
 def scatter(values, axis):
@@ -823,101 +827,116 @@
     )(*inputs)
 
 
-def add_pair_kernel(keep_ref, got_ref, first_hbm, *refs):
-    out_refs, (first_ref, sem) = refs[:-2], refs[-2:]
-    leave = pltpu.make_async_copy(first_ref, first_hbm, sem)
-    for place, out_ref in enumerate((first_ref,) + tuple(out_refs)):
-        total = keep_ref[place].astype(F32) + got_ref[place].astype(F32)
-        out_ref[...] = total.astype(BF16)
-        if place == 0:
-            leave.start()
-    leave.wait()
-
-
-def add_pair(keep, got):
-    shape = keep.shape[1:]
-    outs = (pltpu.HBM(shape, BF16),) + (jax.ShapeDtypeStruct(shape, BF16),) * (keep.shape[0] - 1)
-    return pl.pallas_call(
-        add_pair_kernel,
-        in_specs=[VMEM, VMEM],
-        out_specs=(HBM,) + (VMEM,) * (keep.shape[0] - 1),
-        out_shape=outs,
-        scratch_shapes=[pltpu.VMEM(shape, BF16), pltpu.SemaphoreType.DMA(())],
-        compiler_params=pltpu.CompilerParams(vmem_limit_bytes=8 * MIB),
-        name="add_pair",
-    )(keep, got)
-
-
-def add_cut_kernel(copies, me_ref, *refs):
-    terms, outs = refs[:-copies], refs[-copies:]
+def sum_of(refs):
+    total = refs[0][...].astype(F32)
+    for ref in refs[1:]:
+        total = total + ref[...].astype(F32)
+    return total
+
+
+def add_pair_kernel(fc_rows, copies, me_ref, keep_ref, got_ref, *outs):
+    chips = keep_ref.shape[0]
+    for chip in range(chips):
+        total = keep_ref[chip, :fc_rows].astype(F32) + got_ref[chip, :fc_rows].astype(F32)
+        outs[chip][...] = total.astype(BF16)
+    rows = (keep_ref.shape[1] - fc_rows) // copies
+    for relative, out_ref in enumerate(outs[chips:]):
+        at = pl.ds(pl.multiple_of(fc_rows + (me_ref[0] ^ relative) * rows, 16), rows)
+        for chip in range(chips):
+            total = keep_ref[chip, at, :].astype(F32) + got_ref[chip, at, :].astype(F32)
+            out_ref[chip] = total.astype(BF16)
+
+
+def add_pair(me, fc_rows, copies, keep, got):
+    chips, rows, width = keep.shape
+    fc = (jax.ShapeDtypeStruct((fc_rows, width), BF16),) * chips
+    att = (jax.ShapeDtypeStruct((chips, (rows - fc_rows) // copies, width), BF16),) * copies
+    outs = small_call(
+        functools.partial(add_pair_kernel, fc_rows, copies),
+        (me, keep, got),
+        [SMEM, VMEM, VMEM],
+        fc + att,
+        "add_pair",
+    )
+    return outs[:chips], outs[chips:]
+
+
+def add_cut_kernel(chips, copies, me_ref, *refs):
+    fc, att = refs[:chips], refs[chips : chips + copies]
+    outs = refs[chips + copies :]
     rows = outs[0].shape[0]
-    for relative, out_ref in enumerate(outs):
+    for relative, out_ref in enumerate(outs[:copies]):
         at = pl.ds(pl.multiple_of((me_ref[0] ^ relative) * rows, 16), rows)
-        total = terms[0][at, :].astype(F32)
-        for term in terms[1:]:
-            total = total + term[at, :].astype(F32)
-        out_ref[...] = total.astype(BF16)
-
-
-def add_cut(me, copies, terms):
-    rows, width = terms[0].shape
+        out_ref[...] = sum_of([ref.at[at, :] for ref in fc]).astype(BF16)
+    for chip, out_ref in enumerate(outs[copies:]):
+        out_ref[...] = sum_of([ref.at[chip] for ref in att]).astype(BF16)
+
+
+def add_cut(me, fc, att):
+    chips, copies = len(fc), len(att)
+    rows, width = fc[0].shape
     outs = (jax.ShapeDtypeStruct((rows // copies, width), BF16),) * copies
-    return small_call(
-        functools.partial(add_cut_kernel, copies),
-        (me,) + tuple(terms),
-        [SMEM] + [VMEM] * len(terms),
+    outs += (jax.ShapeDtypeStruct(att[0].shape[1:], BF16),) * chips
+    outs = small_call(
+        functools.partial(add_cut_kernel, chips, copies),
+        (me,) + tuple(fc) + tuple(att),
+        [SMEM] + [VMEM] * (chips + copies),
         outs,
         "add_cut",
     )
-
-
-def join_kernel(conv_ref, *refs):
-    terms, out_ref = refs[:-1], refs[-1]
-    rows = terms[0].shape[0]
-    total = terms[0][...].astype(F32)
-    for term in terms[1:]:
-        total = total + term[...].astype(F32)
-    out_ref[:rows, :] = total.astype(BF16)
-    conv = conv_ref[0].astype(F32)
-    for place in range(1, conv_ref.shape[0]):
-        conv = conv + conv_ref[place].astype(F32)
+    return outs[:copies], outs[copies:]
+
+
+def join_kernel(copies, conv_ref, *refs):
+    fc, att, out_ref = refs[:copies], refs[copies:-1], refs[-1]
+    at = fc[0].shape[0]
+    out_ref[:at, :] = sum_of(fc).astype(BF16)
+    out_ref[at : at + att[0].shape[0], :] = sum_of(att).astype(BF16)
+    at += att[0].shape[0]
+    conv = sum_of([conv_ref.at[place] for place in range(conv_ref.shape[0])])
     strips = out_ref.shape[1] // conv.shape[1]
     tall = conv.shape[0] // strips
     conv = [conv[strip * tall : (strip + 1) * tall] for strip in range(strips)]
-    out_ref[rows:, :] = jnp.concatenate(conv, axis=1).astype(BF16)
-
-
-def join(terms, conv_all):
-    rows, width = terms[0].shape
-    more = conv_all.shape[1] * conv_all.shape[2] // width
-    out = jax.ShapeDtypeStruct((rows + more, width), BF16)
+    out_ref[at:, :] = jnp.concatenate(conv, axis=1).astype(BF16)
+
+
+def join(fc, att, conv_all):
+    width = fc[0].shape[1]
+    rows = fc[0].shape[0] + att[0].shape[0] + conv_all.shape[1] * conv_all.shape[2] // width
     return small_call(
-        join_kernel, (conv_all,) + tuple(terms), [VMEM] * (1 + len(terms)), out, "join"
+        functools.partial(join_kernel, len(fc)),
+        (conv_all,) + tuple(fc) + tuple(att),
+        [VMEM] * (1 + len(fc) + len(att)),
+        jax.ShapeDtypeStruct((rows, width), BF16),
+        "join",
     )
 
 
 def finish_kernel(copies, lanes, me_ref, *refs):
     pieces = refs[:copies]
-    qkv_ref, proj_ref, fc1_ref, fc2_ref, conv_ref, whole = refs[copies:]
+    qkv_ref, proj_ref, fc1_ref, fc2_ref, conv_ref, fc, att = refs[copies:]
     width = proj_ref.shape[1]
-    rows = whole.shape[0] // copies
+    fc_rows, att_rows = fc.shape[0] // copies, att.shape[0] // copies
     total = None
     for relative, piece in enumerate(pieces):
-        at = pl.ds(pl.multiple_of((me_ref[0] ^ relative) * rows, 16), rows)
-        whole[at, :] = piece[:rows, :].astype(F32)
-        conv = piece[rows:, :].astype(F32)
+        place = me_ref[0] ^ relative
+        at = pl.ds(pl.multiple_of(place * fc_rows, 16), fc_rows)
+        fc[at, :] = piece[:fc_rows, :].astype(F32)
+        at = pl.ds(pl.multiple_of(place * att_rows, 16), att_rows)
+        att[at, :] = piece[fc_rows : fc_rows + att_rows, :].astype(F32)
+        conv = piece[fc_rows + att_rows :, :].astype(F32)
         total = conv if total is None else total + conv
     share = proj_ref.shape[0]
     at = 0
     for part in range(0, fc1_ref.shape[1], width):
-        fc1_ref[:, part : part + width] = whole[at : at + share, :]
+        fc1_ref[:, part : part + width] = fc[at : at + share, :]
         at += share
-    fc2_ref[...] = whole[at : at + fc2_ref.shape[0], :]
-    at += fc2_ref.shape[0]
+    fc2_ref[...] = fc[at : at + fc2_ref.shape[0], :]
+    at = 0
     for part in range(0, qkv_ref.shape[1], width):
-        qkv_ref[:, part : part + width] = whole[at : at + share, :]
+        qkv_ref[:, part : part + width] = att[at : at + share, :]
         at += share
-    proj_ref[...] = whole[at : at + share, :]
+    proj_ref[...] = att[at : at + share, :]
     total = jnp.concatenate(
         [total[:, strip : strip + lanes] for strip in range(0, width, lanes)], axis=0
     )
@@ -929,14 +948,17 @@
                 conv_ref[a, b, e] = total[at : at + colours, :channels]
 
 
-def finish(me, pieces, rows, lanes, shapes):
+def finish(me, pieces, fc_rows, att_rows, lanes, shapes):
     copies, width = len(pieces), pieces[0].shape[1]
     return pl.pallas_call(
         functools.partial(finish_kernel, copies, lanes),
         in_specs=[SMEM] + [VMEM] * copies,
         out_specs=(VMEM,) * 5,
         out_shape=tuple(jax.ShapeDtypeStruct(shape, F32) for shape in shapes),
-        scratch_shapes=[pltpu.VMEM((copies * rows, width), F32)],
+        scratch_shapes=[
+            pltpu.VMEM((copies * fc_rows, width), F32),
+            pltpu.VMEM((copies * att_rows, width), F32),
+        ],
         compiler_params=pltpu.CompilerParams(vmem_limit_bytes=12 * MIB),
         name="finish",
     )(me, *pieces)
@@ -972,23 +994,27 @@
         for array in (pos_embed, qkv_weight, proj_weight, fc1_weight, fc2_weight, out_grad[0])
     )
     params = (pos, patch, norm1, qkv, proj, norm2, fc1, fc2)
-    block_out, wire_grad, keep, send = transformer(sizes, copies, me, wire, cotangent, params)
+    block_out, wire_grad, keep, send, fc_rows = transformer(
+        sizes, copies, me, wire, cotangent, params
+    )
 
     wire_grad = scatter(wire_grad, "space")
     conv_part, tap_rows = conv_weight_grad(sizes, wire_grad, x)
-    feature_grad = feature_gradient(sizes, in_hbm(band), in_hbm(tap_rows))
 
     conv_all = scatter(
         jnp.broadcast_to(conv_part.astype(BF16)[None], (space,) + conv_part.shape), "space"
     )
 
-    chips = add_pair(keep, exchange(send, "space", 1))
-    terms = [exchange(chips[r], "space", 2 * r) for r in range(1, len(chips))]
-    cuts = add_cut(me_dp, copies, [chips[0]] + terms)
-    terms = [exchange(cuts[r], "dp", r) for r in range(1, copies)]
-    conv_all, feature_grad = lax.optimization_barrier((conv_all, feature_grad))
-    piece = join([cuts[0]] + terms, conv_all)
+    fc, att = add_pair(me_dp, fc_rows, copies, keep, exchange(send, "space", 1))
+    fc = [fc[0]] + [exchange(fc[r], "space", 2 * r) for r in range(1, len(fc))]
+    att = [att[0]] + [exchange(att[r], "dp", r) for r in range(1, copies)]
+    fc, att = add_cut(me_dp, fc, att)
+    fc_piece, att_piece = fc[0].shape[0], att[0].shape[0]
+    fc = [fc[0]] + [exchange(fc[r], "dp", r) for r in range(1, copies)]
+    att = [att[0]] + [exchange(att[r], "space", 2 * r) for r in range(1, len(att))]
+    piece = join(fc, att, conv_all)
     pieces = [piece] + [exchange(piece, "dp", r) for r in range(1, copies)]
+    feature_grad = feature_gradient(sizes, in_hbm(band), in_hbm(tap_rows), piece)
     share = width // space
     shapes = (
         (share, 3 * width),
@@ -998,7 +1024,7 @@
         conv_weight.shape,
     )
     qkv_grad, proj_grad, fc1_grad, fc2_grad, conv_grad = finish(
-        me_dp, pieces, cuts[0].shape[0], conv_part.shape[1], shapes
+        me_dp, pieces, fc_piece, att_piece, conv_part.shape[1], shapes
     )
 
     return (

time: 102 us -> 101 us (level)
  waiting for transfers between devices: 20.1 us -> 8.37 us
  starting transfers between devices: 25.3 us -> 35.3 us
  local copies, waits for them, and re-layouts: 1.46 us -> 2.83 us
    ppermute x10 -> x16, starting transfers between devices: 12.5 us -> 22.3 us  [exchange(): lax.ppermute(values, axis, [(i, i ^ relative) for i in range(lax.axis_siz...]
    ppermute x10 -> x16, waiting for transfers between devices: 12.8 us -> 4.81 us  [exchange(): lax.ppermute(values, axis, [(i, i ^ relative) for i in range(lax.axis_siz...]
    all_to_all x3, waiting for transfers between devices: 7.34 us -> 3.56 us  [scatter(): return lax.all_to_all(values, axis, split_axis=0, concat_axis=0, tiled=True)]
    pallas_call x2 -> x1, Pallas kernels: 5.59 us -> 3.63 us  [transformer(): pl.pallas_call(functools.partial(third_kernel, sizes.space, fc_rows), in_...]
    unnamed x10 -> x16, local copies, waits for them, and re-layouts: 0.75 us -> 2.12 us
    pallas_call x2 -> x3, Pallas kernels: 0.32 us -> 1.48 us  [small_call(): pl.pallas_call(kernel, in_specs=specs, out_specs=jax.tree.map(lambda _: V...]
  transfers between devices with their start and end apart: 13 -> 19, of which waited for: 5 -> 3; matrix products, arithmetic and copies ran while one was open for 1% -> 1% of each run, Pallas kernels for 28% -> 27%
where the time goes in v3:
time: 101 us; the launch traced here: 100 us
  Pallas kernels  52.7 us (52%)
  starting transfers between devices  35.3 us (35%)
  waiting for transfers between devices  8.37 us (8%)
  local copies, waits for them, and re-layouts  2.83 us (3%)
    ppermute x16, starting transfers between devices, exchange(): lax.ppermute(values, axis, [(i, i ^ relative) for i in range(lax.axis_siz...  22.3 us
    all_to_all x3, starting transfers between devices, scatter(): return lax.all_to_all(values, axis, split_axis=0, concat_axis=0, tiled=True)  13.1 us
    pallas_call x1, Pallas kernels, conv_weight_grad(): pl.pallas_call(functools.partial(conv_weight_kernel, sizes), in_specs=[VM...  10.7 us
    pallas_call x1, Pallas kernels, feature_gradient(): pl.pallas_call(functools.partial(feature_kernel, sizes), in_specs=[HBM, H...  9.87 us
    pallas_call x1, Pallas kernels, conv_forward(): pl.pallas_call(functools.partial(conv_forward_kernel, sizes), in_specs=[V...  9.15 us
    pallas_call x1, Pallas kernels, transformer(): pl.pallas_call(functools.partial(first_kernel, sizes), in_specs=[VMEM] *...  6.97 us
    pallas_call x1, Pallas kernels, prepare(): pl.pallas_call(functools.partial(prepare_kernel, sizes), grid=(steps,), i...  5.44 us
    ppermute x16, waiting for transfers between devices, exchange(): lax.ppermute(values, axis, [(i, i ^ relative) for i in range(lax.axis_siz...  4.81 us
  transfers between devices with their start and end apart: 19, of which 3 were waited for; matrix products, arithmetic and copies ran while one was open for 1% of the time, Pallas kernels for 27%

profile of v3, /device:TPU:0, one launch (start us, length us, event | category | flops | bytes accessed | tf_op | source)
XLA Modules:
  0.0 100.1 jit_solution(7461476684060716531)
XLA Ops:
  0.6 0.0 copy-start.5
  0.6 0.7 copy-done.5
  1.4 0.0 copy-start.6
  1.4 0.0 copy-start.7
  1.4 0.0 copy-start.4
  1.4 9.1 %conv_forward.1 = (bf16[448,448]{1,0:T(8,128)(2,1)}, bf16[81,96]{1,0:T(8,128)(2,1)S(1)}) custom-call(bf16[27,3,96]{2,1,0:T(4,128)(2,1)S(1)} %bitcast.16, bf16[96,7,16,448]{3,2,1,0:T(8,128)(2,1)} %bitcast.18), custom_call_target="tpu_custom_call" | custom-call | flops 4161798144 | bytes 9633792 | tf_op jit(solution)/shard_map/conv_forward/pallas_call | solution.py:175
  10.5 5.2 %all-to-all-start = ((bf16[8,56,448]{2,1,0:T(8,128)(2,1)}), bf16[8,56,448]{2,1,0:T(8,128)(2,1)S(1)}, u32[]{:S(2)}, u32[]{:S(2)}) async-start(bf16[8,56,448]{2,1,0:T(8,128)(2,1)} %bitcast.3), calls=%async_computation | async-start | bytes 917504 | tf_op jit(solution)/shard_map/all_to_all | solution.py:812
  15.7 0.0 copy-done.6
  15.7 0.0 copy-done.7
  15.8 0.0 copy-done.4
  15.8 5.4 %prepare.1 = (bf16[896,384]{1,0:T(8,128)(2,1)}, bf16[1536,432]{1,0:T(8,128)(2,1)}) custom-call(bf16[81,96]{1,0:T(8,128)(2,1)S(1)} %get-tuple-element.54.weight_ref, bf16[588,384]{1,0:T(8,128)(2,1)S(1)} %copy-done.4), custom_call_target="tpu_custom_call" | custom-call | flops 4000000000 | bytes 4194304 | tf_op jit(solution)/shard_map/prepare/pallas_call | solution.py:231
  21.2 3.6 %all-to-all-done = bf16[8,56,448]{2,1,0:T(8,128)(2,1)S(1)} async-done(((bf16[8,56,448]{2,1,0:T(8,128)(2,1)}), bf16[8,56,448]{2,1,0:T(8,128)(2,1)S(1)}, u32[]{:S(2)}, u32[]{:S(2)}) %all-to-all-start) | async-done | bytes 401440 | tf_op jit(solution)/shard_map/all_to_all | solution.py:812
  24.8 7.0 %block_forward.1 = (bf16[2,128,384]{2,1,0:T(8,128)(2,1)}, bf16[256,384]{1,0:T(8,128)(2,1)S(1)}, bf16[256,1152]{1,0:T(8,128)(2,1)S(1)}, f32[12,128,128]{2,1,0:T(8...) custom-call(bf16[448,448]{1,0:T(8,128)(2,1)S(1)} %bitcast.15, ...), custom_call_target="tpu_custom_call" | custom-call | flops 2164260864 | bytes 12582912 | tf_op jit(solution)/shard_map/block_forward/pallas_call | solution.py:590
  31.7 4.4 %block_backward.1 = (bf16[448,448]{1,0:T(8,128)(2,1)}, bf16[256,1152]{1,0:T(8,128)(2,1)S(1)}) custom-call(bf16[256,1152]{1,0:T(8,128)(2,1)S(1)} %get-tuple-element.58.packed_ref, f32[12,128,128]{2,1,0:T(8,128)S(1)} %get-tuple-element.59.probs_ref, bf16[12,128,128]{2,1,0:T(8,128)(2,1)S(1)} %get-tuple-element.60.probs_b_ref, ...), custom_call_target="tpu_custom_call" | custom-call | flops 956301312 | bytes 6291456 | tf_op jit(solution)/shard_map/block_backward/pallas_call | solution.py:626
  36.2 3.6 %weight_grads.1 = (bf16[4,576,384]{2,1,0:T(8,128)(2,1)S(1)}, bf16[4,576,384]{2,1,0:T(8,128)(2,1)}) custom-call(s32[1]{0:T(128)} %bitcast.11.me_ref, bf16[256,384]{1,0:T(8,128)(2,1)S(1)} %get-tuple-element.70.normed_ref, bf16[256,1152]{1,0:T(8,128)(2,1)S(1)} %get-tuple-element.71.grad_packed_ref, bf16[256,384]{1,0:T(8,128)(2,1)S(1)} %get-tuple-element.72.attended_ref, ...), custom_call_target="tpu_custom_call" | custom-call | flops 905969664 | bytes 8388608 | tf_op jit(solution)/shard_map/weight_grads/pallas_call | solution.py:656
  39.8 0.0 collective-permute-start
  39.8 4.3 %all-to-all-start.1 = ((bf16[8,56,448]{2,1,0:T(8,128)(2,1)}), bf16[8,56,448]{2,1,0:T(8,128)(2,1)}, u32[]{:S(2)}, u32[]{:S(2)}) async-start(bf16[8,56,448]{2,1,0:T(8,128)(2,1)} %bitcast.17), calls=%async_computation.1 | async-start | bytes 917504 | tf_op jit(solution)/shard_map/all_to_all | solution.py:812
  44.1 0.0 collective-permute-done.got_ref
  44.1 1.1 %add_pair.1 = (bf16[384,384]{1,0:T(8,128)(2,1)S(1)}, bf16[384,384]{1,0:T(8,128)(2,1)}, bf16[384,384]{1,0:T(8,128)(2,1)}, bf16[384,384]{1,0:T(8,128)(2,1)}, bf16[...) custom-call(s32[1]{0:T(128)} %bitcast.10.me_ref, ...), custom_call_target="tpu_custom_call" | custom-call | tf_op jit(solution)/shard_map/add_pair/pallas_call | solution.py:820
  45.2 0.0 copy-start
  45.2 0.7 copy-done
  45.9 0.0 copy-start.2
  46.0 0.7 copy-done.2
  46.6 1.6 %collective-permute-start.4 = (bf16[4,48,384]{2,1,0:T(8,128)(2,1)S(1)}, bf16[4,48,384]{2,1,0:T(8,128)(2,1)S(1)}, u32[]{:S(2)}, u32[]{:S(2)}) collective-permute-start(bf16[4,48,384]{2,1,0:T(8,128)(2,1)S(1)} %get-tuple-element.83), channel_id=1, source_target_pairs={{0,8},{8,0},{16,24},{24,16},{1,9},{9,1},{17,25},{25,17},{2,10},{10... | collective-permute-start | bytes 442376 | tf_op jit(solution)/shard_map/ppermute | solution.py:816
  48.2 1.7 %collective-permute-start.1 = (bf16[384,384]{1,0:T(8,128)(2,1)}, bf16[384,384]{1,0:T(8,128)(2,1)S(1)}, u32[]{:S(2)}, u32[]{:S(2)}) collective-permute-start(bf16[384,384]{1,0:T(8,128)(2,1)} %get-tuple-element.79), channel_id=1, source_target_pairs={{0,2},{1,3},{2,0},{3,1},{4,6},{5,7},{6,4},{7,5},{8,10},{9,11},{10,... | collective-permute-start | bytes 884744 | tf_op jit(solution)/shard_map/ppermute | solution.py:816
  49.9 1.5 %collective-permute-start.2 = (bf16[384,384]{1,0:T(8,128)(2,1)}, bf16[384,384]{1,0:T(8,128)(2,1)S(1)}, u32[]{:S(2)}, u32[]{:S(2)}) collective-permute-start(bf16[384,384]{1,0:T(8,128)(2,1)} %get-tuple-element.80), channel_id=1, source_target_pairs={{0,4},{1,5},{2,6},{3,7},{4,0},{5,1},{6,2},{7,3},{8,12},{9,13},{10,... | collective-permute-start | bytes 884744 | tf_op jit(solution)/shard_map/ppermute | solution.py:816
  51.4 0.3 collective-permute-start.3
  51.7 2.6 %collective-permute-start.5 = (bf16[4,48,384]{2,1,0:T(8,128)(2,1)}, bf16[4,48,384]{2,1,0:T(8,128)(2,1)S(1)}, u32[]{:S(2)}, u32[]{:S(2)}) collective-permute-start(bf16[4,48,384]{2,1,0:T(8,128)(2,1)} %get-tuple-element.84), channel_id=1, source_target_pairs={{0,16},{8,24},{16,0},{24,8},{1,17},{9,25},{17,1},{25,9},{2,18},{10... | collective-permute-start | bytes 442376 | tf_op jit(solution)/shard_map/ppermute | solution.py:816
  54.3 0.0 collective-permute-done.4.refs_5_
  54.3 2.2 %collective-permute-start.6 = (bf16[4,48,384]{2,1,0:T(8,128)(2,1)}, bf16[4,48,384]{2,1,0:T(8,128)(2,1)S(1)}, u32[]{:S(2)}, u32[]{:S(2)}) collective-permute-start(bf16[4,48,384]{2,1,0:T(8,128)(2,1)} %get-tuple-element.85), channel_id=1, source_target_pairs={{0,24},{8,16},{16,8},{24,0},{1,25},{9,17},{17,9},{25,1},{2,26},{10... | collective-permute-start | bytes 442376 | tf_op jit(solution)/shard_map/ppermute | solution.py:816
  56.4 0.0 all-to-all-done.1
  56.4 10.7 %conv_weight_grad.1 = (f32[96,128]{1,0:T(8,128)S(1)}, bf16[1296,448]{1,0:T(8,128)(2,1)}) custom-call(bf16[448,448]{1,0:T(8,128)(2,1)} %bitcast.8.wire_ref, bf16[96,7,16,448]{3,2,1,0:T(8,128)(2,1)} %bitcast.19), custom_call_target="tpu_custom_call" | custom-call | flops 4161798144 | bytes 9633792 | tf_op jit(solution)/shard_map/conv_weight_grad/pallas_call | solution.py:735
  67.2 0.7 broadcast_in_dim.21
  67.9 3.6 %all-to-all-start.2 = ((bf16[8,96,128]{2,1,0:T(8,128)(2,1)}), bf16[8,96,128]{2,1,0:T(8,128)(2,1)S(1)}, u32[]{:S(2)}, u32[]{:S(2)}) async-start(bf16[8,96,128]{2,1,0:T(8,128)(2,1)} %broadcast_in_dim.21), calls=%async_computation.2 | async-start | bytes 393216 | tf_op jit(solution)/shard_map/all_to_all | solution.py:812
  71.5 0.0 collective-permute-done.5.refs_6_
  71.5 0.0 collective-permute-done.6.refs_7_
  71.5 0.0 collective-permute-done.1.refs_1_
  71.5 0.0 collective-permute-done.2.refs_2_
  71.5 0.0 collective-permute-done.3.refs_3_
  71.5 0.0 copy-done.1
  71.5 0.0 copy-done.3
  71.6 0.3 add_cut.1
  71.8 2.1 %collective-permute-start.10 = (bf16[48,384]{1,0:T(8,128)(2,1)S(1)}, bf16[48,384]{1,0:T(8,128)(2,1)S(1)}, u32[]{:S(2)}, u32[]{:S(2)}) collective-permute-start(bf16[48,384]{1,0:T(8,128)(2,1)S(1)} %get-tuple-element.91), channel_id=1, source_target_pairs={{0,2},{1,3},{2,0},{3,1},{4,6},{5,7},{6,4},{7,5},{8,10},{9,11},{10,... | collective-permute-start | bytes 110600 | tf_op jit(solution)/shard_map/ppermute | solution.py:816
  73.9 0.0 collective-permute-start.7
  73.9 2.5 %collective-permute-start.8 = (bf16[96,384]{1,0:T(8,128)(2,1)S(1)}, bf16[96,384]{1,0:T(8,128)(2,1)S(1)}, u32[]{:S(2)}, u32[]{:S(2)}) collective-permute-start(bf16[96,384]{1,0:T(8,128)(2,1)S(1)} %get-tuple-element.88), channel_id=1, source_target_pairs={{0,16},{8,24},{16,0},{24,8},{1,17},{9,25},{17,1},{25,9},{2,18},{10... | collective-permute-start | bytes 221192 | tf_op jit(solution)/shard_map/ppermute | solution.py:816
  76.4 1.8 %collective-permute-start.9 = (bf16[96,384]{1,0:T(8,128)(2,1)S(1)}, bf16[96,384]{1,0:T(8,128)(2,1)S(1)}, u32[]{:S(2)}, u32[]{:S(2)}) collective-permute-start(bf16[96,384]{1,0:T(8,128)(2,1)S(1)} %get-tuple-element.89), channel_id=1, source_target_pairs={{0,24},{8,16},{16,8},{24,0},{1,25},{9,17},{17,9},{25,1},{2,26},{10... | collective-permute-start | bytes 221192 | tf_op jit(solution)/shard_map/ppermute | solution.py:816
  78.3 1.5 %collective-permute-start.11 = (bf16[48,384]{1,0:T(8,128)(2,1)S(1)}, bf16[48,384]{1,0:T(8,128)(2,1)S(1)}, u32[]{:S(2)}, u32[]{:S(2)}) collective-permute-start(bf16[48,384]{1,0:T(8,128)(2,1)S(1)} %get-tuple-element.92), channel_id=1, source_target_pairs={{0,4},{1,5},{2,6},{3,7},{4,0},{5,1},{6,2},{7,3},{8,12},{9,13},{10,... | collective-permute-start | bytes 110600 | tf_op jit(solution)/shard_map/ppermute | solution.py:816
  79.7 0.0 collective-permute-done.10.refs_5_
  79.8 0.1 collective-permute-start.12
  79.8 0.0 all-to-all-done.2.conv_ref
  79.8 2.8 %collective-permute-done.11.refs_6_ = bf16[48,384]{1,0:T(8,128)(2,1)S(1)} collective-permute-done((bf16[48,384]{1,0:T(8,128)(2,1)S(1)}, bf16[48,384]{1,0:T(8,128)(2,1)S(1)}, u32[]{:S(2)}, u32[]{:S(2)}) %collective-permute-start.11) | collective-permute-done | bytes 36896 | tf_op jit(solution)/shard_map/ppermute | solution.py:816
  82.6 2.0 %collective-permute-done.12.refs_7_ = bf16[48,384]{1,0:T(8,128)(2,1)S(1)} collective-permute-done((bf16[48,384]{1,0:T(8,128)(2,1)S(1)}, bf16[48,384]{1,0:T(8,128)(2,1)S(1)}, u32[]{:S(2)}, u32[]{:S(2)}) %collective-permute-start.12) | collective-permute-done | bytes 36896 | tf_op jit(solution)/shard_map/ppermute | solution.py:816
  84.6 0.0 collective-permute-done.7.refs_1_
  84.6 0.0 collective-permute-done.8.refs_2_
  84.6 0.0 collective-permute-done.9.refs_3_
  84.6 0.1 join.1._.refs_0_
  84.7 0.1 collective-permute-start.13
  84.8 2.5 %collective-permute-start.14 = (bf16[176,384]{1,0:T(8,128)(2,1)S(1)}, bf16[176,384]{1,0:T(8,128)(2,1)S(1)}, u32[]{:S(2)}, u32[]{:S(2)}) collective-permute-start(bf16[176,384]{1,0:T(8,128)(2,1)S(1)} %join.1._.refs_0_), channel_id=1, source_target_pairs={{0,16},{8,24},{16,0},{24,8},{1,17},{9,25},{17,1},{25,9},{2,18},{10... | collective-permute-start | bytes 405512 | tf_op jit(solution)/shard_map/ppermute | solution.py:816
  87.3 1.8 %collective-permute-start.15 = (bf16[176,384]{1,0:T(8,128)(2,1)S(1)}, bf16[176,384]{1,0:T(8,128)(2,1)S(1)}, u32[]{:S(2)}, u32[]{:S(2)}) collective-permute-start(bf16[176,384]{1,0:T(8,128)(2,1)S(1)} %join.1._.refs_0_), channel_id=1, source_target_pairs={{0,24},{8,16},{16,8},{24,0},{1,25},{9,17},{17,9},{25,1},{2,26},{10... | collective-permute-start | bytes 405512 | tf_op jit(solution)/shard_map/ppermute | solution.py:816
  89.2 9.9 %feature_grad.1 = bf16[96,7,16,448]{3,2,1,0:T(8,128)(2,1)} custom-call(bf16[1536,432]{1,0:T(8,128)(2,1)} %get-tuple-element.57.band_hbm, bf16[1296,448]{1,0:T(8,128)(2,1)} %get-tuple-element.68.taps_hbm, bf16[176,384]{1,0:T(8,128)(2,1)S(1)} %join.1._.refs_0_), custom_call_target="tpu_custom_call" | custom-call | flops 4161798144 | bytes 9633792 | tf_op jit(solution)/shard_map/feature_grad/pallas_call | solution.py:789
  99.0 0.0 collective-permute-done.13.refs_1_
  99.1 0.0 collective-permute-done.14.refs_2_
  99.1 0.0 collective-permute-done.15.refs_3_
  99.1 1.0 %finish.1 = (f32[48,1152]{1,0:T(8,128)}, f32[48,384]{1,0:T(8,128)}, f32[48,1536]{1,0:T(8,128)}, f32[192,384]{1,0:T(8,128)}, f32[3,3,3,3,96]{4,3,2,1,0:T(4,128)}) custom-call(s32[1]{0:T(128)} %bitcast.10.me_ref, bf16[176,384]{1,0:T(8,128)(2,1)S(1)} %join.1._.refs_0_, bf16[176,384]{1,0:T(8,128)(2,1)S(1)} %collective-permute-done.13.refs_1_, ...), custom_call_target="tpu_custom_call" | custom-call | tf_op jit(solution)/shard_map/finish/pallas_call | solution.py:953
  (5 shorter events, 0.0 us)
Async XLA Ops:
  0.6 0.7 copy-start.5
  1.4 14.3 %copy-start.6 = (f32[384]{0:T(512)S(1)}, f32[384]{0:T(512)}, u32[]{:S(2)}) copy-start(f32[384]{0:T(512)} %param.16) | copy-start | bytes 4612
  1.4 14.4 %copy-start.7 = (f32[384]{0:T(512)S(1)}, f32[384]{0:T(512)}, u32[]{:S(2)}) copy-start(f32[384]{0:T(512)} %param.19) | copy-start | bytes 4612
  1.4 14.4 %copy-start.4 = (bf16[588,384]{1,0:T(8,128)(2,1)S(1)}, bf16[588,384]{1,0:T(8,128)(2,1)}, u32[]{:S(2)}) copy-start(bf16[588,384]{1,0:T(8,128)(2,1)} %patch_ref.1) | copy-start | bytes 1354756
  10.5 14.2 %all-to-all-start = ((bf16[8,56,448]{2,1,0:T(8,128)(2,1)}), bf16[8,56,448]{2,1,0:T(8,128)(2,1)S(1)}, u32[]{:S(2)}, u32[]{:S(2)}) async-start(bf16[8,56,448]{2,1,0:T(8,128)(2,1)} %bitcast.3), calls=%async_computation | async-start | bytes 917504 | tf_op jit(solution)/shard_map/all_to_all | solution.py:812
  39.8 4.3 %collective-permute-start = (bf16[4,576,384]{2,1,0:T(8,128)(2,1)}, bf16[4,576,384]{2,1,0:T(8,128)(2,1)S(1)}, u32[]{:S(2)}, u32[]{:S(2)}) collective-permute-start(bf16[4,576,384]{2,1,0:T(8,128)(2,1)} %get-tuple-element.77), channel_id=1, source_target_pairs={{0,1},{1,0},{2,3},{3,2},{4,5},{5,4},{6,7},{7,6},{8,9},{9,8},{10,11... | collective-permute-start | bytes 5308424 | tf_op jit(solution)/shard_map/ppermute | solution.py:816
  39.8 16.6 %all-to-all-start.1 = ((bf16[8,56,448]{2,1,0:T(8,128)(2,1)}), bf16[8,56,448]{2,1,0:T(8,128)(2,1)}, u32[]{:S(2)}, u32[]{:S(2)}) async-start(bf16[8,56,448]{2,1,0:T(8,128)(2,1)} %bitcast.17), calls=%async_computation.1 | async-start | bytes 917504 | tf_op jit(solution)/shard_map/all_to_all | solution.py:812
  45.2 0.7 copy-start
  45.9 0.7 copy-start.2
  46.6 7.7 %collective-permute-start.4 = (bf16[4,48,384]{2,1,0:T(8,128)(2,1)S(1)}, bf16[4,48,384]{2,1,0:T(8,128)(2,1)S(1)}, u32[]{:S(2)}, u32[]{:S(2)}) collective-permute-start(bf16[4,48,384]{2,1,0:T(8,128)(2,1)S(1)} %get-tuple-element.83), channel_id=1, source_target_pairs={{0,8},{8,0},{16,24},{24,16},{1,9},{9,1},{17,25},{25,17},{2,10},{10... | collective-permute-start | bytes 442376 | tf_op jit(solution)/shard_map/ppermute | solution.py:816
  48.2 23.3 %collective-permute-start.1 = (bf16[384,384]{1,0:T(8,128)(2,1)}, bf16[384,384]{1,0:T(8,128)(2,1)S(1)}, u32[]{:S(2)}, u32[]{:S(2)}) collective-permute-start(bf16[384,384]{1,0:T(8,128)(2,1)} %get-tuple-element.79), channel_id=1, source_target_pairs={{0,2},{1,3},{2,0},{3,1},{4,6},{5,7},{6,4},{7,5},{8,10},{9,11},{10,... | collective-permute-start | bytes 884744 | tf_op jit(solution)/shard_map/ppermute | solution.py:816
  49.9 21.6 %collective-permute-start.2 = (bf16[384,384]{1,0:T(8,128)(2,1)}, bf16[384,384]{1,0:T(8,128)(2,1)S(1)}, u32[]{:S(2)}, u32[]{:S(2)}) collective-permute-start(bf16[384,384]{1,0:T(8,128)(2,1)} %get-tuple-element.80), channel_id=1, source_target_pairs={{0,4},{1,5},{2,6},{3,7},{4,0},{5,1},{6,2},{7,3},{8,12},{9,13},{10,... | collective-permute-start | bytes 884744 | tf_op jit(solution)/shard_map/ppermute | solution.py:816
  51.4 20.1 %collective-permute-start.3 = (bf16[384,384]{1,0:T(8,128)(2,1)}, bf16[384,384]{1,0:T(8,128)(2,1)S(1)}, u32[]{:S(2)}, u32[]{:S(2)}) collective-permute-start(bf16[384,384]{1,0:T(8,128)(2,1)} %get-tuple-element.81), channel_id=1, source_target_pairs={{0,6},{1,7},{2,4},{3,5},{4,2},{5,3},{6,0},{7,1},{8,14},{9,15},{10,... | collective-permute-start | bytes 884744 | tf_op jit(solution)/shard_map/ppermute | solution.py:816
  51.7 19.8 %collective-permute-start.5 = (bf16[4,48,384]{2,1,0:T(8,128)(2,1)}, bf16[4,48,384]{2,1,0:T(8,128)(2,1)S(1)}, u32[]{:S(2)}, u32[]{:S(2)}) collective-permute-start(bf16[4,48,384]{2,1,0:T(8,128)(2,1)} %get-tuple-element.84), channel_id=1, source_target_pairs={{0,16},{8,24},{16,0},{24,8},{1,17},{9,25},{17,1},{25,9},{2,18},{10... | collective-permute-start | bytes 442376 | tf_op jit(solution)/shard_map/ppermute | solution.py:816
  54.3 17.2 %collective-permute-start.6 = (bf16[4,48,384]{2,1,0:T(8,128)(2,1)}, bf16[4,48,384]{2,1,0:T(8,128)(2,1)S(1)}, u32[]{:S(2)}, u32[]{:S(2)}) collective-permute-start(bf16[4,48,384]{2,1,0:T(8,128)(2,1)} %get-tuple-element.85), channel_id=1, source_target_pairs={{0,24},{8,16},{16,8},{24,0},{1,25},{9,17},{17,9},{25,1},{2,26},{10... | collective-permute-start | bytes 442376 | tf_op jit(solution)/shard_map/ppermute | solution.py:816
  56.4 15.1 %copy-start.1 = (bf16[384,384]{1,0:T(8,128)(2,1)S(1)}, bf16[384,384]{1,0:T(8,128)(2,1)}, u32[]{:S(2)}) copy-start(bf16[384,384]{1,0:T(8,128)(2,1)} %copy-done) | copy-start | bytes 884740
  56.4 15.1 %copy-start.3 = (bf16[4,48,384]{2,1,0:T(8,128)(2,1)S(1)}, bf16[4,48,384]{2,1,0:T(8,128)(2,1)}, u32[]{:S(2)}) copy-start(bf16[4,48,384]{2,1,0:T(8,128)(2,1)} %copy-done.2) | copy-start | bytes 442372
  67.9 11.9 %all-to-all-start.2 = ((bf16[8,96,128]{2,1,0:T(8,128)(2,1)}), bf16[8,96,128]{2,1,0:T(8,128)(2,1)S(1)}, u32[]{:S(2)}, u32[]{:S(2)}) async-start(bf16[8,96,128]{2,1,0:T(8,128)(2,1)} %broadcast_in_dim.21), calls=%async_computation.2 | async-start | bytes 393216 | tf_op jit(solution)/shard_map/all_to_all | solution.py:812
  71.8 7.9 %collective-permute-start.10 = (bf16[48,384]{1,0:T(8,128)(2,1)S(1)}, bf16[48,384]{1,0:T(8,128)(2,1)S(1)}, u32[]{:S(2)}, u32[]{:S(2)}) collective-permute-start(bf16[48,384]{1,0:T(8,128)(2,1)S(1)} %get-tuple-element.91), channel_id=1, source_target_pairs={{0,2},{1,3},{2,0},{3,1},{4,6},{5,7},{6,4},{7,5},{8,10},{9,11},{10,... | collective-permute-start | bytes 110600 | tf_op jit(solution)/shard_map/ppermute | solution.py:816
  73.9 10.7 %collective-permute-start.7 = (bf16[96,384]{1,0:T(8,128)(2,1)S(1)}, bf16[96,384]{1,0:T(8,128)(2,1)S(1)}, u32[]{:S(2)}, u32[]{:S(2)}) collective-permute-start(bf16[96,384]{1,0:T(8,128)(2,1)S(1)} %get-tuple-element.87), channel_id=1, source_target_pairs={{0,8},{8,0},{16,24},{24,16},{1,9},{9,1},{17,25},{25,17},{2,10},{10... | collective-permute-start | bytes 221192 | tf_op jit(solution)/shard_map/ppermute | solution.py:816
  73.9 10.7 %collective-permute-start.8 = (bf16[96,384]{1,0:T(8,128)(2,1)S(1)}, bf16[96,384]{1,0:T(8,128)(2,1)S(1)}, u32[]{:S(2)}, u32[]{:S(2)}) collective-permute-start(bf16[96,384]{1,0:T(8,128)(2,1)S(1)} %get-tuple-element.88), channel_id=1, source_target_pairs={{0,16},{8,24},{16,0},{24,8},{1,17},{9,25},{17,1},{25,9},{2,18},{10... | collective-permute-start | bytes 221192 | tf_op jit(solution)/shard_map/ppermute | solution.py:816
  76.4 8.2 %collective-permute-start.9 = (bf16[96,384]{1,0:T(8,128)(2,1)S(1)}, bf16[96,384]{1,0:T(8,128)(2,1)S(1)}, u32[]{:S(2)}, u32[]{:S(2)}) collective-permute-start(bf16[96,384]{1,0:T(8,128)(2,1)S(1)} %get-tuple-element.89), channel_id=1, source_target_pairs={{0,24},{8,16},{16,8},{24,0},{1,25},{9,17},{17,9},{25,1},{2,26},{10... | collective-permute-start | bytes 221192 | tf_op jit(solution)/shard_map/ppermute | solution.py:816
  78.3 4.4 %collective-permute-start.11 = (bf16[48,384]{1,0:T(8,128)(2,1)S(1)}, bf16[48,384]{1,0:T(8,128)(2,1)S(1)}, u32[]{:S(2)}, u32[]{:S(2)}) collective-permute-start(bf16[48,384]{1,0:T(8,128)(2,1)S(1)} %get-tuple-element.92), channel_id=1, source_target_pairs={{0,4},{1,5},{2,6},{3,7},{4,0},{5,1},{6,2},{7,3},{8,12},{9,13},{10,... | collective-permute-start | bytes 110600 | tf_op jit(solution)/shard_map/ppermute | solution.py:816
  79.8 4.9 %collective-permute-start.12 = (bf16[48,384]{1,0:T(8,128)(2,1)S(1)}, bf16[48,384]{1,0:T(8,128)(2,1)S(1)}, u32[]{:S(2)}, u32[]{:S(2)}) collective-permute-start(bf16[48,384]{1,0:T(8,128)(2,1)S(1)} %get-tuple-element.93), channel_id=1, source_target_pairs={{0,6},{1,7},{2,4},{3,5},{4,2},{5,3},{6,0},{7,1},{8,14},{9,15},{10,... | collective-permute-start | bytes 110600 | tf_op jit(solution)/shard_map/ppermute | solution.py:816
  84.7 14.3 %collective-permute-start.13 = (bf16[176,384]{1,0:T(8,128)(2,1)S(1)}, bf16[176,384]{1,0:T(8,128)(2,1)S(1)}, u32[]{:S(2)}, u32[]{:S(2)}) collective-permute-start(bf16[176,384]{1,0:T(8,128)(2,1)S(1)} %join.1._.refs_0_), channel_id=1, source_target_pairs={{0,8},{8,0},{16,24},{24,16},{1,9},{9,1},{17,25},{25,17},{2,10},{10... | collective-permute-start | bytes 405512 | tf_op jit(solution)/shard_map/ppermute | solution.py:816
  84.8 14.3 %collective-permute-start.14 = (bf16[176,384]{1,0:T(8,128)(2,1)S(1)}, bf16[176,384]{1,0:T(8,128)(2,1)S(1)}, u32[]{:S(2)}, u32[]{:S(2)}) collective-permute-start(bf16[176,384]{1,0:T(8,128)(2,1)S(1)} %join.1._.refs_0_), channel_id=1, source_target_pairs={{0,16},{8,24},{16,0},{24,8},{1,17},{9,25},{17,1},{25,9},{2,18},{10... | collective-permute-start | bytes 405512 | tf_op jit(solution)/shard_map/ppermute | solution.py:816
  87.3 11.7 %collective-permute-start.15 = (bf16[176,384]{1,0:T(8,128)(2,1)S(1)}, bf16[176,384]{1,0:T(8,128)(2,1)S(1)}, u32[]{:S(2)}, u32[]{:S(2)}) collective-permute-start(bf16[176,384]{1,0:T(8,128)(2,1)S(1)} %join.1._.refs_0_), channel_id=1, source_target_pairs={{0,24},{8,16},{16,8},{24,0},{1,25},{9,17},{17,9},{25,1},{2,26},{10... | collective-permute-start | bytes 405512 | tf_op jit(solution)/shard_map/ppermute | solution.py:816

commit v4 on v3

--- a/solution.py
+++ b/solution.py
@@ -836,21 +836,31 @@
 
 def add_pair_kernel(fc_rows, copies, me_ref, keep_ref, got_ref, *outs):
     chips = keep_ref.shape[0]
+    own_ref = outs[0]
     for chip in range(chips):
         total = keep_ref[chip, :fc_rows].astype(F32) + got_ref[chip, :fc_rows].astype(F32)
-        outs[chip][...] = total.astype(BF16)
+        if chip:
+            outs[chip][...] = total.astype(BF16)
+        else:
+            own_ref[:fc_rows, :] = total.astype(BF16)
     rows = (keep_ref.shape[1] - fc_rows) // copies
-    for relative, out_ref in enumerate(outs[chips:]):
+    for relative in range(copies):
         at = pl.ds(pl.multiple_of(fc_rows + (me_ref[0] ^ relative) * rows, 16), rows)
         for chip in range(chips):
             total = keep_ref[chip, at, :].astype(F32) + got_ref[chip, at, :].astype(F32)
-            out_ref[chip] = total.astype(BF16)
+            if relative:
+                outs[chips - 1 + relative][chip] = total.astype(BF16)
+            else:
+                low = fc_rows + chip * rows
+                own_ref[low : low + rows, :] = total.astype(BF16)
 
 
 def add_pair(me, fc_rows, copies, keep, got):
     chips, rows, width = keep.shape
-    fc = (jax.ShapeDtypeStruct((fc_rows, width), BF16),) * chips
-    att = (jax.ShapeDtypeStruct((chips, (rows - fc_rows) // copies, width), BF16),) * copies
+    piece = (rows - fc_rows) // copies
+    fc = (jax.ShapeDtypeStruct((fc_rows + chips * piece, width), BF16),)
+    fc += (jax.ShapeDtypeStruct((fc_rows, width), BF16),) * (chips - 1)
+    att = (jax.ShapeDtypeStruct((chips, piece, width), BF16),) * (copies - 1)
     outs = small_call(
         functools.partial(add_pair_kernel, fc_rows, copies),
         (me, keep, got),
@@ -858,29 +868,31 @@
         fc + att,
         "add_pair",
     )
-    return outs[:chips], outs[chips:]
-
-
-def add_cut_kernel(chips, copies, me_ref, *refs):
-    fc, att = refs[:chips], refs[chips : chips + copies]
-    outs = refs[chips + copies :]
-    rows = outs[0].shape[0]
+    return outs[0], outs[1:chips], outs[chips:]
+
+
+def add_cut_kernel(chips, copies, me_ref, own_ref, *refs):
+    fc, att = refs[: chips - 1], refs[chips - 1 : chips + copies - 2]
+    outs = refs[chips + copies - 2 :]
+    rows, piece = outs[0].shape[0], outs[-1].shape[0]
     for relative, out_ref in enumerate(outs[:copies]):
         at = pl.ds(pl.multiple_of((me_ref[0] ^ relative) * rows, 16), rows)
-        out_ref[...] = sum_of([ref.at[at, :] for ref in fc]).astype(BF16)
+        out_ref[...] = sum_of([ref.at[at, :] for ref in (own_ref,) + tuple(fc)]).astype(BF16)
     for chip, out_ref in enumerate(outs[copies:]):
-        out_ref[...] = sum_of([ref.at[chip] for ref in att]).astype(BF16)
-
-
-def add_cut(me, fc, att):
-    chips, copies = len(fc), len(att)
+        low = copies * rows + chip * piece
+        terms = [own_ref.at[low : low + piece, :]] + [ref.at[chip] for ref in att]
+        out_ref[...] = sum_of(terms).astype(BF16)
+
+
+def add_cut(me, own, fc, att):
+    chips, copies = len(fc) + 1, len(att) + 1
     rows, width = fc[0].shape
     outs = (jax.ShapeDtypeStruct((rows // copies, width), BF16),) * copies
     outs += (jax.ShapeDtypeStruct(att[0].shape[1:], BF16),) * chips
     outs = small_call(
         functools.partial(add_cut_kernel, chips, copies),
-        (me,) + tuple(fc) + tuple(att),
-        [SMEM] + [VMEM] * (chips + copies),
+        (me, own) + tuple(fc) + tuple(att),
+        [SMEM] + [VMEM] * (chips + copies - 1),
         outs,
         "add_cut",
     )
@@ -1005,10 +1017,10 @@
         jnp.broadcast_to(conv_part.astype(BF16)[None], (space,) + conv_part.shape), "space"
     )
 
-    fc, att = add_pair(me_dp, fc_rows, copies, keep, exchange(send, "space", 1))
-    fc = [fc[0]] + [exchange(fc[r], "space", 2 * r) for r in range(1, len(fc))]
-    att = [att[0]] + [exchange(att[r], "dp", r) for r in range(1, copies)]
-    fc, att = add_cut(me_dp, fc, att)
+    own, fc, att = add_pair(me_dp, fc_rows, copies, keep, exchange(send, "space", 1))
+    fc = [exchange(part, "space", 2 * r) for r, part in enumerate(fc, 1)]
+    att = [exchange(part, "dp", r) for r, part in enumerate(att, 1)]
+    fc, att = add_cut(me_dp, own, fc, att)
     fc_piece, att_piece = fc[0].shape[0], att[0].shape[0]
     fc = [fc[0]] + [exchange(fc[r], "dp", r) for r in range(1, copies)]
     att = [att[0]] + [exchange(att[r], "space", 2 * r) for r in range(1, len(att))]

time: 101 us -> 100 us (0.990)
    unnamed x16 -> x12, local copies, waits for them, and re-layouts: 2.12 us -> 1.51 us
  transfers between devices with their start and end apart: 19 -> 19, of which waited for: 3 -> 3; matrix products, arithmetic and copies ran while one was open for 1% -> 1% of each run, Pallas kernels for 27% -> 28%
where the time goes in v4:
time: 100 us; the launch traced here: 99.5 us
  Pallas kernels  52.7 us (53%)
  starting transfers between devices  35.3 us (35%)
  waiting for transfers between devices  8.37 us (8%)
  local copies, waits for them, and re-layouts  2.22 us (2%)
    ppermute x16, starting transfers between devices, exchange(): lax.ppermute(values, axis, [(i, i ^ relative) for i in range(lax.axis_siz...  22.3 us
    all_to_all x3, starting transfers between devices, scatter(): return lax.all_to_all(values, axis, split_axis=0, concat_axis=0, tiled=True)  13.1 us
    pallas_call x1, Pallas kernels, conv_weight_grad(): pl.pallas_call(functools.partial(conv_weight_kernel, sizes), in_specs=[VM...  10.7 us
    pallas_call x1, Pallas kernels, feature_gradient(): pl.pallas_call(functools.partial(feature_kernel, sizes), in_specs=[HBM, H...  9.87 us
    pallas_call x1, Pallas kernels, conv_forward(): pl.pallas_call(functools.partial(conv_forward_kernel, sizes), in_specs=[V...  9.16 us
    pallas_call x1, Pallas kernels, transformer(): pl.pallas_call(functools.partial(first_kernel, sizes), in_specs=[VMEM] *...  6.99 us
    pallas_call x1, Pallas kernels, prepare(): pl.pallas_call(functools.partial(prepare_kernel, sizes), grid=(steps,), i...  5.45 us
    ppermute x16, waiting for transfers between devices, exchange(): lax.ppermute(values, axis, [(i, i ^ relative) for i in range(lax.axis_siz...  4.81 us
  transfers between devices with their start and end apart: 19, of which 3 were waited for; matrix products, arithmetic and copies ran while one was open for 1% of the time, Pallas kernels for 28%

profile of v4, /device:TPU:0, one launch (start us, length us, event | category | flops | bytes accessed | tf_op | source)
XLA Modules:
  0.0 99.5 jit_solution(11602689532678793225)
XLA Ops:
  0.6 0.0 copy-start.3
  0.6 0.7 copy-done.3
  1.4 0.0 copy-start.4
  1.4 0.0 copy-start.5
  1.4 0.0 copy-start.2
  1.4 9.2 %conv_forward.1 = (bf16[448,448]{1,0:T(8,128)(2,1)}, bf16[81,96]{1,0:T(8,128)(2,1)S(1)}) custom-call(bf16[27,3,96]{2,1,0:T(4,128)(2,1)S(1)} %bitcast.16, bf16[96,7,16,448]{3,2,1,0:T(8,128)(2,1)} %bitcast.18), custom_call_target="tpu_custom_call" | custom-call | flops 4161798144 | bytes 9633792 | tf_op jit(solution)/shard_map/conv_forward/pallas_call | solution.py:175
  10.5 5.2 %all-to-all-start = ((bf16[8,56,448]{2,1,0:T(8,128)(2,1)}), bf16[8,56,448]{2,1,0:T(8,128)(2,1)S(1)}, u32[]{:S(2)}, u32[]{:S(2)}) async-start(bf16[8,56,448]{2,1,0:T(8,128)(2,1)} %bitcast.3), calls=%async_computation | async-start | bytes 917504 | tf_op jit(solution)/shard_map/all_to_all | solution.py:812
  15.7 0.0 copy-done.4
  15.8 0.0 copy-done.5
  15.8 0.0 copy-done.2
  15.8 5.4 %prepare.1 = (bf16[896,384]{1,0:T(8,128)(2,1)}, bf16[1536,432]{1,0:T(8,128)(2,1)}) custom-call(bf16[81,96]{1,0:T(8,128)(2,1)S(1)} %get-tuple-element.53.weight_ref, bf16[588,384]{1,0:T(8,128)(2,1)S(1)} %copy-done.2), custom_call_target="tpu_custom_call" | custom-call | flops 4000000000 | bytes 4194304 | tf_op jit(solution)/shard_map/prepare/pallas_call | solution.py:231
  21.2 3.5 %all-to-all-done = bf16[8,56,448]{2,1,0:T(8,128)(2,1)S(1)} async-done(((bf16[8,56,448]{2,1,0:T(8,128)(2,1)}), bf16[8,56,448]{2,1,0:T(8,128)(2,1)S(1)}, u32[]{:S(2)}, u32[]{:S(2)}) %all-to-all-start) | async-done | bytes 401440 | tf_op jit(solution)/shard_map/all_to_all | solution.py:812
  24.8 7.0 %block_forward.1 = (bf16[2,128,384]{2,1,0:T(8,128)(2,1)}, bf16[256,384]{1,0:T(8,128)(2,1)S(1)}, bf16[256,1152]{1,0:T(8,128)(2,1)S(1)}, f32[12,128,128]{2,1,0:T(8...) custom-call(bf16[448,448]{1,0:T(8,128)(2,1)S(1)} %bitcast.15, ...), custom_call_target="tpu_custom_call" | custom-call | flops 2164260864 | bytes 12582912 | tf_op jit(solution)/shard_map/block_forward/pallas_call | solution.py:590
  31.8 4.5 %block_backward.1 = (bf16[448,448]{1,0:T(8,128)(2,1)}, bf16[256,1152]{1,0:T(8,128)(2,1)S(1)}) custom-call(bf16[256,1152]{1,0:T(8,128)(2,1)S(1)} %get-tuple-element.57.packed_ref, f32[12,128,128]{2,1,0:T(8,128)S(1)} %get-tuple-element.58.probs_ref, bf16[12,128,128]{2,1,0:T(8,128)(2,1)S(1)} %get-tuple-element.59.probs_b_ref, ...), custom_call_target="tpu_custom_call" | custom-call | flops 956301312 | bytes 6291456 | tf_op jit(solution)/shard_map/block_backward/pallas_call | solution.py:626
  36.3 3.6 %weight_grads.1 = (bf16[4,576,384]{2,1,0:T(8,128)(2,1)S(1)}, bf16[4,576,384]{2,1,0:T(8,128)(2,1)}) custom-call(s32[1]{0:T(128)} %bitcast.11.me_ref, bf16[256,384]{1,0:T(8,128)(2,1)S(1)} %get-tuple-element.69.normed_ref, bf16[256,1152]{1,0:T(8,128)(2,1)S(1)} %get-tuple-element.70.grad_packed_ref, bf16[256,384]{1,0:T(8,128)(2,1)S(1)} %get-tuple-element.71.attended_ref, ...), custom_call_target="tpu_custom_call" | custom-call | flops 905969664 | bytes 8388608 | tf_op jit(solution)/shard_map/weight_grads/pallas_call | solution.py:656
  39.9 0.0 collective-permute-start
  39.9 4.3 %all-to-all-start.1 = ((bf16[8,56,448]{2,1,0:T(8,128)(2,1)}), bf16[8,56,448]{2,1,0:T(8,128)(2,1)}, u32[]{:S(2)}, u32[]{:S(2)}) async-start(bf16[8,56,448]{2,1,0:T(8,128)(2,1)} %bitcast.17), calls=%async_computation.1 | async-start | bytes 917504 | tf_op jit(solution)/shard_map/all_to_all | solution.py:812
  44.2 0.0 collective-permute-done.got_ref
  44.2 1.1 %add_pair.1 = (bf16[576,384]{1,0:T(8,128)(2,1)S(1)}, bf16[384,384]{1,0:T(8,128)(2,1)}, bf16[384,384]{1,0:T(8,128)(2,1)}, bf16[384,384]{1,0:T(8,128)(2,1)}, bf16[...) custom-call(s32[1]{0:T(128)} %bitcast.10.me_ref, ...), custom_call_target="tpu_custom_call" | custom-call | tf_op jit(solution)/shard_map/add_pair/pallas_call | solution.py:820
  45.3 0.0 copy-start
  45.3 0.8 copy-done
  46.1 1.6 %collective-permute-start.4 = (bf16[4,48,384]{2,1,0:T(8,128)(2,1)S(1)}, bf16[4,48,384]{2,1,0:T(8,128)(2,1)S(1)}, u32[]{:S(2)}, u32[]{:S(2)}) collective-permute-start(bf16[4,48,384]{2,1,0:T(8,128)(2,1)S(1)} %get-tuple-element.81), channel_id=1, source_target_pairs={{0,8},{8,0},{16,24},{24,16},{1,9},{9,1},{17,25},{25,17},{2,10},{10... | collective-permute-start | bytes 442376 | tf_op jit(solution)/shard_map/ppermute | solution.py:816
  47.6 1.7 %collective-permute-start.1 = (bf16[384,384]{1,0:T(8,128)(2,1)}, bf16[384,384]{1,0:T(8,128)(2,1)S(1)}, u32[]{:S(2)}, u32[]{:S(2)}) collective-permute-start(bf16[384,384]{1,0:T(8,128)(2,1)} %get-tuple-element.78), channel_id=1, source_target_pairs={{0,2},{1,3},{2,0},{3,1},{4,6},{5,7},{6,4},{7,5},{8,10},{9,11},{10,... | collective-permute-start | bytes 884744 | tf_op jit(solution)/shard_map/ppermute | solution.py:816
  49.4 1.5 %collective-permute-start.2 = (bf16[384,384]{1,0:T(8,128)(2,1)}, bf16[384,384]{1,0:T(8,128)(2,1)S(1)}, u32[]{:S(2)}, u32[]{:S(2)}) collective-permute-start(bf16[384,384]{1,0:T(8,128)(2,1)} %get-tuple-element.79), channel_id=1, source_target_pairs={{0,4},{1,5},{2,6},{3,7},{4,0},{5,1},{6,2},{7,3},{8,12},{9,13},{10,... | collective-permute-start | bytes 884744 | tf_op jit(solution)/shard_map/ppermute | solution.py:816
  50.8 0.3 collective-permute-start.3
  51.1 2.6 %collective-permute-start.5 = (bf16[4,48,384]{2,1,0:T(8,128)(2,1)}, bf16[4,48,384]{2,1,0:T(8,128)(2,1)S(1)}, u32[]{:S(2)}, u32[]{:S(2)}) collective-permute-start(bf16[4,48,384]{2,1,0:T(8,128)(2,1)} %get-tuple-element.82), channel_id=1, source_target_pairs={{0,16},{8,24},{16,0},{24,8},{1,17},{9,25},{17,1},{25,9},{2,18},{10... | collective-permute-start | bytes 442376 | tf_op jit(solution)/shard_map/ppermute | solution.py:816
  53.7 0.0 collective-permute-done.4.refs_3_
  53.7 2.2 %collective-permute-start.6 = (bf16[4,48,384]{2,1,0:T(8,128)(2,1)}, bf16[4,48,384]{2,1,0:T(8,128)(2,1)S(1)}, u32[]{:S(2)}, u32[]{:S(2)}) collective-permute-start(bf16[4,48,384]{2,1,0:T(8,128)(2,1)} %get-tuple-element.83), channel_id=1, source_target_pairs={{0,24},{8,16},{16,8},{24,0},{1,25},{9,17},{17,9},{25,1},{2,26},{10... | collective-permute-start | bytes 442376 | tf_op jit(solution)/shard_map/ppermute | solution.py:816
  55.9 0.0 all-to-all-done.1
  55.9 0.0 copy-start.1
  55.9 10.7 %conv_weight_grad.1 = (f32[96,128]{1,0:T(8,128)S(1)}, bf16[1296,448]{1,0:T(8,128)(2,1)}) custom-call(bf16[448,448]{1,0:T(8,128)(2,1)} %bitcast.8.wire_ref, bf16[96,7,16,448]{3,2,1,0:T(8,128)(2,1)} %bitcast.19), custom_call_target="tpu_custom_call" | custom-call | flops 4161798144 | bytes 9633792 | tf_op jit(solution)/shard_map/conv_weight_grad/pallas_call | solution.py:735
  66.7 0.7 broadcast_in_dim.21
  67.4 3.6 %all-to-all-start.2 = ((bf16[8,96,128]{2,1,0:T(8,128)(2,1)}), bf16[8,96,128]{2,1,0:T(8,128)(2,1)S(1)}, u32[]{:S(2)}, u32[]{:S(2)}) async-start(bf16[8,96,128]{2,1,0:T(8,128)(2,1)} %broadcast_in_dim.21), calls=%async_computation.2 | async-start | bytes 393216 | tf_op jit(solution)/shard_map/all_to_all | solution.py:812
  70.9 0.0 collective-permute-done.5.refs_4_
  71.0 0.0 collective-permute-done.6.refs_5_
  71.0 0.0 collective-permute-done.1.refs_0_
  71.0 0.0 collective-permute-done.2.refs_1_
  71.0 0.0 collective-permute-done.3.refs_2_
  71.0 0.0 copy-done.1
  71.0 0.2 add_cut.1
  71.2 2.1 %collective-permute-start.10 = (bf16[48,384]{1,0:T(8,128)(2,1)S(1)}, bf16[48,384]{1,0:T(8,128)(2,1)S(1)}, u32[]{:S(2)}, u32[]{:S(2)}) collective-permute-start(bf16[48,384]{1,0:T(8,128)(2,1)S(1)} %get-tuple-element.89), channel_id=1, source_target_pairs={{0,2},{1,3},{2,0},{3,1},{4,6},{5,7},{6,4},{7,5},{8,10},{9,11},{10,... | collective-permute-start | bytes 110600 | tf_op jit(solution)/shard_map/ppermute | solution.py:816
  73.3 0.0 collective-permute-start.7
  73.3 2.5 %collective-permute-start.8 = (bf16[96,384]{1,0:T(8,128)(2,1)S(1)}, bf16[96,384]{1,0:T(8,128)(2,1)S(1)}, u32[]{:S(2)}, u32[]{:S(2)}) collective-permute-start(bf16[96,384]{1,0:T(8,128)(2,1)S(1)} %get-tuple-element.86), channel_id=1, source_target_pairs={{0,16},{8,24},{16,0},{24,8},{1,17},{9,25},{17,1},{25,9},{2,18},{10... | collective-permute-start | bytes 221192 | tf_op jit(solution)/shard_map/ppermute | solution.py:816
  75.9 1.8 %collective-permute-start.9 = (bf16[96,384]{1,0:T(8,128)(2,1)S(1)}, bf16[96,384]{1,0:T(8,128)(2,1)S(1)}, u32[]{:S(2)}, u32[]{:S(2)}) collective-permute-start(bf16[96,384]{1,0:T(8,128)(2,1)S(1)} %get-tuple-element.87), channel_id=1, source_target_pairs={{0,24},{8,16},{16,8},{24,0},{1,25},{9,17},{17,9},{25,1},{2,26},{10... | collective-permute-start | bytes 221192 | tf_op jit(solution)/shard_map/ppermute | solution.py:816
  77.7 1.5 %collective-permute-start.11 = (bf16[48,384]{1,0:T(8,128)(2,1)S(1)}, bf16[48,384]{1,0:T(8,128)(2,1)S(1)}, u32[]{:S(2)}, u32[]{:S(2)}) collective-permute-start(bf16[48,384]{1,0:T(8,128)(2,1)S(1)} %get-tuple-element.90), channel_id=1, source_target_pairs={{0,4},{1,5},{2,6},{3,7},{4,0},{5,1},{6,2},{7,3},{8,12},{9,13},{10,... | collective-permute-start | bytes 110600 | tf_op jit(solution)/shard_map/ppermute | solution.py:816
  79.2 0.0 collective-permute-done.10.refs_5_
  79.2 0.1 collective-permute-start.12
  79.3 0.0 all-to-all-done.2.conv_ref
  79.3 2.8 %collective-permute-done.11.refs_6_ = bf16[48,384]{1,0:T(8,128)(2,1)S(1)} collective-permute-done((bf16[48,384]{1,0:T(8,128)(2,1)S(1)}, bf16[48,384]{1,0:T(8,128)(2,1)S(1)}, u32[]{:S(2)}, u32[]{:S(2)}) %collective-permute-start.11) | collective-permute-done | bytes 36896 | tf_op jit(solution)/shard_map/ppermute | solution.py:816
  82.1 2.0 %collective-permute-done.12.refs_7_ = bf16[48,384]{1,0:T(8,128)(2,1)S(1)} collective-permute-done((bf16[48,384]{1,0:T(8,128)(2,1)S(1)}, bf16[48,384]{1,0:T(8,128)(2,1)S(1)}, u32[]{:S(2)}, u32[]{:S(2)}) %collective-permute-start.12) | collective-permute-done | bytes 36896 | tf_op jit(solution)/shard_map/ppermute | solution.py:816
  84.0 0.0 collective-permute-done.7.refs_1_
  84.0 0.0 collective-permute-done.8.refs_2_
  84.0 0.0 collective-permute-done.9.refs_3_
  84.1 0.1 join.1._.refs_0_
  84.1 0.1 collective-permute-start.13
  84.2 2.5 %collective-permute-start.14 = (bf16[176,384]{1,0:T(8,128)(2,1)S(1)}, bf16[176,384]{1,0:T(8,128)(2,1)S(1)}, u32[]{:S(2)}, u32[]{:S(2)}) collective-permute-start(bf16[176,384]{1,0:T(8,128)(2,1)S(1)} %join.1._.refs_0_), channel_id=1, source_target_pairs={{0,16},{8,24},{16,0},{24,8},{1,17},{9,25},{17,1},{25,9},{2,18},{10... | collective-permute-start | bytes 405512 | tf_op jit(solution)/shard_map/ppermute | solution.py:816
  86.8 1.8 %collective-permute-start.15 = (bf16[176,384]{1,0:T(8,128)(2,1)S(1)}, bf16[176,384]{1,0:T(8,128)(2,1)S(1)}, u32[]{:S(2)}, u32[]{:S(2)}) collective-permute-start(bf16[176,384]{1,0:T(8,128)(2,1)S(1)} %join.1._.refs_0_), channel_id=1, source_target_pairs={{0,24},{8,16},{16,8},{24,0},{1,25},{9,17},{17,9},{25,1},{2,26},{10... | collective-permute-start | bytes 405512 | tf_op jit(solution)/shard_map/ppermute | solution.py:816
  88.6 9.9 %feature_grad.1 = bf16[96,7,16,448]{3,2,1,0:T(8,128)(2,1)} custom-call(bf16[1536,432]{1,0:T(8,128)(2,1)} %get-tuple-element.56.band_hbm, bf16[1296,448]{1,0:T(8,128)(2,1)} %get-tuple-element.67.taps_hbm, bf16[176,384]{1,0:T(8,128)(2,1)S(1)} %join.1._.refs_0_), custom_call_target="tpu_custom_call" | custom-call | flops 4161798144 | bytes 9633792 | tf_op jit(solution)/shard_map/feature_grad/pallas_call | solution.py:789
  98.5 0.0 collective-permute-done.13.refs_1_
  98.5 0.0 collective-permute-done.14.refs_2_
  98.5 0.0 collective-permute-done.15.refs_3_
  98.5 1.0 %finish.1 = (f32[48,1152]{1,0:T(8,128)}, f32[48,384]{1,0:T(8,128)}, f32[48,1536]{1,0:T(8,128)}, f32[192,384]{1,0:T(8,128)}, f32[3,3,3,3,96]{4,3,2,1,0:T(4,128)}) custom-call(s32[1]{0:T(128)} %bitcast.10.me_ref, bf16[176,384]{1,0:T(8,128)(2,1)S(1)} %join.1._.refs_0_, bf16[176,384]{1,0:T(8,128)(2,1)S(1)} %collective-permute-done.13.refs_1_, ...), custom_call_target="tpu_custom_call" | custom-call | tf_op jit(solution)/shard_map/finish/pallas_call | solution.py:965
  (3 shorter events, 0.0 us)
Async XLA Ops:
  0.6 0.7 copy-start.3
  1.4 14.4 %copy-start.4 = (f32[384]{0:T(512)S(1)}, f32[384]{0:T(512)}, u32[]{:S(2)}) copy-start(f32[384]{0:T(512)} %param.16) | copy-start | bytes 4612
  1.4 14.4 %copy-start.5 = (f32[384]{0:T(512)S(1)}, f32[384]{0:T(512)}, u32[]{:S(2)}) copy-start(f32[384]{0:T(512)} %param.19) | copy-start | bytes 4612
  1.4 14.4 %copy-start.2 = (bf16[588,384]{1,0:T(8,128)(2,1)S(1)}, bf16[588,384]{1,0:T(8,128)(2,1)}, u32[]{:S(2)}) copy-start(bf16[588,384]{1,0:T(8,128)(2,1)} %patch_ref.1) | copy-start | bytes 1354756
  10.5 14.2 %all-to-all-start = ((bf16[8,56,448]{2,1,0:T(8,128)(2,1)}), bf16[8,56,448]{2,1,0:T(8,128)(2,1)S(1)}, u32[]{:S(2)}, u32[]{:S(2)}) async-start(bf16[8,56,448]{2,1,0:T(8,128)(2,1)} %bitcast.3), calls=%async_computation | async-start | bytes 917504 | tf_op jit(solution)/shard_map/all_to_all | solution.py:812
  39.9 4.3 %collective-permute-start = (bf16[4,576,384]{2,1,0:T(8,128)(2,1)}, bf16[4,576,384]{2,1,0:T(8,128)(2,1)S(1)}, u32[]{:S(2)}, u32[]{:S(2)}) collective-permute-start(bf16[4,576,384]{2,1,0:T(8,128)(2,1)} %get-tuple-element.76), channel_id=1, source_target_pairs={{0,1},{1,0},{2,3},{3,2},{4,5},{5,4},{6,7},{7,6},{8,9},{9,8},{10,11... | collective-permute-start | bytes 5308424 | tf_op jit(solution)/shard_map/ppermute | solution.py:816
  39.9 16.0 %all-to-all-start.1 = ((bf16[8,56,448]{2,1,0:T(8,128)(2,1)}), bf16[8,56,448]{2,1,0:T(8,128)(2,1)}, u32[]{:S(2)}, u32[]{:S(2)}) async-start(bf16[8,56,448]{2,1,0:T(8,128)(2,1)} %bitcast.17), calls=%async_computation.1 | async-start | bytes 917504 | tf_op jit(solution)/shard_map/all_to_all | solution.py:812
  45.3 0.8 copy-start
  46.1 7.7 %collective-permute-start.4 = (bf16[4,48,384]{2,1,0:T(8,128)(2,1)S(1)}, bf16[4,48,384]{2,1,0:T(8,128)(2,1)S(1)}, u32[]{:S(2)}, u32[]{:S(2)}) collective-permute-start(bf16[4,48,384]{2,1,0:T(8,128)(2,1)S(1)} %get-tuple-element.81), channel_id=1, source_target_pairs={{0,8},{8,0},{16,24},{24,16},{1,9},{9,1},{17,25},{25,17},{2,10},{10... | collective-permute-start | bytes 442376 | tf_op jit(solution)/shard_map/ppermute | solution.py:816
  47.6 23.3 %collective-permute-start.1 = (bf16[384,384]{1,0:T(8,128)(2,1)}, bf16[384,384]{1,0:T(8,128)(2,1)S(1)}, u32[]{:S(2)}, u32[]{:S(2)}) collective-permute-start(bf16[384,384]{1,0:T(8,128)(2,1)} %get-tuple-element.78), channel_id=1, source_target_pairs={{0,2},{1,3},{2,0},{3,1},{4,6},{5,7},{6,4},{7,5},{8,10},{9,11},{10,... | collective-permute-start | bytes 884744 | tf_op jit(solution)/shard_map/ppermute | solution.py:816
  49.4 21.6 %collective-permute-start.2 = (bf16[384,384]{1,0:T(8,128)(2,1)}, bf16[384,384]{1,0:T(8,128)(2,1)S(1)}, u32[]{:S(2)}, u32[]{:S(2)}) collective-permute-start(bf16[384,384]{1,0:T(8,128)(2,1)} %get-tuple-element.79), channel_id=1, source_target_pairs={{0,4},{1,5},{2,6},{3,7},{4,0},{5,1},{6,2},{7,3},{8,12},{9,13},{10,... | collective-permute-start | bytes 884744 | tf_op jit(solution)/shard_map/ppermute | solution.py:816
  50.8 20.1 %collective-permute-start.3 = (bf16[384,384]{1,0:T(8,128)(2,1)}, bf16[384,384]{1,0:T(8,128)(2,1)S(1)}, u32[]{:S(2)}, u32[]{:S(2)}) collective-permute-start(bf16[384,384]{1,0:T(8,128)(2,1)} %get-tuple-element.80), channel_id=1, source_target_pairs={{0,6},{1,7},{2,4},{3,5},{4,2},{5,3},{6,0},{7,1},{8,14},{9,15},{10,... | collective-permute-start | bytes 884744 | tf_op jit(solution)/shard_map/ppermute | solution.py:816
  51.1 19.8 %collective-permute-start.5 = (bf16[4,48,384]{2,1,0:T(8,128)(2,1)}, bf16[4,48,384]{2,1,0:T(8,128)(2,1)S(1)}, u32[]{:S(2)}, u32[]{:S(2)}) collective-permute-start(bf16[4,48,384]{2,1,0:T(8,128)(2,1)} %get-tuple-element.82), channel_id=1, source_target_pairs={{0,16},{8,24},{16,0},{24,8},{1,17},{9,25},{17,1},{25,9},{2,18},{10... | collective-permute-start | bytes 442376 | tf_op jit(solution)/shard_map/ppermute | solution.py:816
  53.7 17.2 %collective-permute-start.6 = (bf16[4,48,384]{2,1,0:T(8,128)(2,1)}, bf16[4,48,384]{2,1,0:T(8,128)(2,1)S(1)}, u32[]{:S(2)}, u32[]{:S(2)}) collective-permute-start(bf16[4,48,384]{2,1,0:T(8,128)(2,1)} %get-tuple-element.83), channel_id=1, source_target_pairs={{0,24},{8,16},{16,8},{24,0},{1,25},{9,17},{17,9},{25,1},{2,26},{10... | collective-permute-start | bytes 442376 | tf_op jit(solution)/shard_map/ppermute | solution.py:816
  55.9 15.1 %copy-start.1 = (bf16[576,384]{1,0:T(8,128)(2,1)S(1)}, bf16[576,384]{1,0:T(8,128)(2,1)}, u32[]{:S(2)}) copy-start(bf16[576,384]{1,0:T(8,128)(2,1)} %copy-done) | copy-start | bytes 1327108
  67.4 11.9 %all-to-all-start.2 = ((bf16[8,96,128]{2,1,0:T(8,128)(2,1)}), bf16[8,96,128]{2,1,0:T(8,128)(2,1)S(1)}, u32[]{:S(2)}, u32[]{:S(2)}) async-start(bf16[8,96,128]{2,1,0:T(8,128)(2,1)} %broadcast_in_dim.21), calls=%async_computation.2 | async-start | bytes 393216 | tf_op jit(solution)/shard_map/all_to_all | solution.py:812
  71.2 7.9 %collective-permute-start.10 = (bf16[48,384]{1,0:T(8,128)(2,1)S(1)}, bf16[48,384]{1,0:T(8,128)(2,1)S(1)}, u32[]{:S(2)}, u32[]{:S(2)}) collective-permute-start(bf16[48,384]{1,0:T(8,128)(2,1)S(1)} %get-tuple-element.89), channel_id=1, source_target_pairs={{0,2},{1,3},{2,0},{3,1},{4,6},{5,7},{6,4},{7,5},{8,10},{9,11},{10,... | collective-permute-start | bytes 110600 | tf_op jit(solution)/shard_map/ppermute | solution.py:816
  73.3 10.7 %collective-permute-start.7 = (bf16[96,384]{1,0:T(8,128)(2,1)S(1)}, bf16[96,384]{1,0:T(8,128)(2,1)S(1)}, u32[]{:S(2)}, u32[]{:S(2)}) collective-permute-start(bf16[96,384]{1,0:T(8,128)(2,1)S(1)} %get-tuple-element.85), channel_id=1, source_target_pairs={{0,8},{8,0},{16,24},{24,16},{1,9},{9,1},{17,25},{25,17},{2,10},{10... | collective-permute-start | bytes 221192 | tf_op jit(solution)/shard_map/ppermute | solution.py:816
  73.3 10.7 %collective-permute-start.8 = (bf16[96,384]{1,0:T(8,128)(2,1)S(1)}, bf16[96,384]{1,0:T(8,128)(2,1)S(1)}, u32[]{:S(2)}, u32[]{:S(2)}) collective-permute-start(bf16[96,384]{1,0:T(8,128)(2,1)S(1)} %get-tuple-element.86), channel_id=1, source_target_pairs={{0,16},{8,24},{16,0},{24,8},{1,17},{9,25},{17,1},{25,9},{2,18},{10... | collective-permute-start | bytes 221192 | tf_op jit(solution)/shard_map/ppermute | solution.py:816
  75.9 8.2 %collective-permute-start.9 = (bf16[96,384]{1,0:T(8,128)(2,1)S(1)}, bf16[96,384]{1,0:T(8,128)(2,1)S(1)}, u32[]{:S(2)}, u32[]{:S(2)}) collective-permute-start(bf16[96,384]{1,0:T(8,128)(2,1)S(1)} %get-tuple-element.87), channel_id=1, source_target_pairs={{0,24},{8,16},{16,8},{24,0},{1,25},{9,17},{17,9},{25,1},{2,26},{10... | collective-permute-start | bytes 221192 | tf_op jit(solution)/shard_map/ppermute | solution.py:816
  77.7 4.4 %collective-permute-start.11 = (bf16[48,384]{1,0:T(8,128)(2,1)S(1)}, bf16[48,384]{1,0:T(8,128)(2,1)S(1)}, u32[]{:S(2)}, u32[]{:S(2)}) collective-permute-start(bf16[48,384]{1,0:T(8,128)(2,1)S(1)} %get-tuple-element.90), channel_id=1, source_target_pairs={{0,4},{1,5},{2,6},{3,7},{4,0},{5,1},{6,2},{7,3},{8,12},{9,13},{10,... | collective-permute-start | bytes 110600 | tf_op jit(solution)/shard_map/ppermute | solution.py:816
  79.2 4.9 %collective-permute-start.12 = (bf16[48,384]{1,0:T(8,128)(2,1)S(1)}, bf16[48,384]{1,0:T(8,128)(2,1)S(1)}, u32[]{:S(2)}, u32[]{:S(2)}) collective-permute-start(bf16[48,384]{1,0:T(8,128)(2,1)S(1)} %get-tuple-element.91), channel_id=1, source_target_pairs={{0,6},{1,7},{2,4},{3,5},{4,2},{5,3},{6,0},{7,1},{8,14},{9,15},{10,... | collective-permute-start | bytes 110600 | tf_op jit(solution)/shard_map/ppermute | solution.py:816
  84.1 14.3 %collective-permute-start.13 = (bf16[176,384]{1,0:T(8,128)(2,1)S(1)}, bf16[176,384]{1,0:T(8,128)(2,1)S(1)}, u32[]{:S(2)}, u32[]{:S(2)}) collective-permute-start(bf16[176,384]{1,0:T(8,128)(2,1)S(1)} %join.1._.refs_0_), channel_id=1, source_target_pairs={{0,8},{8,0},{16,24},{24,16},{1,9},{9,1},{17,25},{25,17},{2,10},{10... | collective-permute-start | bytes 405512 | tf_op jit(solution)/shard_map/ppermute | solution.py:816
  84.2 14.3 %collective-permute-start.14 = (bf16[176,384]{1,0:T(8,128)(2,1)S(1)}, bf16[176,384]{1,0:T(8,128)(2,1)S(1)}, u32[]{:S(2)}, u32[]{:S(2)}) collective-permute-start(bf16[176,384]{1,0:T(8,128)(2,1)S(1)} %join.1._.refs_0_), channel_id=1, source_target_pairs={{0,16},{8,24},{16,0},{24,8},{1,17},{9,25},{17,1},{25,9},{2,18},{10... | collective-permute-start | bytes 405512 | tf_op jit(solution)/shard_map/ppermute | solution.py:816
  86.8 11.7 %collective-permute-start.15 = (bf16[176,384]{1,0:T(8,128)(2,1)S(1)}, bf16[176,384]{1,0:T(8,128)(2,1)S(1)}, u32[]{:S(2)}, u32[]{:S(2)}) collective-permute-start(bf16[176,384]{1,0:T(8,128)(2,1)S(1)} %join.1._.refs_0_), channel_id=1, source_target_pairs={{0,24},{8,16},{16,8},{24,0},{1,25},{9,17},{17,9},{25,1},{2,26},{10... | collective-permute-start | bytes 405512 | tf_op jit(solution)/shard_map/ppermute | solution.py:816
